TPU v7x, 256 devices: a whole 4x4x8 slice. The times are simulated.
256 devices in a mesh: row: 16 (over z, x_hi), col: 4 (over x_lo, core), depth: 4 (over y).
Axes of the slice: x: 4 (x_hi: 2, x_lo: 2; x = x_hi * 2 + x_lo), y: 4, z: 8, core: 2. Of those that a mesh axis runs over, the one named last changes fastest.
Arguments:
- a_tiles: bfloat16 [16, 4, 4, 4, 6, 128, 128], P('row', 'col', 'depth'), may hold values from -0.5 to 0.5
- a_index: int32 [16, 4, 4, 4, 6], P('row', 'col', 'depth'), may hold values from 0 to 127, as said below
- a_count: int32 [16, 4, 4, 4], P('row', 'col', 'depth'), may hold values from 1 to 6, as said below
- b_tiles: bfloat16 [16, 4, 4, 16, 2, 128, 128], P('row', 'col', 'depth'), may hold values from -6 to 6
- b_place: int32 [16, 4, 4, 16, 2], P('row', 'col', 'depth'), may hold values from 0 to 15, as said below
- b_count: int32 [16, 4, 4, 16], P('row', 'col', 'depth'), may hold values from 1 to 2, as said below
Outputs:
- product: float32 [64, 32, 128, 128], P(('col', 'depth'), 'row')
Inputs may be any that keep to these rules, and one draw needn't show every extreme that they name: Within one panel all 6 slots name distinct places; a_index // 8 is the block row and a_index % 8 the inner block inside the panel. `a_count`: slots at or past the count carry no block; some panel is full in every draw. Within one panel all 2 slots name distinct places; b_place // 2 is the inner block and b_place % 2 the block column inside the panel. `b_count`: slots at or past the count carry no block; some panel is full in every draw.
All inputs are finite; a program needn't handle non-finite values.
Results may differ from a plain program's by a relative error of at most 0.0003.
Values may be sent and summed in bfloat16 or wider, within the bound.
No kernel may reach another device: no remote copies, remote signals or barrier semaphores. Data moves between devices by JAX's collectives and lax.ppermute only.
A program may use at most 192 MiB of HBM per device.

v0:
```python
import jax
import jax.numpy as jnp
from jax import lax
from jax.sharding import PartitionSpec as P

BK = 8
NCB = 2
MBR = 16


def from_behind(block, axis, distance):
    devices = range(lax.axis_size(axis))
    route = [((i - distance) % len(devices), i) for i in devices]
    return lax.ppermute(block, axis, route)


def shards(a_tiles, a_index, a_count, b_tiles, b_place, b_count):
    col_count = lax.axis_size("col")
    row_count = lax.axis_size("row")
    col_pos = lax.axis_index("col")
    row_pos = lax.axis_index("row")
    left_home = a_tiles[0, 0, 0]
    right_home = b_tiles[0, 0, 0]
    left_slots = left_home.shape[1]
    right_slots = right_home.shape[1]
    tile_size = left_home.shape[-1]
    left_known, left_sizes = (
        lax.all_gather(a_index[0, 0, 0], "row", axis=0, tiled=True),
        lax.all_gather(a_count[0, 0, 0], "row", axis=0, tiled=True),
    )
    right_known, right_sizes = (
        lax.all_gather(b_place[0, 0, 0], "col", axis=0, tiled=True),
        lax.all_gather(b_count[0, 0, 0], "col", axis=0, tiled=True),
    )
    right_range = jnp.arange(right_slots, dtype=jnp.int32)
    slot_range = jnp.arange(left_slots, dtype=jnp.int32)
    column_range = jnp.arange(NCB, dtype=jnp.int32)
    target_range = jnp.arange(MBR * NCB, dtype=jnp.int32)
    source_range = jnp.arange(row_count * right_slots, dtype=jnp.int32)

    def accumulate(running, tile_stack, global_slot, panel_index, right_flat):
        stack_rows = tile_stack.shape[0]
        source = global_slot // left_slots
        slot_pos = global_slot % left_slots
        list_row = source * col_count + panel_index
        position = left_known[list_row, slot_pos]
        usable = slot_pos < left_sizes[list_row]
        block_row = position // BK
        block_inner = position % BK
        right_row = panel_index * row_count + source
        places = right_known[right_row]
        right_live = right_range[None, :] < right_sizes[right_row][:, None]
        matched = (places // NCB == block_inner[:, None]) & right_live & usable[:, None]
        spread = matched[:, :, None] & ((places % NCB)[:, :, None] == column_range[None, None, :])
        hit = jnp.any(spread, axis=1)
        picked = jnp.sum(jnp.where(spread, right_range[None, :, None], 0), axis=1)
        flat_pick = source[:, None] * right_slots + picked
        selector = (
            hit[:, :, None] & (flat_pick[:, :, None] == source_range[None, None, :])
        ).reshape(stack_rows * NCB, -1)
        chosen = jnp.dot(
            selector.astype(jnp.bfloat16),
            right_flat.reshape(right_flat.shape[0], -1),
            preferred_element_type=jnp.float32,
        )
        chosen = chosen.astype(jnp.bfloat16).reshape(stack_rows, NCB, tile_size, tile_size)
        product = jnp.einsum(
            "nij,ncjk->ncik", tile_stack, chosen, preferred_element_type=jnp.float32
        )
        target = (block_row[:, None] * NCB + column_range[None, :]).reshape(-1)
        placer = (target_range[:, None] == target[None, :]) & hit.reshape(-1)[None, :]
        added = jnp.dot(
            placer.astype(jnp.float32),
            product.reshape(stack_rows * NCB, -1),
            precision=lax.Precision.HIGHEST,
            preferred_element_type=jnp.float32,
        )
        return running + added.reshape(running.shape)

    running = jnp.zeros((MBR * NCB, tile_size, tile_size), jnp.float32)
    right_now = right_home
    for outer_turn in range(col_count):
        panel_index = (col_pos + outer_turn) % col_count
        if outer_turn > 0:
            right_now = from_behind(right_now, "col", -1)
        right_flat = right_now.reshape(row_count * right_slots, tile_size, tile_size)
        left_current = lax.dynamic_index_in_dim(left_home, panel_index, 0, keepdims=False)
        running = accumulate(
            running, left_current, row_pos * left_slots + slot_range, panel_index, right_flat
        )

        def advance(turn_index, loop_state, panel_index=panel_index, right_flat=right_flat):
            running_sum, left_moving = loop_state
            left_moving = from_behind(left_moving, "row", -1)
            source = (row_pos + turn_index) % row_count
            running_sum = accumulate(
                running_sum, left_moving, source * left_slots + slot_range, panel_index, right_flat
            )
            return (running_sum, left_moving)

        running, left_current = lax.fori_loop(1, row_count, advance, (running, left_current))
    reduced = lax.psum_scatter(running, "depth", scatter_dimension=0, tiled=True)
    return reduced.reshape(-1, NCB, tile_size, tile_size)


def solution(mesh):
    placed = (
        P("row", "col", "depth", None, None, None, None),
        P("row", "col", "depth", None, None),
        P("row", "col", "depth", None),
        P("row", "col", "depth", None, None, None, None),
        P("row", "col", "depth", None, None),
        P("row", "col", "depth", None),
    )
    return jax.shard_map(
        shards,
        mesh=mesh,
        in_specs=placed,
        out_specs=P(("col", "depth"), "row", None, None),
        check_vma=False,
    )
```

profile of v0, /device:TPU:8, one launch (start us, length us, event | category | flops | bytes accessed | tf_op | source)
XLA Modules:
  0.0 1096.8 jit_solution(11910980476783749469)
XLA Ops:
  8.3 13.7 %all-gather.1 = s32[1,1,1,64,2]{4,2,1,0,3:T(1,128)S(1)} all-gather(s32[1,1,1,16,2]{4,2,1,0,3:T(1,128)S(1)} %copy.126), channel_id=3, replica_groups=mesh['row'=16,'col'=4,'depth'=4] {'col'}, dimensions={3}, use_global_device_ids=true | all-gather | bytes 640 | tf_op jit(solution)/shard_map/all_gather | solution.py:32
  22.9 44.2 %all-gather = s32[1,1,1,64,6]{4,2,1,0,3:T(1,128)S(1)} all-gather(s32[1,1,1,4,6]{4,2,1,0,3:T(1,128)} %bitcast.668), channel_id=2, replica_groups=mesh['row'=16,'col'=4,'depth'=4] {'row'}, dimensions={3}, use_global_device_ids=true | all-gather | bytes 1632 | tf_op jit(solution)/shard_map/all_gather | solution.py:28
  70.6 13.7 %all-reduce.1 = s32[64]{0:T(128)S(1)} all-reduce(s32[64]{0:T(128)S(1)} %bitcast_dynamic-update-slice_fusion), channel_id=5, replica_groups=mesh['row'=16,'col'=4,'depth'=4] {'row'}, use_global_device_ids=true, to_apply=%add.1 | all-reduce | flops 64 | bytes 512 | tf_op jit(solution)/shard_map/all_gather | solution.py:29
  118.0 234.9 %while.84 = (s32[]{:T(128)}, f32[32,128,128]{2,0,1:T(8,128)S(1)}, bf16[6,128,128]{2,1,0:T(8,128)(2,1)}, s32[]{:T(128)}, s32[]{:T(128)}, /*index=5*/s32[64,6]{0,1...) while((s32[]{:T(128)}, f32[32,128,128]{2,0,1:T(8,128)S(1)}, ...), condition=%wide.region_5.6_spmd.clone.clone, body=%wide.region_2.5_spmd.clone.clone.sunk | while | flops 139137552 | bytes 18163812 | solution.py:101
  126.0 10.5 collective-permute-done
  168.8 5.2 collective-permute-start
  183.7 5.2 collective-permute-start
  198.7 5.2 collective-permute-start
  213.6 5.2 collective-permute-start
  228.7 6.0 collective-permute-start
  245.7 6.0 collective-permute-start
  261.9 6.0 collective-permute-start
  277.7 5.6 collective-permute-start
  293.1 5.2 collective-permute-start
  308.0 5.2 collective-permute-start
  323.0 5.2 collective-permute-start
  337.9 5.2 collective-permute-start
  365.9 225.9 %while.85 = (s32[]{:T(128)}, f32[32,128,128]{2,0,1:T(8,128)S(1)}, bf16[6,128,128]{2,1,0:T(8,128)(2,1)S(1)}, s32[]{:T(128)}, s32[]{:T(128)}, /*index=5*/s32[64,6]...) while((s32[]{:T(128)}, f32[32,128,128]{2,0,1:T(8,128)S(1)}, ...), condition=%wide.region_11.12_spmd.clone.clone, body=%wide.region_8.11_spmd.clone.clone.sunk | while | flops 139137552 | bytes 13969474 | solution.py:101
  365.9 5.2 collective-permute-start.1
  376.6 4.9 collective-permute-done.1
  386.3 6.4 collective-permute-start.1
  459.9 4.6 collective-permute-start.1
  474.9 5.8 collective-permute-start.1
  491.0 5.1 collective-permute-start.1
  603.7 217.3 %while.86 = (s32[]{:T(128)}, f32[32,128,128]{2,0,1:T(8,128)S(1)}, bf16[6,128,128]{2,1,0:T(8,128)(2,1)S(1)}, s32[]{:T(128)}, s32[]{:T(128)}, /*index=5*/s32[64,6]...) while((s32[]{:T(128)}, f32[32,128,128]{2,0,1:T(8,128)S(1)}, ...), condition=%wide.region_17.18_spmd.clone.clone, body=%wide.region_14.17_spmd.clone.clone.sunk | while | flops 139137552 | bytes 13969474 | solution.py:101
  646.3 4.6 collective-permute-start.2
  661.3 5.8 collective-permute-start.2
  677.4 5.1 collective-permute-start.2
  824.5 234.8 %while.87 = (s32[]{:T(128)}, f32[32,128,128]{2,0,1:T(8,128)}, bf16[6,128,128]{2,1,0:T(8,128)(2,1)S(1)}, s32[]{:T(128)}, s32[]{:T(128)}, /*index=5*/s32[64,6]{0,1...) while((s32[]{:T(128)}, f32[32,128,128]{2,0,1:T(8,128)}, ...), condition=%wide.region_23.24_spmd.clone.clone, body=%wide.region_20.23_spmd.clone.clone.sunk | while | flops 139137552 | bytes 30746744 | solution.py:101
  886.7 5.7 collective-permute-start.3
  904.0 5.0 collective-permute-start.3
  1059.3 28.7 %reduce-scatter.2.cloned.1.call-done = f32[8,128,128]{2,0,1:T(8,128)} async-done(((f32[32,128,128]{2,0,1:T(8,128)}), f32[8,128,128]{2,0,1:T(8,128)}) %reduce-scatter.2.cloned.1.call-update) | async-done | bytes 524304 | tf_op jit(solution)/shard_map/reduce_scatter | solution.py:102
  (2259 shorter events, 841.8 us)
Async XLA Ops:
  6.5 1081.4 %reduce-scatter.2.cloned.1.call-start = ((), (), s32[]{:S(2)}) async-start(), calls=%async_computation.1 | async-start | bytes 2621440 | tf_op jit(solution)/shard_map/reduce_scatter | solution.py:102
  6.5 102.9 %collective-permute-start.4 = (bf16[16,2,128,128]{3,2,1,0:T(8,128)(2,1)}, bf16[16,2,128,128]{3,2,1,0:T(8,128)(2,1)}, u32[]{:S(2)}, u32[]{:S(2)}) collective-permute-start(bf16[16,2,128,128]{3,2,1,0:T(8,128)(2,1)} %bitcast.648), channel_id=1, source_target_pairs={{4,0},{8,4},{12,8},{0,12},{5,1},{9,5},{13,9},{1,13},{6,2},{10,6},{... | collective-permute-start | bytes 3145736 | tf_op jit(solution)/shard_map/ppermute | solution.py:14
  118.0 239.5 %collective-permute-start.5 = (bf16[16,2,128,128]{3,2,1,0:T(8,128)(2,1)}, bf16[16,2,128,128]{3,2,1,0:T(8,128)(2,1)}, u32[]{:S(2)}, u32[]{:S(2)}) collective-permute-start(bf16[16,2,128,128]{3,2,1,0:T(8,128)(2,1)} %collective-permute-done.4), channel_id=1, source_target_pairs={{4,0},{8,4},{12,8},{0,12},{5,1},{9,5},{13,9},{1,13},{6,2},{10,6},{... | collective-permute-start | bytes 3145736 | tf_op jit(solution)/shard_map/ppermute | solution.py:14
  118.0 18.5 %collective-permute-start = (bf16[6,128,128]{2,1,0:T(8,128)(2,1)}, bf16[6,128,128]{2,1,0:T(8,128)(2,1)S(1)}, u32[]{:S(2)}, u32[]{:S(2)}) collective-permute-start(bf16[6,128,128]{2,1,0:T(8,128)(2,1)} %get-tuple-element.2943), channel_id=1, source_target_pairs={{16,0},{32,16},{48,32},{64,48},{80,64},{96,80},{112,96},{128,112},... | collective-permute-start | bytes 589832 | tf_op jit(solution)/shard_map/while/body/eval_jaxpr/ppermute | solution.py:14
  168.8 9.5 collective-permute-start
  183.7 9.5 collective-permute-start
  198.7 9.5 collective-permute-start
  213.6 9.6 collective-permute-start
  228.7 11.5 %collective-permute-start = (bf16[6,128,128]{2,1,0:T(8,128)(2,1)}, bf16[6,128,128]{2,1,0:T(8,128)(2,1)S(1)}, u32[]{:S(2)}, u32[]{:S(2)}) collective-permute-start(bf16[6,128,128]{2,1,0:T(8,128)(2,1)} %get-tuple-element.2943), channel_id=1, source_target_pairs={{16,0},{32,16},{48,32},{64,48},{80,64},{96,80},{112,96},{128,112},... | collective-permute-start | bytes 589832 | tf_op jit(solution)/shard_map/while/body/eval_jaxpr/ppermute | solution.py:14
  245.7 10.8 collective-permute-start
  261.9 10.3 collective-permute-start
  277.7 9.9 collective-permute-start
  293.1 9.5 collective-permute-start
  308.0 9.5 collective-permute-start
  323.0 9.5 collective-permute-start
  337.9 9.5 collective-permute-start
  365.9 229.3 %collective-permute-start.6 = (bf16[16,2,128,128]{3,2,1,0:T(8,128)(2,1)}, bf16[16,2,128,128]{3,2,1,0:T(8,128)(2,1)}, u32[]{:S(2)}, u32[]{:S(2)}) collective-permute-start(bf16[16,2,128,128]{3,2,1,0:T(8,128)(2,1)} %collective-permute-done.5), channel_id=1, source_target_pairs={{4,0},{8,4},{12,8},{0,12},{5,1},{9,5},{13,9},{1,13},{6,2},{10,6},{... | collective-permute-start | bytes 3145736 | tf_op jit(solution)/shard_map/ppermute | solution.py:14
  365.9 15.6 %collective-permute-start.1 = (bf16[6,128,128]{2,1,0:T(8,128)(2,1)S(1)}, bf16[6,128,128]{2,1,0:T(8,128)(2,1)S(1)}, u32[]{:S(2)}, u32[]{:S(2)}) collective-permute-start(bf16[6,128,128]{2,1,0:T(8,128)(2,1)S(1)} %get-tuple-element.2991), channel_id=1, source_target_pairs={{16,0},{32,16},{48,32},{64,48},{80,64},{96,80},{112,96},{128,112},... | collective-permute-start | bytes 589832 | tf_op jit(solution)/shard_map/while/body/eval_jaxpr/ppermute | solution.py:14
  386.3 11.9 %collective-permute-start.1 = (bf16[6,128,128]{2,1,0:T(8,128)(2,1)S(1)}, bf16[6,128,128]{2,1,0:T(8,128)(2,1)S(1)}, u32[]{:S(2)}, u32[]{:S(2)}) collective-permute-start(bf16[6,128,128]{2,1,0:T(8,128)(2,1)S(1)} %get-tuple-element.2991), channel_id=1, source_target_pairs={{16,0},{32,16},{48,32},{64,48},{80,64},{96,80},{112,96},{128,112},... | collective-permute-start | bytes 589832 | tf_op jit(solution)/shard_map/while/body/eval_jaxpr/ppermute | solution.py:14
  403.0 9.6 collective-permute-start.1
  459.9 10.2 collective-permute-start.1
  474.9 11.3 %collective-permute-start.1 = (bf16[6,128,128]{2,1,0:T(8,128)(2,1)S(1)}, bf16[6,128,128]{2,1,0:T(8,128)(2,1)S(1)}, u32[]{:S(2)}, u32[]{:S(2)}) collective-permute-start(bf16[6,128,128]{2,1,0:T(8,128)(2,1)S(1)} %get-tuple-element.2991), channel_id=1, source_target_pairs={{16,0},{32,16},{48,32},{64,48},{80,64},{96,80},{112,96},{128,112},... | collective-permute-start | bytes 589832 | tf_op jit(solution)/shard_map/while/body/eval_jaxpr/ppermute | solution.py:14
  491.0 10.6 collective-permute-start.1
  506.4 9.8 collective-permute-start.1
  646.3 10.1 collective-permute-start.2
  661.3 11.3 %collective-permute-start.2 = (bf16[6,128,128]{2,1,0:T(8,128)(2,1)S(1)}, bf16[6,128,128]{2,1,0:T(8,128)(2,1)S(1)}, u32[]{:S(2)}, u32[]{:S(2)}) collective-permute-start(bf16[6,128,128]{2,1,0:T(8,128)(2,1)S(1)} %get-tuple-element.3039), channel_id=1, source_target_pairs={{16,0},{32,16},{48,32},{64,48},{80,64},{96,80},{112,96},{128,112},... | collective-permute-start | bytes 589832 | tf_op jit(solution)/shard_map/while/body/eval_jaxpr/ppermute | solution.py:14
  677.4 10.6 collective-permute-start.2
  692.9 9.8 collective-permute-start.2
  870.6 10.1 collective-permute-start.3
  886.7 11.2 %collective-permute-start.3 = (bf16[6,128,128]{2,1,0:T(8,128)(2,1)S(1)}, bf16[6,128,128]{2,1,0:T(8,128)(2,1)S(1)}, u32[]{:S(2)}, u32[]{:S(2)}) collective-permute-start(bf16[6,128,128]{2,1,0:T(8,128)(2,1)S(1)} %get-tuple-element.3087), channel_id=1, source_target_pairs={{16,0},{32,16},{48,32},{64,48},{80,64},{96,80},{112,96},{128,112},... | collective-permute-start | bytes 589832 | tf_op jit(solution)/shard_map/while/body/eval_jaxpr/ppermute | solution.py:14
  904.0 10.5 collective-permute-start.3
  920.6 9.7 collective-permute-start.3
  (84 other events, 423.7 us)
Sparse Core Ops, SparseCore 0:
  1059.4 28.5 reduce-scatter.1
where the time goes:
time: 1100 us
  local copies, waits for them, and re-layouts  346 us (31%)
  matrix products  317 us (29%)
  starting transfers between devices  264 us (24%)
  blocking collectives  75.9 us (7%)
  waiting for transfers between devices  47 us (4%)
  other arithmetic  25.7 us (2%)
  between operations  15.1 us (1%)
    ppermute x63, starting transfers between devices, from_behind(): return lax.ppermute(block, axis, route)  264 us
    dot_general x64, matrix products, accumulate(): jnp.dot(placer.astype(jnp.float32), product.reshape(stack_rows * NCB, -1)...  136 us
    dot_general x64, matrix products, accumulate(): jnp.dot(selector.astype(jnp.bfloat16), right_flat.reshape(right_flat.shap...  102 us
    transpose x64, local copies, waits for them, and re-layouts, accumulate(): jnp.einsum('nij,ncjk->ncik', tile_stack, chosen, preferred_element_type=j...  89.7 us
    dot_general x64, matrix products, accumulate(): jnp.einsum('nij,ncjk->ncik', tile_stack, chosen, preferred_element_type=j...  78.3 us
    all_gather x1, blocking collectives, shards(): lax.all_gather(a_index[0, 0, 0], 'row', axis=0, tiled=True)  44.2 us
    gather x64, local copies, waits for them, and re-layouts, accumulate(): position = left_known[list_row, slot_pos]  41.6 us
    gather x64, local copies, waits for them, and re-layouts, accumulate(): usable = slot_pos < left_sizes[list_row]  41.2 us
  transfers between devices with their start and end apart: 64, of which 7 were waited for; matrix products, arithmetic and copies ran while one was open for 45% of the time, Pallas kernels for 0%

commit v1 on v0

v1 whole, which is shorter than its diff:
```python
import functools

import jax
import jax.numpy as jnp
from jax import lax
from jax.experimental import pallas as pl
from jax.experimental.pallas import tpu as pltpu
from jax.sharding import PartitionSpec as P

NZ = 8
SA = 6
SB = 2
PANELS = 4
ATILES = PANELS * SA
TILE = 128
LEFT_ROWS = ATILES * TILE
LEFT_SIDE = 16
RIGHT_ROWS = 8 * SB * TILE
RIGHT_SIDE = 32
RIGHT_PART = RIGHT_ROWS + RIGHT_SIDE
QUARTER = 1024
BOTH = ("row", "col")
ALL = ("row", "col", "depth")
HBM = pl.BlockSpec(memory_space=pltpu.HBM)
VMEM = pl.BlockSpec(memory_space=pltpu.VMEM)
SMEM = pl.BlockSpec(memory_space=pltpu.SMEM)


def gid(z, h, l, c):
    return ((z * 2 + h) * 2 + l) * 2 + c


def group():
    return [(z, h, l, c) for z in range(NZ) for h in range(2) for l in range(2) for c in range(2)]


def swap_route():
    return [(gid(z, h, l, c), gid(z, c, 1 - l, h)) for z, h, l, c in group()]


def home_route(d):
    return [(s * 4 + y, t * 4 + (y + d) % 4) for s, t in swap_route() for y in range(4)]


def z_route(d):
    return [(2 * z + h, 2 * ((z + d) % NZ) + h) for z in range(NZ) for h in range(2)]


def y_route(d):
    return [(y, (y + d) % 4) for y in range(4)]


def outer_route():
    return [(gid(z, h, l, c), gid(z, 1 - h, 1 - l, c)) for z, h, l, c in group()]


CORE_ROUTE = [(i, i ^ 1) for i in range(4)]
INNER_ROUTE = [(i, i ^ 2) for i in range(4)]


def copy_all(pairs, sem):
    copies = []
    for src, dst in pairs:
        copy = pltpu.make_async_copy(src, dst, sem.at[len(copies)])
        copy.start()
        copies.append(copy)
    return copies


def pack_kernel(ids, index, sizes, place, right_sizes, tiles, right_tiles, left, mine, theirs, wide, sem):
    c = ids[3]
    pairs = [(tiles, left.at[pl.ds(0, LEFT_ROWS)])]
    for z in range(NZ):
        rows = pl.ds(z * 256, 256)
        pairs.append((right_tiles.at[z * 2 + c], mine.at[rows]))
        pairs.append((right_tiles.at[z * 2 + 1 - c], theirs.at[rows]))
    copies = copy_all(pairs, sem)
    wide[...] = jnp.zeros_like(wide)
    wide[0:PANELS, 0:SA] = index[...].astype(jnp.float32)
    wide[8:9, 0:PANELS] = sizes[...].astype(jnp.float32)
    wide[16:32, 0:SB] = place[...].astype(jnp.float32)
    wide[32:33, 0:16] = right_sizes[...].astype(jnp.float32)
    left[LEFT_ROWS:, :] = wide[0:16, :].astype(jnp.bfloat16)
    for out in (mine, theirs):
        out[RIGHT_ROWS:, :] = wide[16:48, :].astype(jnp.bfloat16)
    for copy in copies:
        copy.wait()


def pack(ids, index, sizes, place, right_sizes, tiles, right_tiles):
    return pl.pallas_call(
        pack_kernel,
        out_shape=[jax.ShapeDtypeStruct((LEFT_ROWS + LEFT_SIDE, TILE), jnp.bfloat16)]
        + [jax.ShapeDtypeStruct((RIGHT_PART, TILE), jnp.bfloat16)] * 2,
        in_specs=[SMEM, VMEM, VMEM, VMEM, VMEM, HBM, HBM],
        out_specs=[VMEM] * 3,
        scratch_shapes=[pltpu.VMEM((48, TILE), jnp.float32), pltpu.SemaphoreType.DMA((17,))],
        name="pack",
    )(ids, index, sizes, place, right_sizes, tiles, right_tiles)


def kernel(deltas, nparts, first, outs_rows, nafter, *refs):
    n = len(deltas)
    refs = list(refs)

    def take(k):
        got = refs[:k]
        del refs[:k]
        return got

    (ids,) = take(1)
    lefts = take(n * nparts)
    rights = take(4)
    c_in = None if first else take(1)[0]
    take(nafter)
    outs = take(len(outs_rows))
    abuf, bbuf, acc, side, side_int, meta, work, side_sem, in_sem, meta_sem = refs

    z, h, l, c, y = (ids[k] for k in range(5))
    right_at = n * LEFT_SIDE
    pairs = []
    for s in range(n):
        part = lefts[s * nparts + nparts - 1]
        pairs.append(
            (part.at[pl.ds(part.shape[0] - LEFT_SIDE, LEFT_SIDE)], side.at[pl.ds(s * LEFT_SIDE, LEFT_SIDE)])
        )
    for k in range(4):
        for rel in range(2):
            pairs.append(
                (
                    rights[k].at[pl.ds(rel * RIGHT_PART + RIGHT_ROWS, RIGHT_SIDE)],
                    side.at[pl.ds(right_at + (k * 2 + rel) * RIGHT_SIDE, RIGHT_SIDE)],
                )
            )
    side_copies = copy_all(pairs, side_sem)
    size = LEFT_ROWS // nparts
    pairs = []
    for p in range(n * nparts):
        pairs.append((lefts[p].at[pl.ds(0, size)], abuf.at[pl.ds(p * size, size)]))
    for s, delta in enumerate(deltas):
        zs = (z + delta) & (NZ - 1)
        for k in range(4):
            for rel in range(2):
                rows = pl.ds(pl.multiple_of(rel * RIGHT_PART + zs * 256, 16), 256)
                pairs.append((rights[k].at[rows], bbuf.at[pl.ds((s * 8 + k * 2 + rel) * 256, 256)]))
    copies = copy_all(pairs, in_sem)

    for copy in side_copies:
        copy.wait()
    side_int[...] = side[...].astype(jnp.float32).astype(jnp.int32)
    copy = pltpu.make_async_copy(side_int, meta, meta_sem)
    copy.start()
    if first:
        acc[...] = jnp.zeros_like(acc)
    else:
        acc[pl.ds(0, 64 * TILE)] = c_in[...]
    copy.wait()

    count = jnp.int32(0)
    for s, delta in enumerate(deltas):
        a = ((z + delta) & (NZ - 1)) * 2 + c
        ra = s * LEFT_SIDE

        def panel(k, count, s=s, a=a, ra=ra):
            block_at = k >> 1
            b = (l ^ ((block_at ^ (block_at >> 1)) & 1)) * 2 + (c ^ (k & 1))
            half = (h ^ (block_at >> 1) ^ c) * 32
            rb = right_at + k * RIGHT_SIDE
            live_a = meta[ra + 8, b]
            live_b = meta[rb + 16, a]
            ta = s * ATILES + b * SA
            tb = s * 16 + k * 2
            for q in range(SB):
                place = meta[rb + a, q]
                for t in range(SA):
                    index = meta[ra + b, t]
                    i = index >> 3
                    chunk = ((i >> 2) - y) & 3
                    spot = chunk ^ (chunk >> 1)
                    block = half + (spot * 4 + (i & 3)) * 2 + (place & 1)
                    hit = ((index & 7) == (place >> 1)) & (t < live_a) & (q < live_b)
                    work[count] = (block << 20) | ((tb + q) << 10) | (ta + t)
                    count = count + hit.astype(jnp.int32)
            return count

        count = lax.fori_loop(0, 8, panel, count)
    for k in range(3):
        work[count + k] = jnp.int32(64 << 20)

    for copy in copies:
        copy.wait()

    def rows_of(k):
        return pl.ds(pl.multiple_of(k * TILE, TILE), TILE)

    def products(g, carry):
        for k in range(4):
            w = work[g * 4 + k]
            block = rows_of(w >> 20)
            acc[block] = acc[block] + jnp.dot(
                abuf[rows_of(w & 1023)], bbuf[rows_of((w >> 10) & 1023)], preferred_element_type=jnp.float32
            )
        return carry

    lax.fori_loop(0, (count + 3) >> 2, products, 0)

    for (start, size), out in zip(outs_rows, outs):
        out[...] = acc[pl.ds(start * TILE, size * TILE)]


def multiply(deltas, ids, lefts, rights, total, outs_rows, after):
    n = len(deltas)
    nparts = len(lefts) // n
    first = total is None
    operands = [ids, *lefts, *rights] + ([] if first else [total]) + list(after)
    sides = n * LEFT_SIDE + 8 * RIGHT_SIDE
    return pl.pallas_call(
        functools.partial(kernel, deltas, nparts, first, outs_rows, len(after)),
        out_shape=[jax.ShapeDtypeStruct((k * TILE, TILE), jnp.float32) for _, k in outs_rows],
        in_specs=[SMEM] + [HBM] * (len(lefts) + 4) + ([] if first else [VMEM]) + [HBM] * len(after),
        out_specs=[VMEM] * len(outs_rows),
        scratch_shapes=[
            pltpu.VMEM((n * LEFT_ROWS, TILE), jnp.bfloat16),
            pltpu.VMEM((n * 16 * TILE, TILE), jnp.bfloat16),
            pltpu.VMEM((65 * TILE, TILE), jnp.float32),
            pltpu.VMEM((sides, TILE), jnp.bfloat16),
            pltpu.VMEM((sides, TILE), jnp.int32),
            pltpu.SMEM((sides, TILE), jnp.int32),
            pltpu.SMEM((n * 96 + 8,), jnp.int32),
            pltpu.SemaphoreType.DMA((n + 8,)),
            pltpu.SemaphoreType.DMA((n * nparts + 8 * n,)),
            pltpu.SemaphoreType.DMA,
        ],
        compiler_params=pltpu.CompilerParams(vmem_limit_bytes=(24 + 2 * n) * 1024 * 1024),
        cost_estimate=pl.CostEstimate(
            flops=n * 40_000_000, bytes_accessed=8_000_000 + n * 4_000_000, transcendentals=0
        ),
        name="products_%s" % "_".join(str(d & 7) for d in deltas),
    )(*operands)


def shards(a_tiles, a_index, a_count, b_tiles, b_place, b_count):
    row = lax.axis_index("row")
    col = lax.axis_index("col")
    y = lax.axis_index("depth")
    ids = jnp.stack([row >> 1, row & 1, col >> 1, col & 1, y, y, y, y]).astype(jnp.int32)
    send = lax.ppermute
    barrier = lax.optimization_barrier

    left, mine, theirs = pack(
        ids,
        a_index.reshape(PANELS, SA),
        a_count.reshape(1, PANELS),
        b_place.reshape(16, SB),
        b_count.reshape(1, 16),
        a_tiles.reshape(LEFT_ROWS, TILE),
        b_tiles.reshape(16, SB * TILE, TILE),
    )
    own = send(left, BOTH, swap_route())
    right = jnp.concatenate([mine, send(theirs, "col", CORE_ROUTE)], axis=0)
    own, right = barrier((own, right))

    def onward(f, b):
        return send(f, "row", z_route(1)), send(b, "row", z_route(-1))

    def inner(x):
        return send(x, "col", INNER_ROUTE)

    def outer(x):
        return send(x, BOTH, outer_route())

    f1, b1 = onward(own, own)
    rest = 2 * RIGHT_PART - QUARTER
    in1, out1 = inner(right[QUARTER:]), outer(right[:rest])
    f1, b1, in1, out1 = barrier((f1, b1, in1, out1))

    f2, b2 = onward(f1, b1)
    in2 = inner(jnp.concatenate([right[:QUARTER], out1[:RIGHT_PART]], axis=0))
    out2 = outer(jnp.concatenate([right[rest:], in1[RIGHT_PART - QUARTER :]], axis=0))
    f2, b2, in2, out2 = barrier((f2, b2, in2, out2))

    f3, b3 = onward(f2, b2)
    rights = [
        right,
        jnp.concatenate([in2[:QUARTER], in1], axis=0),
        jnp.concatenate([out1, out2[:QUARTER]], axis=0),
        jnp.concatenate([in2[QUARTER:], out2[QUARTER:]], axis=0),
    ]
    whole = ((0, 64),)
    (total,) = multiply((0, -1, 1, -2, 2), ids, [own, f1, b1, f2, b2], rights, None, whole, [])

    f3, b3, total = barrier((f3, b3, total))
    half = LEFT_ROWS // 2
    far = [send(f3[:half], "row", z_route(1)), send(b3[half:], "row", z_route(-1))]
    (total,) = multiply((-3, 3), ids, [f3, b3], rights, total, whole, [])
    kept, other = multiply((4,), ids, far, rights, total, ((0, 32), (32, 32)), [])

    other = send(other, "col", CORE_ROUTE)
    half = 4 * TILE

    def unit(k, kept=kept, other=other):
        return kept[k * half : (k + 1) * half] + other[k * half : (k + 1) * half]

    units = barrier((unit(6), unit(7), unit(3), unit(4)))
    up2 = send(units[0], "depth", y_route(1))
    down2 = send(units[1], "depth", y_route(-1))
    up1 = send(units[2], "depth", y_route(1))
    down1 = send(units[3], "depth", y_route(-1))
    up3, down3, kept, other = barrier((unit(2) + up2, unit(5) + down2, kept, other))
    up3 = send(up3, ALL, home_route(1))
    down3 = send(down3, ALL, home_route(-1))
    low = send(unit(0, kept, other) + down1, BOTH, swap_route()) + up3
    high = send(unit(1, kept, other) + up1, BOTH, swap_route()) + down3
    return jnp.concatenate([low, high], axis=0).reshape(4, 2, TILE, TILE)


def solution(mesh):
    placed = (
        P("row", "col", "depth", None, None, None, None),
        P("row", "col", "depth", None, None),
        P("row", "col", "depth", None),
        P("row", "col", "depth", None, None, None, None),
        P("row", "col", "depth", None, None),
        P("row", "col", "depth", None),
    )
    return jax.shard_map(
        shards,
        mesh=mesh,
        in_specs=placed,
        out_specs=P(("col", "depth"), "row", None, None),
        check_vma=False,
    )
```

time: 1100 us -> 149 us (0.14)
  local copies, waits for them, and re-layouts: 346 us -> 2.77 us
  matrix products: 317 us -> 0 us
  starting transfers between devices: 264 us -> 36 us
  blocking collectives: 75.9 us -> 0 us
  Pallas kernels: 0 us -> 33 us
  waiting for transfers between devices: 47 us -> 73.3 us
  other arithmetic: 25.7 us -> 2.62 us
  between operations: 15.1 us -> 0.22 us
    dot_general x192 -> x0, matrix products: 317 us -> none  [the longest x64 136 us: accumulate(): jnp.dot(placer.astype(jnp.float32), product.reshape(stack_rows * NCB, -1)...]
    ppermute x63 -> x23, starting transfers between devices: 264 us -> 36 us  [the longest x6 12.4 us: onward(): return (send(f, 'row', z_route(1)), send(b, 'row', z_route(-1)))]
    gather x256 -> x0, local copies, waits for them, and re-layouts: 159 us -> none  [the longest x64 41.6 us: accumulate(): position = left_known[list_row, slot_pos]]
    transpose x64 -> x0, local copies, waits for them, and re-layouts: 89.7 us -> none  [accumulate(): jnp.einsum('nij,ncjk->ncik', tile_stack, chosen, preferred_element_type=j...]
    all_gather x4 -> x0, blocking collectives: 75.9 us -> none  [the longest x1 44.2 us: shards(): lax.all_gather(a_index[0, 0, 0], 'row', axis=0, tiled=True)]
    ppermute x63 -> x23, waiting for transfers between devices: 18.3 us -> 73.3 us  [the longest x6 35.1 us: onward(): return (send(f, 'row', z_route(1)), send(b, 'row', z_route(-1)))]
    while x270 -> x0, local copies, waits for them, and re-layouts: 37.6 us -> none
    pallas_call x0 -> x4, Pallas kernels: none -> 33 us  [the longest x3 29.4 us: multiply(): pl.pallas_call(functools.partial(kernel, deltas, nparts, first, outs_rows...]
  transfers between devices with their start and end apart: 64 -> 23, of which waited for: 7 -> 14; matrix products, arithmetic and copies ran while one was open for 45% -> 1% of each run, Pallas kernels for 0% -> 16%
where the time goes in v1:
time: 149 us; the launch traced here: 148 us
  waiting for transfers between devices  73.3 us (49%)
  starting transfers between devices  36 us (24%)
  Pallas kernels  33 us (22%)
  local copies, waits for them, and re-layouts  2.77 us (2%)
  other arithmetic  2.62 us (2%)
    ppermute x6, waiting for transfers between devices, onward(): return (send(f, 'row', z_route(1)), send(b, 'row', z_route(-1)))  35.1 us
    pallas_call x3, Pallas kernels, multiply(): pl.pallas_call(functools.partial(kernel, deltas, nparts, first, outs_rows...  29.4 us
    ppermute x6, starting transfers between devices, onward(): return (send(f, 'row', z_route(1)), send(b, 'row', z_route(-1)))  12.4 us
    ppermute x1, waiting for transfers between devices, shards(): own = send(left, BOTH, swap_route())  9.09 us
    ppermute x1, waiting for transfers between devices, shards(): down3 = send(down3, ALL, home_route(-1))  6.95 us
    ppermute x2, starting transfers between devices, outer(): return send(x, BOTH, outer_route())  5.54 us
    ppermute x1, starting transfers between devices, shards(): up2 = send(units[0], 'depth', y_route(1))  4.98 us
    ppermute x1, starting transfers between devices, shards(): down1 = send(units[3], 'depth', y_route(-1))  4.74 us
  transfers between devices with their start and end apart: 23, of which 14 were waited for; matrix products, arithmetic and copies ran while one was open for 1% of the time, Pallas kernels for 16%

profile of v1, /device:TPU:8, one launch (start us, length us, event | category | flops | bytes accessed | tf_op | source)
XLA Modules:
  0.0 147.9 jit_solution(3542339456117052066)
XLA Ops:
  0.0 1.4 copy.7.place
  1.4 0.6 stack.26.ids.refs_0_
  2.0 3.6 %pack.1 = (bf16[3088,128]{1,0:T(8,128)(2,1)}, bf16[2080,128]{1,0:T(8,128)(2,1)}, bf16[2080,128]{1,0:T(8,128)(2,1)}) custom-call(s32[8]{0:T(128)} %stack.26.ids.refs_0_, s32[4,6]{1,0:T(4,128)} %bitcast.14, s32[1,4]{1,0:T(1,128)} %bitcast.16, s32[16,2]{1,0:T(8,128)} %copy.7.place, s32[1,16]{1,0:T(1,128)} %bitcast.17, bf16[3072,128]{1,0:T(8,128)(2,1)} %bitcast.13, ...), custom_call_target="tpu_custom_call" | custom-call | tf_op jit(solution)/shard_map/pack/pallas_call | solution.py:91
  5.6 1.6 %collective-permute-start = (bf16[3088,128]{1,0:T(8,128)(2,1)}, bf16[3088,128]{1,0:T(8,128)(2,1)S(1)}, u32[]{:S(2)}, u32[]{:S(2)}) collective-permute-start(bf16[3088,128]{1,0:T(8,128)(2,1)} %get-tuple-element.31), channel_id=1, source_target_pairs={{0,8},{4,24},{8,0},{12,16},{16,12},{20,28},{24,4},{28,20},{32,40},... | collective-permute-start | bytes 2371592 | tf_op jit(solution)/shard_map/ppermute | solution.py:259
  7.8 1.1 pad_maximum_fusion.refs_6_.refs_3_
  8.9 9.1 %collective-permute-done.refs_1_ = bf16[3088,128]{1,0:T(8,128)(2,1)S(1)} collective-permute-done((bf16[3088,128]{1,0:T(8,128)(2,1)}, bf16[3088,128]{1,0:T(8,128)(2,1)S(1)}, u32[]{:S(2)}, u32[]{:S(2)}) %collective-permute-start) | collective-permute-done | bytes 790560 | tf_op jit(solution)/shard_map/ppermute | solution.py:259
  18.1 3.5 %collective-permute-start.5 = (bf16[3136,128]{1,0:T(8,128)(2,1)S(1)}, bf16[3136,128]{1,0:T(8,128)(2,1)S(1)}, u32[]{:S(2)}, u32[]{:S(2)}) collective-permute-start(bf16[3136,128]{1,0:T(8,128)(2,1)S(1)} %get-tuple-element.67), channel_id=1, source_target_pairs={{0,24},{4,28},{8,16},{12,20},{16,8},{20,12},{24,0},{28,4},{32,56},... | collective-permute-start | bytes 2408456 | tf_op jit(solution)/shard_map/ppermute | solution.py:270
  21.6 5.9 %collective-permute-start.3 = (bf16[3088,128]{1,0:T(8,128)(2,1)S(1)}, bf16[3088,128]{1,0:T(8,128)(2,1)S(1)}, u32[]{:S(2)}, u32[]{:S(2)}) collective-permute-start(bf16[3088,128]{1,0:T(8,128)(2,1)S(1)} %collective-permute-done.refs_1_), channel_id=1, source_target_pairs={{0,224},{16,240},{32,0},{48,16},{64,32},{80,48},{96,64},{112,80},{... | collective-permute-start | bytes 2371592 | tf_op jit(solution)/shard_map/ppermute | solution.py:264
  27.5 15.7 %collective-permute-done.3.refs_3_ = bf16[3088,128]{1,0:T(8,128)(2,1)S(1)} collective-permute-done((bf16[3088,128]{1,0:T(8,128)(2,1)S(1)}, bf16[3088,128]{1,0:T(8,128)(2,1)S(1)}, u32[]{:S(2)}, u32[]{:S(2)}) %collective-permute-start.3) | collective-permute-done | bytes 790560 | tf_op jit(solution)/shard_map/ppermute | solution.py:264
  43.1 3.4 %collective-permute-done.2.refs_2_ = bf16[3088,128]{1,0:T(8,128)(2,1)S(1)} collective-permute-done((bf16[3088,128]{1,0:T(8,128)(2,1)S(1)}, bf16[3088,128]{1,0:T(8,128)(2,1)S(1)}, u32[]{:S(2)}, u32[]{:S(2)}) %collective-permute-start.2) | collective-permute-done | bytes 790560 | tf_op jit(solution)/shard_map/ppermute | solution.py:264
  46.7 2.1 %collective-permute-start.9 = (bf16[3104,128]{1,0:T(8,128)(2,1)S(1)}, bf16[3104,128]{1,0:T(8,128)(2,1)S(1)}, u32[]{:S(2)}, u32[]{:S(2)}) collective-permute-start(bf16[3104,128]{1,0:T(8,128)(2,1)S(1)} %pad_maximum_fusion.5), channel_id=1, source_target_pairs={{0,24},{4,28},{8,16},{12,20},{16,8},{20,12},{24,0},{28,4},{32,56},... | collective-permute-start | bytes 2383880 | tf_op jit(solution)/shard_map/ppermute | solution.py:270
  48.8 1.2 collective-permute-start.8
  50.0 3.2 %collective-permute-start.7 = (bf16[3088,128]{1,0:T(8,128)(2,1)S(1)}, bf16[3088,128]{1,0:T(8,128)(2,1)S(1)}, u32[]{:S(2)}, u32[]{:S(2)}) collective-permute-start(bf16[3088,128]{1,0:T(8,128)(2,1)S(1)} %collective-permute-done.3.refs_3_), channel_id=1, source_target_pairs={{0,224},{16,240},{32,0},{48,16},{64,32},{80,48},{96,64},{112,80},{... | collective-permute-start | bytes 2371592 | tf_op jit(solution)/shard_map/ppermute | solution.py:264
  53.2 16.0 %collective-permute-done.6.refs_4_ = bf16[3088,128]{1,0:T(8,128)(2,1)S(1)} collective-permute-done((bf16[3088,128]{1,0:T(8,128)(2,1)S(1)}, bf16[3088,128]{1,0:T(8,128)(2,1)S(1)}, u32[]{:S(2)}, u32[]{:S(2)}) %collective-permute-start.6) | collective-permute-done | bytes 790560 | tf_op jit(solution)/shard_map/ppermute | solution.py:264
  69.5 3.2 %collective-permute-start.11 = (bf16[3088,128]{1,0:T(8,128)(2,1)S(1)}, bf16[3088,128]{1,0:T(8,128)(2,1)S(1)}, u32[]{:S(2)}, u32[]{:S(2)}) collective-permute-start(bf16[3088,128]{1,0:T(8,128)(2,1)S(1)} %collective-permute-done.7.refs_5_), channel_id=1, source_target_pairs={{0,224},{16,240},{32,0},{48,16},{64,32},{80,48},{96,64},{112,80},{... | collective-permute-start | bytes 2371592 | tf_op jit(solution)/shard_map/ppermute | solution.py:264
  73.4 15.2 %products_0_7_1_6_2.1.refs_7_ = f32[8192,128]{1,0:T(8,128)S(1)} custom-call(s32[8]{0:T(128)S(1)} %copy-done, bf16[3088,128]{1,0:T(8,128)(2,1)S(1)} %collective-permute-done.refs_1_, bf16[3088,128]{1,0:T(8,128)(2,1)S(1)} %collective-permute-done.2.refs_2_, bf16[3088,128]{1,0:T(8,128)(2,1)S(1)} %collective-permute-done.3.refs_3_, ...), custom_call_target="tpu_custom_call" | custom-call | flops 200000000 | bytes 28000000 | tf_op jit(solution)/shard_map/products_0_7_1_6_2/pallas_call | solution.py:217
  88.7 2.2 %collective-permute-start.13 = (bf16[1552,128]{1,0:T(8,128)(2,1)S(1)}, bf16[1552,128]{1,0:T(8,128)(2,1)S(1)}, u32[]{:S(2)}, u32[]{:S(2)}) collective-permute-start(bf16[1552,128]{1,0:T(8,128)(2,1)S(1)} %slice.95), channel_id=1, source_target_pairs={{0,224},{16,240},{32,0},{48,16},{64,32},{80,48},{96,64},{112,80},{... | collective-permute-start | bytes 1191944 | tf_op jit(solution)/shard_map/ppermute | solution.py:294
  91.2 7.9 %products_5_3.1.refs_7_ = f32[8192,128]{1,0:T(8,128)S(1)} custom-call(s32[8]{0:T(128)S(1)} %copy-done, bf16[3088,128]{1,0:T(8,128)(2,1)S(1)} %collective-permute-done.10.refs_1_, bf16[3088,128]{1,0:T(8,128)(2,1)S(1)} %collective-permute-done.11.refs_2_, bf16[4160,128]{1,0:T(8,128)(2,1)S(1)} %pad_maximum_fusion.refs_6_.refs_3_, ...), custom_call_target="tpu_custom_call" | custom-call | flops 80000000 | bytes 16000000 | tf_op jit(solution)/shard_map/products_5_3/pallas_call | solution.py:217
  99.1 1.0 collective-permute-done.12.refs_1_
  100.2 6.2 %products_4.1 = (f32[4096,128]{1,0:T(8,128)S(1)}, f32[4096,128]{1,0:T(8,128)S(1)}) custom-call(s32[8]{0:T(128)S(1)} %copy-done, bf16[1536,128]{1,0:T(8,128)(2,1)S(1)} %collective-permute-done.12.refs_1_, bf16[1552,128]{1,0:T(8,128)(2,1)S(1)} %collective-permute-done.13.refs_2_, bf16[4160,128]{1,0:T(8,128)(2,1)S(1)} %pad_maximum_fusion.refs_6_.refs_3_, ...), custom_call_target="tpu_custom_call" | custom-call | flops 40000000 | bytes 12000000 | tf_op jit(solution)/shard_map/products_4/pallas_call | solution.py:217
  106.5 4.1 %collective-permute-done.14 = f32[4096,128]{1,0:T(8,128)S(1)} collective-permute-done((f32[4096,128]{1,0:T(8,128)S(1)}, f32[4096,128]{1,0:T(8,128)S(1)}, u32[]{:S(2)}, u32[]{:S(2)}) %collective-permute-start.14) | collective-permute-done | bytes 2097184 | tf_op jit(solution)/shard_map/ppermute | solution.py:298
  110.8 5.0 %collective-permute-start.15 = (f32[512,128]{1,0:T(8,128)S(1)}, f32[512,128]{1,0:T(8,128)S(1)}, u32[]{:S(2)}, u32[]{:S(2)}) collective-permute-start(f32[512,128]{1,0:T(8,128)S(1)} %get-tuple-element.49), channel_id=1, source_target_pairs={{0,1},{1,2},{2,3},{3,0},{4,5},{5,6},{6,7},{7,4},{8,9},{9,10},{10,1... | collective-permute-start | bytes 786440 | tf_op jit(solution)/shard_map/ppermute | solution.py:305
  115.8 4.7 %collective-permute-start.17 = (f32[512,128]{1,0:T(8,128)S(1)}, f32[512,128]{1,0:T(8,128)S(1)}, u32[]{:S(2)}, u32[]{:S(2)}) collective-permute-start(f32[512,128]{1,0:T(8,128)S(1)} %get-tuple-element.53), channel_id=1, source_target_pairs={{0,3},{1,0},{2,1},{3,2},{4,7},{5,4},{6,5},{7,6},{8,11},{9,8},{10,9... | collective-permute-start | bytes 786440 | tf_op jit(solution)/shard_map/ppermute | solution.py:308
  120.5 1.9 %collective-permute-done.15 = f32[512,128]{1,0:T(8,128)S(1)} collective-permute-done((f32[512,128]{1,0:T(8,128)S(1)}, f32[512,128]{1,0:T(8,128)S(1)}, u32[]{:S(2)}, u32[]{:S(2)}) %collective-permute-start.15) | collective-permute-done | bytes 262176 | tf_op jit(solution)/shard_map/ppermute | solution.py:305
  122.4 4.5 %collective-permute-done.16 = f32[512,128]{1,0:T(8,128)S(1)} collective-permute-done((f32[512,128]{1,0:T(8,128)S(1)}, f32[512,128]{1,0:T(8,128)S(1)}, u32[]{:S(2)}, u32[]{:S(2)}) %collective-permute-start.16) | collective-permute-done | bytes 262176 | tf_op jit(solution)/shard_map/ppermute | solution.py:306
  127.1 4.6 %collective-permute-done.17 = f32[512,128]{1,0:T(8,128)S(1)} collective-permute-done((f32[512,128]{1,0:T(8,128)S(1)}, f32[512,128]{1,0:T(8,128)S(1)}, u32[]{:S(2)}, u32[]{:S(2)}) %collective-permute-start.17) | collective-permute-done | bytes 262176 | tf_op jit(solution)/shard_map/ppermute | solution.py:308
  131.8 2.6 %collective-permute-start.18 = (f32[512,128]{1,0:T(8,128)S(1)}, f32[512,128]{1,0:T(8,128)S(1)}, u32[]{:S(2)}, u32[]{:S(2)}) collective-permute-start(f32[512,128]{1,0:T(8,128)S(1)} %get-tuple-element.57), channel_id=1, source_target_pairs={{0,8},{4,24},{8,0},{12,16},{16,12},{20,28},{24,4},{28,20},{32,40},... | collective-permute-start | bytes 786440 | tf_op jit(solution)/shard_map/ppermute | solution.py:312
  134.7 1.9 %collective-permute-done.19 = f32[512,128]{1,0:T(8,128)S(1)} collective-permute-done((f32[512,128]{1,0:T(8,128)S(1)}, f32[512,128]{1,0:T(8,128)S(1)}, u32[]{:S(2)}, u32[]{:S(2)}) %collective-permute-start.19) | collective-permute-done | bytes 262176 | tf_op jit(solution)/shard_map/ppermute | solution.py:310
  136.5 2.7 %collective-permute-done.18 = f32[512,128]{1,0:T(8,128)S(1)} collective-permute-done((f32[512,128]{1,0:T(8,128)S(1)}, f32[512,128]{1,0:T(8,128)S(1)}, u32[]{:S(2)}, u32[]{:S(2)}) %collective-permute-start.18) | collective-permute-done | bytes 262176 | tf_op jit(solution)/shard_map/ppermute | solution.py:312
  139.2 7.0 %collective-permute-done.22 = f32[512,128]{1,0:T(8,128)S(1)} collective-permute-done((f32[512,128]{1,0:T(8,128)S(1)}, f32[512,128]{1,0:T(8,128)S(1)}, u32[]{:S(2)}, u32[]{:S(2)}) %collective-permute-start.22) | collective-permute-done | bytes 262176 | tf_op jit(solution)/shard_map/ppermute | solution.py:311
  146.2 0.8 collective-permute-done.21
  147.1 0.8 pad_maximum_fusion.6
  (43 shorter events, 2.9 us)
Async XLA Ops:
  5.5 2.2 %collective-permute-start.1 = (bf16[2080,128]{1,0:T(8,128)(2,1)}, bf16[2080,128]{1,0:T(8,128)(2,1)S(1)}, u32[]{:S(2)}, u32[]{:S(2)}) collective-permute-start(bf16[2080,128]{1,0:T(8,128)(2,1)} %get-tuple-element.33), channel_id=1, source_target_pairs={{0,4},{4,0},{8,12},{12,8},{1,5},{5,1},{9,13},{13,9},{2,6},{6,2},{1... | collective-permute-start | bytes 1597448 | tf_op jit(solution)/shard_map/ppermute | solution.py:260
  5.6 12.3 %collective-permute-start = (bf16[3088,128]{1,0:T(8,128)(2,1)}, bf16[3088,128]{1,0:T(8,128)(2,1)S(1)}, u32[]{:S(2)}, u32[]{:S(2)}) collective-permute-start(bf16[3088,128]{1,0:T(8,128)(2,1)} %get-tuple-element.31), channel_id=1, source_target_pairs={{0,8},{4,24},{8,0},{12,16},{16,12},{20,28},{24,4},{28,20},{32,40},... | collective-permute-start | bytes 2371592 | tf_op jit(solution)/shard_map/ppermute | solution.py:259
  18.1 28.4 %collective-permute-start.5 = (bf16[3136,128]{1,0:T(8,128)(2,1)S(1)}, bf16[3136,128]{1,0:T(8,128)(2,1)S(1)}, u32[]{:S(2)}, u32[]{:S(2)}) collective-permute-start(bf16[3136,128]{1,0:T(8,128)(2,1)S(1)} %get-tuple-element.67), channel_id=1, source_target_pairs={{0,24},{4,28},{8,16},{12,20},{16,8},{20,12},{24,0},{28,4},{32,56},... | collective-permute-start | bytes 2408456 | tf_op jit(solution)/shard_map/ppermute | solution.py:270
  21.6 25.0 %collective-permute-start.4 = (bf16[3136,128]{1,0:T(8,128)(2,1)S(1)}, bf16[3136,128]{1,0:T(8,128)(2,1)S(1)}, u32[]{:S(2)}, u32[]{:S(2)}) collective-permute-start(bf16[3136,128]{1,0:T(8,128)(2,1)S(1)} %get-tuple-element.68), channel_id=1, source_target_pairs={{0,8},{4,12},{8,0},{12,4},{1,9},{5,13},{9,1},{13,5},{2,10},{6,14},... | collective-permute-start | bytes 2408456 | tf_op jit(solution)/shard_map/ppermute | solution.py:267
  21.6 21.5 %collective-permute-start.3 = (bf16[3088,128]{1,0:T(8,128)(2,1)S(1)}, bf16[3088,128]{1,0:T(8,128)(2,1)S(1)}, u32[]{:S(2)}, u32[]{:S(2)}) collective-permute-start(bf16[3088,128]{1,0:T(8,128)(2,1)S(1)} %collective-permute-done.refs_1_), channel_id=1, source_target_pairs={{0,224},{16,240},{32,0},{48,16},{64,32},{80,48},{96,64},{112,80},{... | collective-permute-start | bytes 2371592 | tf_op jit(solution)/shard_map/ppermute | solution.py:264
  27.4 19.1 %collective-permute-start.2 = (bf16[3088,128]{1,0:T(8,128)(2,1)S(1)}, bf16[3088,128]{1,0:T(8,128)(2,1)S(1)}, u32[]{:S(2)}, u32[]{:S(2)}) collective-permute-start(bf16[3088,128]{1,0:T(8,128)(2,1)S(1)} %collective-permute-done.refs_1_), channel_id=1, source_target_pairs={{0,32},{16,48},{32,64},{48,80},{64,96},{80,112},{96,128},{112,144}... | collective-permute-start | bytes 2371592 | tf_op jit(solution)/shard_map/ppermute | solution.py:264
  46.7 22.6 %collective-permute-start.9 = (bf16[3104,128]{1,0:T(8,128)(2,1)S(1)}, bf16[3104,128]{1,0:T(8,128)(2,1)S(1)}, u32[]{:S(2)}, u32[]{:S(2)}) collective-permute-start(bf16[3104,128]{1,0:T(8,128)(2,1)S(1)} %pad_maximum_fusion.5), channel_id=1, source_target_pairs={{0,24},{4,28},{8,16},{12,20},{16,8},{20,12},{24,0},{28,4},{32,56},... | collective-permute-start | bytes 2383880 | tf_op jit(solution)/shard_map/ppermute | solution.py:270
  48.8 20.5 %collective-permute-start.8 = (bf16[3104,128]{1,0:T(8,128)(2,1)S(1)}, bf16[3104,128]{1,0:T(8,128)(2,1)S(1)}, u32[]{:S(2)}, u32[]{:S(2)}) collective-permute-start(bf16[3104,128]{1,0:T(8,128)(2,1)S(1)} %pad_maximum_fusion.4), channel_id=1, source_target_pairs={{0,8},{4,12},{8,0},{12,4},{1,9},{5,13},{9,1},{13,5},{2,10},{6,14},... | collective-permute-start | bytes 2383880 | tf_op jit(solution)/shard_map/ppermute | solution.py:267
  50.0 19.3 %collective-permute-start.6 = (bf16[3088,128]{1,0:T(8,128)(2,1)S(1)}, bf16[3088,128]{1,0:T(8,128)(2,1)S(1)}, u32[]{:S(2)}, u32[]{:S(2)}) collective-permute-start(bf16[3088,128]{1,0:T(8,128)(2,1)S(1)} %collective-permute-done.2.refs_2_), channel_id=1, source_target_pairs={{0,32},{16,48},{32,64},{48,80},{64,96},{80,112},{96,128},{112,144}... | collective-permute-start | bytes 2371592 | tf_op jit(solution)/shard_map/ppermute | solution.py:264
  50.0 19.3 %collective-permute-start.7 = (bf16[3088,128]{1,0:T(8,128)(2,1)S(1)}, bf16[3088,128]{1,0:T(8,128)(2,1)S(1)}, u32[]{:S(2)}, u32[]{:S(2)}) collective-permute-start(bf16[3088,128]{1,0:T(8,128)(2,1)S(1)} %collective-permute-done.3.refs_3_), channel_id=1, source_target_pairs={{0,224},{16,240},{32,0},{48,16},{64,32},{80,48},{96,64},{112,80},{... | collective-permute-start | bytes 2371592 | tf_op jit(solution)/shard_map/ppermute | solution.py:264
  69.4 19.3 %collective-permute-start.10 = (bf16[3088,128]{1,0:T(8,128)(2,1)S(1)}, bf16[3088,128]{1,0:T(8,128)(2,1)S(1)}, u32[]{:S(2)}, u32[]{:S(2)}) collective-permute-start(bf16[3088,128]{1,0:T(8,128)(2,1)S(1)} %collective-permute-done.6.refs_4_), channel_id=1, source_target_pairs={{0,32},{16,48},{32,64},{48,80},{64,96},{80,112},{96,128},{112,144}... | collective-permute-start | bytes 2371592 | tf_op jit(solution)/shard_map/ppermute | solution.py:264
  69.5 19.2 %collective-permute-start.11 = (bf16[3088,128]{1,0:T(8,128)(2,1)S(1)}, bf16[3088,128]{1,0:T(8,128)(2,1)S(1)}, u32[]{:S(2)}, u32[]{:S(2)}) collective-permute-start(bf16[3088,128]{1,0:T(8,128)(2,1)S(1)} %collective-permute-done.7.refs_5_), channel_id=1, source_target_pairs={{0,224},{16,240},{32,0},{48,16},{64,32},{80,48},{96,64},{112,80},{... | collective-permute-start | bytes 2371592 | tf_op jit(solution)/shard_map/ppermute | solution.py:264
  72.8 0.6 copy-start
  88.7 11.5 %collective-permute-start.13 = (bf16[1552,128]{1,0:T(8,128)(2,1)S(1)}, bf16[1552,128]{1,0:T(8,128)(2,1)S(1)}, u32[]{:S(2)}, u32[]{:S(2)}) collective-permute-start(bf16[1552,128]{1,0:T(8,128)(2,1)S(1)} %slice.95), channel_id=1, source_target_pairs={{0,224},{16,240},{32,0},{48,16},{64,32},{80,48},{96,64},{112,80},{... | collective-permute-start | bytes 1191944 | tf_op jit(solution)/shard_map/ppermute | solution.py:294
  90.9 9.2 %collective-permute-start.12 = (bf16[1536,128]{1,0:T(8,128)(2,1)S(1)}, bf16[1536,128]{1,0:T(8,128)(2,1)S(1)}, u32[]{:S(2)}, u32[]{:S(2)}) collective-permute-start(bf16[1536,128]{1,0:T(8,128)(2,1)S(1)} %slice.94), channel_id=1, source_target_pairs={{0,32},{16,48},{32,64},{48,80},{64,96},{80,112},{96,128},{112,144}... | collective-permute-start | bytes 1179656 | tf_op jit(solution)/shard_map/ppermute | solution.py:294
  106.4 4.2 %collective-permute-start.14 = (f32[4096,128]{1,0:T(8,128)S(1)}, f32[4096,128]{1,0:T(8,128)S(1)}, u32[]{:S(2)}, u32[]{:S(2)}) collective-permute-start(f32[4096,128]{1,0:T(8,128)S(1)} %get-tuple-element.48), channel_id=1, source_target_pairs={{0,4},{4,0},{8,12},{12,8},{1,5},{5,1},{9,13},{13,9},{2,6},{6,2},{1... | collective-permute-start | bytes 6291464 | tf_op jit(solution)/shard_map/ppermute | solution.py:298
  110.8 11.7 %collective-permute-start.15 = (f32[512,128]{1,0:T(8,128)S(1)}, f32[512,128]{1,0:T(8,128)S(1)}, u32[]{:S(2)}, u32[]{:S(2)}) collective-permute-start(f32[512,128]{1,0:T(8,128)S(1)} %get-tuple-element.49), channel_id=1, source_target_pairs={{0,1},{1,2},{2,3},{3,0},{4,5},{5,6},{6,7},{7,4},{8,9},{9,10},{10,1... | collective-permute-start | bytes 786440 | tf_op jit(solution)/shard_map/ppermute | solution.py:305
  115.7 11.2 %collective-permute-start.16 = (f32[512,128]{1,0:T(8,128)S(1)}, f32[512,128]{1,0:T(8,128)S(1)}, u32[]{:S(2)}, u32[]{:S(2)}) collective-permute-start(f32[512,128]{1,0:T(8,128)S(1)} %get-tuple-element.50), channel_id=1, source_target_pairs={{0,3},{1,0},{2,1},{3,2},{4,7},{5,4},{6,5},{7,6},{8,11},{9,8},{10,9... | collective-permute-start | bytes 786440 | tf_op jit(solution)/shard_map/ppermute | solution.py:306
  115.8 16.0 %collective-permute-start.17 = (f32[512,128]{1,0:T(8,128)S(1)}, f32[512,128]{1,0:T(8,128)S(1)}, u32[]{:S(2)}, u32[]{:S(2)}) collective-permute-start(f32[512,128]{1,0:T(8,128)S(1)} %get-tuple-element.53), channel_id=1, source_target_pairs={{0,3},{1,0},{2,1},{3,2},{4,7},{5,4},{6,5},{7,6},{8,11},{9,8},{10,9... | collective-permute-start | bytes 786440 | tf_op jit(solution)/shard_map/ppermute | solution.py:308
  120.5 11.2 %collective-permute-start.20 = (f32[512,128]{1,0:T(8,128)S(1)}, f32[512,128]{1,0:T(8,128)S(1)}, u32[]{:S(2)}, u32[]{:S(2)}) collective-permute-start(f32[512,128]{1,0:T(8,128)S(1)} %get-tuple-element.55), channel_id=1, source_target_pairs={{0,1},{1,2},{2,3},{3,0},{4,5},{5,6},{6,7},{7,4},{8,9},{9,10},{10,1... | collective-permute-start | bytes 786440 | tf_op jit(solution)/shard_map/ppermute | solution.py:307
  127.0 9.5 %collective-permute-start.19 = (f32[512,128]{1,0:T(8,128)S(1)}, f32[512,128]{1,0:T(8,128)S(1)}, u32[]{:S(2)}, u32[]{:S(2)}) collective-permute-start(f32[512,128]{1,0:T(8,128)S(1)} %get-tuple-element.54), channel_id=1, source_target_pairs={{0,9},{1,10},{2,11},{3,8},{4,25},{5,26},{6,27},{7,24},{8,1},{9,2},... | collective-permute-start | bytes 786440 | tf_op jit(solution)/shard_map/ppermute | solution.py:310
  131.8 7.4 %collective-permute-start.18 = (f32[512,128]{1,0:T(8,128)S(1)}, f32[512,128]{1,0:T(8,128)S(1)}, u32[]{:S(2)}, u32[]{:S(2)}) collective-permute-start(f32[512,128]{1,0:T(8,128)S(1)} %get-tuple-element.57), channel_id=1, source_target_pairs={{0,8},{4,24},{8,0},{12,16},{16,12},{20,28},{24,4},{28,20},{32,40},... | collective-permute-start | bytes 786440 | tf_op jit(solution)/shard_map/ppermute | solution.py:312
  134.5 11.7 %collective-permute-start.22 = (f32[512,128]{1,0:T(8,128)S(1)}, f32[512,128]{1,0:T(8,128)S(1)}, u32[]{:S(2)}, u32[]{:S(2)}) collective-permute-start(f32[512,128]{1,0:T(8,128)S(1)} %get-tuple-element.56), channel_id=1, source_target_pairs={{0,11},{1,8},{2,9},{3,10},{4,27},{5,24},{6,25},{7,26},{8,3},{9,0},... | collective-permute-start | bytes 786440 | tf_op jit(solution)/shard_map/ppermute | solution.py:311
  134.5 12.6 %collective-permute-start.21 = (f32[512,128]{1,0:T(8,128)S(1)}, f32[512,128]{1,0:T(8,128)S(1)}, u32[]{:S(2)}, u32[]{:S(2)}) collective-permute-start(f32[512,128]{1,0:T(8,128)S(1)} %get-tuple-element.58), channel_id=1, source_target_pairs={{0,8},{4,24},{8,0},{12,16},{16,12},{20,28},{24,4},{28,20},{32,40},... | collective-permute-start | bytes 786440 | tf_op jit(solution)/shard_map/ppermute | solution.py:313

commit v2 on v1

v2 whole, which is shorter than its diff:
```python
import functools

import jax
import jax.numpy as jnp
from jax import lax
from jax.experimental import pallas as pl
from jax.experimental.pallas import tpu as pltpu
from jax.sharding import PartitionSpec as P

NZ = 8
SA = 6
SB = 2
PANELS = 4
ATILES = PANELS * SA
TILE = 128
LEFT_ROWS = ATILES * TILE
RIGHT_ROWS = 8 * SB * TILE
QUARTER = 1024
BOTH = ("row", "col")
ALL = ("row", "col", "depth")
HBM = pl.BlockSpec(memory_space=pltpu.HBM)
VMEM = pl.BlockSpec(memory_space=pltpu.VMEM)
SMEM = pl.BlockSpec(memory_space=pltpu.SMEM)


def gid(z, h, l, c):
    return ((z * 2 + h) * 2 + l) * 2 + c


def group():
    return [(z, h, l, c) for z in range(NZ) for h in range(2) for l in range(2) for c in range(2)]


def swap_route():
    return [(gid(z, h, l, c), gid(z, c, 1 - l, h)) for z, h, l, c in group()]


def home_route(d):
    return [(s * 4 + y, t * 4 + (y + d) % 4) for s, t in swap_route() for y in range(4)]


def z_route(d):
    return [(2 * z + h, 2 * ((z + d) % NZ) + h) for z in range(NZ) for h in range(2)]


def y_route(d):
    return [(y, (y + d) % 4) for y in range(4)]


def outer_route():
    return [(gid(z, h, l, c), gid(z, 1 - h, 1 - l, c)) for z, h, l, c in group()]


BITS = (3, 4, 5, 1, 0, 2)


def slot(offset):
    return sum(((offset >> bit) & 1) << k for k, bit in enumerate(BITS))


CORE_ROUTE = [(i, i ^ 1) for i in range(4)]
INNER_ROUTE = [(i, i ^ 2) for i in range(4)]


def copy_all(pairs, sem):
    copies = []
    for src, dst in pairs:
        copy = pltpu.make_async_copy(src, dst, sem.at[len(copies)])
        copy.start()
        copies.append(copy)
    return copies


def kernel(deltas, parts, tiles, first, outs_rows, *refs):
    n = len(deltas)
    nparts = len(parts)
    refs = list(refs)

    def take(k):
        got = refs[:k]
        del refs[:k]
        return got

    ids, meta = take(2)
    lefts = take(n * nparts)
    rights = take(4)
    c_in = None if first else take(1)[0]
    outs = take(len(outs_rows))
    abuf, bbuf, acc, work, in_sem = refs

    z, h, l, c, y = (ids[k] for k in range(5))
    me = gid(z, h, l, c)
    pairs = []
    for s in range(n):
        spot = s * tiles * TILE
        for p, (start, size) in enumerate(parts):
            pairs.append((lefts[s * nparts + p].at[pl.ds(start, size)], abuf.at[pl.ds(spot, size)]))
            spot += size
    for s, delta in enumerate(deltas):
        zs = (z + delta) & (NZ - 1)
        for k in range(4):
            for rel in range(2):
                rows = pl.ds(pl.multiple_of(rel * RIGHT_ROWS + zs * 256, 256), 256)
                pairs.append((rights[k].at[rows], bbuf.at[pl.ds((s * 8 + k * 2 + rel) * 256, 256)]))
    copies = copy_all(pairs, in_sem)

    if first:
        acc[...] = jnp.zeros_like(acc)
    else:
        acc[pl.ds(0, 64 * TILE)] = c_in[...]

    count = jnp.int32(0)
    for s, delta in enumerate(deltas):
        zs = (z + delta) & (NZ - 1)
        ra = slot(gid(zs, c, 1 - l, h) ^ me)

        def panel(k, count, s=s, zs=zs, ra=ra):
            at = k >> 1
            b_l = l ^ ((at ^ (at >> 1)) & 1)
            b_c = c ^ (k & 1)
            b = b_l * 2 + b_c
            rb = slot(gid(z, h ^ (at >> 1), b_l, b_c) ^ me)
            half = (h ^ (at >> 1) ^ c) * 32
            base = 32 + (zs * 2 + c) * 4
            live_a = meta[ra, b * 8 + 6]
            live_b = meta[rb, base + 2]
            ta = s * tiles + b * SA
            tb = s * 16 + k * 2
            for q in range(SB):
                place = meta[rb, base + q]
                for t in range(SA):
                    index = meta[ra, b * 8 + t]
                    i = index >> 3
                    chunk = ((i >> 2) - y) & 3
                    spot = chunk ^ (chunk >> 1)
                    block = half + (spot * 4 + (i & 3)) * 2 + (place & 1)
                    hit = ((index & 7) == (place >> 1)) & (t < live_a) & (q < live_b)
                    work[count] = (block << 20) | ((tb + q) << 10) | (ta + t)
                    count = count + hit.astype(jnp.int32)
            return count

        count = lax.fori_loop(0, 8, panel, count)
    for k in range(3):
        work[count + k] = jnp.int32(64 << 20)

    for copy in copies:
        copy.wait()

    def rows_of(k):
        return pl.ds(pl.multiple_of(k * TILE, TILE), TILE)

    def products(g, carry):
        for k in range(4):
            w = work[g * 4 + k]
            block = rows_of(w >> 20)
            acc[block] = acc[block] + jnp.dot(
                abuf[rows_of(w & 1023)], bbuf[rows_of((w >> 10) & 1023)], preferred_element_type=jnp.float32
            )
        return carry

    lax.fori_loop(0, (count + 3) >> 2, products, 0)

    for (start, size), out in zip(outs_rows, outs):
        out[...] = acc[pl.ds(start * TILE, size * TILE)]


def multiply(deltas, parts, tiles, ids, meta, lefts, rights, total, outs_rows):
    n = len(deltas)
    first = total is None
    operands = [ids, meta, *lefts, *rights] + ([] if first else [total])
    return pl.pallas_call(
        functools.partial(kernel, deltas, parts, tiles, first, outs_rows),
        out_shape=[jax.ShapeDtypeStruct((k * TILE, TILE), jnp.float32) for _, k in outs_rows],
        in_specs=[SMEM, SMEM] + [HBM] * (len(lefts) + 4) + ([] if first else [VMEM]),
        out_specs=[VMEM] * len(outs_rows),
        scratch_shapes=[
            pltpu.VMEM((n * tiles * TILE, TILE), jnp.bfloat16),
            pltpu.VMEM((n * 16 * TILE, TILE), jnp.bfloat16),
            pltpu.VMEM((65 * TILE, TILE), jnp.float32),
            pltpu.SMEM((n * 96 + 8,), jnp.int32),
            pltpu.SemaphoreType.DMA((len(lefts) + 8 * n,)),
        ],
        compiler_params=pltpu.CompilerParams(vmem_limit_bytes=(24 + 2 * n) * 1024 * 1024),
        cost_estimate=pl.CostEstimate(
            flops=n * 40_000_000, bytes_accessed=8_000_000 + n * 4_000_000, transcendentals=0
        ),
        name="products_%s" % "_".join(str(d & 7) for d in deltas),
    )(*operands)


send = lax.ppermute
barrier = lax.optimization_barrier


def onward(f, b):
    return send(f, "row", z_route(1)), send(b, "row", z_route(-1))


def inner(x):
    return send(x, "col", INNER_ROUTE)


def outer(x):
    return send(x, BOTH, outer_route())


REST = 2 * RIGHT_ROWS - QUARTER


def spread(meta, bit):
    return jnp.concatenate([meta, send(meta, BOTH, [(i, i ^ (1 << bit)) for i in range(64)])], axis=0)


def shards(a_tiles, a_index, a_count, b_tiles, b_place, b_count):
    row = lax.axis_index("row")
    col = lax.axis_index("col")
    y = lax.axis_index("depth")
    core = col & 1
    ids = jnp.stack([row >> 1, row & 1, col >> 1, core, y, y, y, y]).astype(jnp.int32)

    own = send(a_tiles.reshape(LEFT_ROWS, TILE), BOTH, swap_route())
    tiles = b_tiles.reshape(NZ, 2, SB * TILE, TILE)
    mine = lax.dynamic_index_in_dim(tiles, core, 1, keepdims=False).reshape(RIGHT_ROWS, TILE)
    theirs = lax.dynamic_index_in_dim(tiles, 1 - core, 1, keepdims=False).reshape(RIGHT_ROWS, TILE)
    right = jnp.concatenate([mine, send(theirs, "col", CORE_ROUTE)], axis=0)
    left_meta = jnp.pad(a_index.reshape(PANELS, SA), ((0, 0), (0, 2))) + jnp.pad(
        a_count.reshape(PANELS, 1), ((0, 0), (6, 1))
    )
    right_meta = jnp.pad(b_place.reshape(16, SB), ((0, 0), (0, 2))) + jnp.pad(
        b_count.reshape(16, 1), ((0, 0), (2, 1))
    )
    meta = jnp.concatenate(
        [left_meta.reshape(1, 32), right_meta.reshape(1, 64), jnp.zeros((1, 32), jnp.int32)], axis=1
    )
    for bit in BITS[:3]:
        meta = spread(meta, bit)
    own, meta = barrier((own, meta))

    f1, b1 = onward(own, own)
    meta = spread(meta, BITS[3])
    right, meta = barrier((right, meta))
    in1, out1 = inner(right[QUARTER:]), outer(right[:REST])
    meta = spread(meta, BITS[4])
    f1, b1 = barrier((f1, b1))

    f2, b2 = onward(f1, b1)
    in1, out1, meta = barrier((in1, out1, meta))
    meta = spread(meta, BITS[5])
    in2 = jnp.concatenate([right[:QUARTER], out1[:RIGHT_ROWS]], axis=0)
    out2 = jnp.concatenate([right[REST:], in1[RIGHT_ROWS - QUARTER :]], axis=0)
    in2, out2, meta = barrier((in2, out2, meta))
    in2, out2 = inner(in2), outer(out2)
    f2, b2 = barrier((f2, b2))

    f3, b3 = onward(f2, b2)
    rights = [
        right,
        jnp.concatenate([in2[:QUARTER], in1], axis=0),
        jnp.concatenate([out1, out2[:QUARTER]], axis=0),
        jnp.concatenate([in2[QUARTER:], out2[QUARTER:]], axis=0),
    ]
    near = LEFT_ROWS // 2
    one = ((0, LEFT_ROWS),)
    two = ((0, near), (0, LEFT_ROWS - near))
    whole = ((0, 64),)
    (total,) = multiply(
        (0, -1, 1, -2, 2), one, ATILES, ids, meta, [own, f1, b1, f2, b2], rights, None, whole
    )
    f3, b3, total = barrier((f3, b3, total))
    far = [send(f3[:near], "row", z_route(1)), send(b3[near:], "row", z_route(-1))]
    (total,) = multiply((-3, 3), one, ATILES, ids, meta, [f3, b3], rights, total, whole)
    kept, other = multiply((4,), two, ATILES, ids, meta, far, rights, total, ((0, 32), (32, 32)))

    other = send(other, "col", CORE_ROUTE)
    half = 4 * TILE

    def unit(k, count=1):
        rows = slice(k * half, (k + count) * half)
        return kept[rows] + other[rows]

    units = barrier((unit(6), unit(7), unit(3), unit(4), unit(0, 2)))
    up2 = send(units[0], "depth", y_route(1))
    down2 = send(units[1], "depth", y_route(-1))
    still = send(units[4], BOTH, swap_route())
    up1 = send(units[2], ALL, home_route(1))
    down1 = send(units[3], ALL, home_route(-1))
    up2, down2, still = barrier((up2, down2, still))
    up3 = send(unit(2) + up2, ALL, home_route(1))
    down3 = send(unit(5) + down2, ALL, home_route(-1))
    low = still[:half] + down1 + up3
    high = still[half:] + up1 + down3
    return jnp.concatenate([low, high], axis=0).reshape(4, 2, TILE, TILE)


def solution(mesh):
    placed = (
        P("row", "col", "depth", None, None, None, None),
        P("row", "col", "depth", None, None),
        P("row", "col", "depth", None),
        P("row", "col", "depth", None, None, None, None),
        P("row", "col", "depth", None, None),
        P("row", "col", "depth", None),
    )
    return jax.shard_map(
        shards,
        mesh=mesh,
        in_specs=placed,
        out_specs=P(("col", "depth"), "row", None, None),
        check_vma=False,
    )
```

time: 149 us -> 135 us (0.906)
  waiting for transfers between devices: 73.3 us -> 54.3 us
  starting transfers between devices: 36 us -> 47 us
  Pallas kernels: 33 us -> 24 us
  local copies, waits for them, and re-layouts: 2.77 us -> 6.09 us
    ppermute x9 -> x14, starting transfers between devices: 11.7 us -> 26.8 us  [the longest x6 14 us: spread(): send(meta, BOTH, [(i, i ^ 1 << bit) for i in range(64)])]
    ppermute x6, waiting for transfers between devices: 35.1 us -> 20.9 us  [onward(): return (send(f, 'row', z_route(1)), send(b, 'row', z_route(-1)))]
    pallas_call x4 -> x3, Pallas kernels: 33 us -> 24 us  [multiply(): pl.pallas_call(functools.partial(kernel, deltas, parts, tiles, first, out...]
    ppermute x9 -> x14, waiting for transfers between devices: 27.1 us -> 19.9 us  [the longest x6 8.53 us: spread(): send(meta, BOTH, [(i, i ^ 1 << bit) for i in range(64)])]
    ppermute x2, starting transfers between devices: 5.54 us -> 1.6 us  [outer(): return send(x, BOTH, outer_route())]
    ppermute x1, starting transfers between devices: 4.98 us -> 3.33 us  [shards(): up2 = send(units[0], 'depth', y_route(1))]
    concatenate x2 -> x9, other arithmetic: 0.11 us -> 1.61 us  [the longest x1 1.22 us: shards(): in2 = jnp.concatenate([right[:QUARTER], out1[:RIGHT_ROWS]], axis=0)]
  transfers between devices with their start and end apart: 23 -> 28, of which waited for: 14 -> 15; matrix products, arithmetic and copies ran while one was open for 1% -> 6% of each run, Pallas kernels for 16% -> 14%
where the time goes in v2:
time: 135 us
  waiting for transfers between devices  54.3 us (40%)
  starting transfers between devices  47 us (35%)
  Pallas kernels  24 us (18%)
  local copies, waits for them, and re-layouts  6.09 us (5%)
  other arithmetic  3.11 us (2%)
    pallas_call x3, Pallas kernels, multiply(): pl.pallas_call(functools.partial(kernel, deltas, parts, tiles, first, out...  24 us
    ppermute x6, waiting for transfers between devices, onward(): return (send(f, 'row', z_route(1)), send(b, 'row', z_route(-1)))  20.9 us
    ppermute x6, starting transfers between devices, spread(): send(meta, BOTH, [(i, i ^ 1 << bit) for i in range(64)])  14 us
    ppermute x6, starting transfers between devices, onward(): return (send(f, 'row', z_route(1)), send(b, 'row', z_route(-1)))  11.2 us
    ppermute x6, waiting for transfers between devices, spread(): send(meta, BOTH, [(i, i ^ 1 << bit) for i in range(64)])  8.53 us
    ppermute x1, waiting for transfers between devices, shards(): up3 = send(unit(2) + up2, ALL, home_route(1))  6.54 us
    ppermute x1, waiting for transfers between devices, shards(): down2 = send(units[1], 'depth', y_route(-1))  5.62 us
    ppermute x1, waiting for transfers between devices, shards(): down3 = send(unit(5) + down2, ALL, home_route(-1))  4.8 us
  transfers between devices with their start and end apart: 28, of which 15 were waited for; matrix products, arithmetic and copies ran while one was open for 6% of the time, Pallas kernels for 14%

profile of v2, /device:TPU:8, one launch (start us, length us, event | category | flops | bytes accessed | tf_op | source)
XLA Modules:
  0.0 134.8 jit_solution(12319180545128650437)
XLA Ops:
  0.0 1.6 %collective-permute-start.1 = (bf16[3072,128]{1,0:T(8,128)(2,1)}, bf16[3072,128]{1,0:T(8,128)(2,1)S(1)}, u32[]{:S(2)}, u32[]{:S(2)}) collective-permute-start(bf16[3072,128]{1,0:T(8,128)(2,1)} %bitcast.25), channel_id=1, source_target_pairs={{0,8},{4,24},{8,0},{12,16},{16,12},{20,28},{24,4},{28,20},{32,40},... | collective-permute-start | bytes 2359304 | tf_op jit(solution)/shard_map/ppermute | solution.py:221
  1.6 1.3 constant_dynamic-slice_fusion.1
  2.9 1.5 %collective-permute-start = (bf16[2048,128]{1,0:T(8,128)(2,1)S(1)}, bf16[2048,128]{1,0:T(8,128)(2,1)S(1)}, u32[]{:S(2)}, u32[]{:S(2)}) collective-permute-start(bf16[2048,128]{1,0:T(8,128)(2,1)S(1)} %bitcast.20), channel_id=1, source_target_pairs={{0,4},{4,0},{8,12},{12,8},{1,5},{5,1},{9,13},{13,9},{2,6},{6,2},{1... | collective-permute-start | bytes 1572872 | tf_op jit(solution)/shard_map/ppermute | solution.py:225
  4.9 1.9 %collective-permute-start.2 = (s32[1,128]{1,0:T(1,128)S(1)}, s32[1,128]{1,0:T(1,128)S(1)}, u32[]{:S(2)}, u32[]{:S(2)}) collective-permute-start(s32[1,128]{1,0:T(1,128)S(1)} %pad_add_fusion.8), channel_id=1, source_target_pairs={{0,32},{4,36},{8,40},{12,44},{16,48},{20,52},{24,56},{28,60},{32,0... | collective-permute-start | bytes 1544 | tf_op jit(solution)/shard_map/ppermute | solution.py:211
  6.8 1.6 %collective-permute-done.2 = s32[1,128]{1,0:T(1,128)S(1)} collective-permute-done((s32[1,128]{1,0:T(1,128)S(1)}, s32[1,128]{1,0:T(1,128)S(1)}, u32[]{:S(2)}, u32[]{:S(2)}) %collective-permute-start.2) | collective-permute-done | bytes 544 | tf_op jit(solution)/shard_map/ppermute | solution.py:211
  8.5 3.3 %collective-permute-start.3 = (s32[2,128]{1,0:T(2,128)S(1)}, s32[2,128]{1,0:T(2,128)S(1)}, u32[]{:S(2)}, u32[]{:S(2)}) collective-permute-start(s32[2,128]{1,0:T(2,128)S(1)} %pad_add_fusion.7), channel_id=1, source_target_pairs={{0,64},{4,68},{8,72},{12,76},{16,80},{20,84},{24,88},{28,92},{32,9... | collective-permute-start | bytes 3080 | tf_op jit(solution)/shard_map/ppermute | solution.py:211
  11.8 1.5 %collective-permute-done.3 = s32[2,128]{1,0:T(2,128)S(1)} collective-permute-done((s32[2,128]{1,0:T(2,128)S(1)}, s32[2,128]{1,0:T(2,128)S(1)}, u32[]{:S(2)}, u32[]{:S(2)}) %collective-permute-start.3) | collective-permute-done | bytes 1056 | tf_op jit(solution)/shard_map/ppermute | solution.py:211
  13.5 6.9 %collective-permute-start.4 = (s32[4,128]{1,0:T(4,128)S(1)}, s32[4,128]{1,0:T(4,128)S(1)}, u32[]{:S(2)}, u32[]{:S(2)}) collective-permute-start(s32[4,128]{1,0:T(4,128)S(1)} %pad_add_fusion.4), channel_id=1, source_target_pairs={{0,128},{4,132},{8,136},{12,140},{16,144},{20,148},{24,152},{28,15... | collective-permute-start | bytes 6152 | tf_op jit(solution)/shard_map/ppermute | solution.py:211
  20.3 1.6 %collective-permute-done.4 = s32[4,128]{1,0:T(4,128)S(1)} collective-permute-done((s32[4,128]{1,0:T(4,128)S(1)}, s32[4,128]{1,0:T(4,128)S(1)}, u32[]{:S(2)}, u32[]{:S(2)}) %collective-permute-start.4) | collective-permute-done | bytes 2080 | tf_op jit(solution)/shard_map/ppermute | solution.py:211
  22.3 4.8 %collective-permute-start.11 = (bf16[3072,128]{1,0:T(8,128)(2,1)S(1)}, bf16[3072,128]{1,0:T(8,128)(2,1)S(1)}, u32[]{:S(2)}, u32[]{:S(2)}) collective-permute-start(bf16[3072,128]{1,0:T(8,128)(2,1)S(1)} %collective-permute-done.1.refs_2_), channel_id=1, source_target_pairs={{0,224},{16,240},{32,0},{48,16},{64,32},{80,48},{96,64},{112,80},{... | collective-permute-start | bytes 2359304 | tf_op jit(solution)/shard_map/ppermute | solution.py:196
  27.2 1.3 collective-permute-start.7
  30.4 10.2 %collective-permute-done.11.refs_4_ = bf16[3072,128]{1,0:T(8,128)(2,1)S(1)} collective-permute-done((bf16[3072,128]{1,0:T(8,128)(2,1)S(1)}, bf16[3072,128]{1,0:T(8,128)(2,1)S(1)}, u32[]{:S(2)}, u32[]{:S(2)}) %collective-permute-start.11) | collective-permute-done | bytes 786464 | tf_op jit(solution)/shard_map/ppermute | solution.py:196
  40.6 4.2 %collective-permute-done.10.refs_3_ = bf16[3072,128]{1,0:T(8,128)(2,1)S(1)} collective-permute-done((bf16[3072,128]{1,0:T(8,128)(2,1)S(1)}, bf16[3072,128]{1,0:T(8,128)(2,1)S(1)}, u32[]{:S(2)}, u32[]{:S(2)}) %collective-permute-start.10) | collective-permute-done | bytes 786464 | tf_op jit(solution)/shard_map/ppermute | solution.py:196
  44.8 3.2 %collective-permute-start.13 = (bf16[3072,128]{1,0:T(8,128)(2,1)S(1)}, bf16[3072,128]{1,0:T(8,128)(2,1)}, u32[]{:S(2)}, u32[]{:S(2)}) collective-permute-start(bf16[3072,128]{1,0:T(8,128)(2,1)S(1)} %collective-permute-done.11.refs_4_), channel_id=1, source_target_pairs={{0,224},{16,240},{32,0},{48,16},{64,32},{80,48},{96,64},{112,80},{... | collective-permute-start | bytes 2359304 | tf_op jit(solution)/shard_map/ppermute | solution.py:196
  48.0 1.6 %collective-permute-start.9 = (s32[32,128]{1,0:T(8,128)S(1)}, s32[32,128]{1,0:T(8,128)S(1)}, u32[]{:S(2)}, u32[]{:S(2)}) collective-permute-start(s32[32,128]{1,0:T(8,128)S(1)} %pad_add_fusion.1), channel_id=1, source_target_pairs={{0,16},{4,20},{8,24},{12,28},{16,0},{20,4},{24,8},{28,12},{32,48},... | collective-permute-start | bytes 49160 | tf_op jit(solution)/shard_map/ppermute | solution.py:211
  49.7 1.2 pad_maximum_fusion.4
  50.9 2.7 %collective-permute-done.9 = s32[32,128]{1,0:T(8,128)S(1)} collective-permute-done((s32[32,128]{1,0:T(8,128)S(1)}, s32[32,128]{1,0:T(8,128)S(1)}, u32[]{:S(2)}, u32[]{:S(2)}) %collective-permute-start.9) | collective-permute-done | bytes 16416 | tf_op jit(solution)/shard_map/ppermute | solution.py:211
  53.6 1.8 %collective-permute-start.16 = (bf16[3072,128]{1,0:T(8,128)(2,1)}, bf16[3072,128]{1,0:T(8,128)(2,1)}, u32[]{:S(2)}, u32[]{:S(2)}) collective-permute-start(bf16[3072,128]{1,0:T(8,128)(2,1)} %get-tuple-element.44), channel_id=1, source_target_pairs={{0,8},{4,12},{8,0},{12,4},{1,9},{5,13},{9,1},{13,5},{2,10},{6,14},... | collective-permute-start | bytes 2359304 | tf_op jit(solution)/shard_map/ppermute | solution.py:200
  55.8 6.5 %collective-permute-done.12.refs_5_ = bf16[3072,128]{1,0:T(8,128)(2,1)} collective-permute-done((bf16[3072,128]{1,0:T(8,128)(2,1)S(1)}, bf16[3072,128]{1,0:T(8,128)(2,1)}, u32[]{:S(2)}, u32[]{:S(2)}) %collective-permute-start.12) | collective-permute-done | bytes 786464 | tf_op jit(solution)/shard_map/ppermute | solution.py:196
  62.3 3.2 %collective-permute-start.15 = (bf16[3072,128]{1,0:T(8,128)(2,1)}, bf16[3072,128]{1,0:T(8,128)(2,1)S(1)}, u32[]{:S(2)}, u32[]{:S(2)}) collective-permute-start(bf16[3072,128]{1,0:T(8,128)(2,1)} %collective-permute-done.13.refs_6_), channel_id=1, source_target_pairs={{0,224},{16,240},{32,0},{48,16},{64,32},{80,48},{96,64},{112,80},{... | collective-permute-start | bytes 2359304 | tf_op jit(solution)/shard_map/ppermute | solution.py:196
  71.1 13.2 %products_0_7_1_6_2.1.refs_8_ = f32[8192,128]{1,0:T(8,128)S(1)} custom-call(s32[8]{0:T(128)S(1)} %stack.26.refs_0_, s32[64,128]{1,0:T(8,128)S(1)} %pad_add_fusion.refs_1_, bf16[3072,128]{1,0:T(8,128)(2,1)S(1)} %collective-permute-done.1.refs_2_, bf16[3072,128]{1,0:T(8,128)(2,1)S(1)} %collective-permute-done.10.refs_3_, ...), custom_call_target="tpu_custom_call" | custom-call | flops 200000000 | bytes 28000000 | tf_op jit(solution)/shard_map/products_0_7_1_6_2/pallas_call | solution.py:171
  84.5 3.2 %collective-permute-start.19 = (bf16[1536,128]{1,0:T(8,128)(2,1)S(1)}, bf16[1536,128]{1,0:T(8,128)(2,1)S(1)}, u32[]{:S(2)}, u32[]{:S(2)}) collective-permute-start(bf16[1536,128]{1,0:T(8,128)(2,1)S(1)} %slice.95), channel_id=1, source_target_pairs={{0,224},{16,240},{32,0},{48,16},{64,32},{80,48},{96,64},{112,80},{... | collective-permute-start | bytes 1179656 | tf_op jit(solution)/shard_map/ppermute | solution.py:270
  87.7 6.1 %products_5_3.1.refs_8_ = f32[8192,128]{1,0:T(8,128)S(1)} custom-call(s32[8]{0:T(128)S(1)} %stack.26.refs_0_, s32[64,128]{1,0:T(8,128)S(1)} %pad_add_fusion.refs_1_, bf16[3072,128]{1,0:T(8,128)(2,1)S(1)} %collective-permute-done.14.refs_2_, bf16[3072,128]{1,0:T(8,128)(2,1)S(1)} %collective-permute-done.15.refs_3_, ...), custom_call_target="tpu_custom_call" | custom-call | flops 80000000 | bytes 16000000 | tf_op jit(solution)/shard_map/products_5_3/pallas_call | solution.py:171
  93.9 4.8 %products_4.1 = (f32[4096,128]{1,0:T(8,128)S(1)}, f32[4096,128]{1,0:T(8,128)S(1)}) custom-call(s32[8]{0:T(128)S(1)} %stack.26.refs_0_, s32[64,128]{1,0:T(8,128)S(1)} %pad_add_fusion.refs_1_, bf16[1536,128]{1,0:T(8,128)(2,1)S(1)} %collective-permute-done.18.refs_2_, bf16[1536,128]{1,0:T(8,128)(2,1)S(1)} %collective-permute-done.19.refs_3_, ...), custom_call_target="tpu_custom_call" | custom-call | flops 40000000 | bytes 12000000 | tf_op jit(solution)/shard_map/products_4/pallas_call | solution.py:171
  98.7 4.1 %collective-permute-done.20 = f32[4096,128]{1,0:T(8,128)S(1)} collective-permute-done((f32[4096,128]{1,0:T(8,128)S(1)}, f32[4096,128]{1,0:T(8,128)S(1)}, u32[]{:S(2)}, u32[]{:S(2)}) %collective-permute-start.20) | collective-permute-done | bytes 2097184 | tf_op jit(solution)/shard_map/ppermute | solution.py:274
  103.7 3.3 %collective-permute-start.21 = (f32[512,128]{1,0:T(8,128)S(1)}, f32[512,128]{1,0:T(8,128)S(1)}, u32[]{:S(2)}, u32[]{:S(2)}) collective-permute-start(f32[512,128]{1,0:T(8,128)S(1)} %get-tuple-element.51), channel_id=1, source_target_pairs={{0,1},{1,2},{2,3},{3,0},{4,5},{5,6},{6,7},{7,4},{8,9},{9,10},{10,1... | collective-permute-start | bytes 786440 | tf_op jit(solution)/shard_map/ppermute | solution.py:282
  107.1 3.4 %collective-permute-start.26 = (f32[512,128]{1,0:T(8,128)S(1)}, f32[512,128]{1,0:T(8,128)S(1)}, u32[]{:S(2)}, u32[]{:S(2)}) collective-permute-start(f32[512,128]{1,0:T(8,128)S(1)} %get-tuple-element.57), channel_id=1, source_target_pairs={{0,9},{1,10},{2,11},{3,8},{4,25},{5,26},{6,27},{7,24},{8,1},{9,2},... | collective-permute-start | bytes 786440 | tf_op jit(solution)/shard_map/ppermute | solution.py:285
  110.4 2.5 %collective-permute-done.21 = f32[512,128]{1,0:T(8,128)S(1)} collective-permute-done((f32[512,128]{1,0:T(8,128)S(1)}, f32[512,128]{1,0:T(8,128)S(1)}, u32[]{:S(2)}, u32[]{:S(2)}) %collective-permute-start.21) | collective-permute-done | bytes 262176 | tf_op jit(solution)/shard_map/ppermute | solution.py:282
  112.9 5.6 %collective-permute-done.22 = f32[512,128]{1,0:T(8,128)S(1)} collective-permute-done((f32[512,128]{1,0:T(8,128)S(1)}, f32[512,128]{1,0:T(8,128)S(1)}, u32[]{:S(2)}, u32[]{:S(2)}) %collective-permute-start.22) | collective-permute-done | bytes 262176 | tf_op jit(solution)/shard_map/ppermute | solution.py:283
  118.6 3.9 %collective-permute-start.25 = (f32[512,128]{1,0:T(8,128)S(1)}, f32[512,128]{1,0:T(8,128)S(1)}, u32[]{:S(2)}, u32[]{:S(2)}) collective-permute-start(f32[512,128]{1,0:T(8,128)S(1)} %get-tuple-element.59), channel_id=1, source_target_pairs={{0,9},{1,10},{2,11},{3,8},{4,25},{5,26},{6,27},{7,24},{8,1},{9,2},... | collective-permute-start | bytes 786440 | tf_op jit(solution)/shard_map/ppermute | solution.py:288
  122.6 6.5 %collective-permute-done.25 = f32[512,128]{1,0:T(8,128)S(1)} collective-permute-done((f32[512,128]{1,0:T(8,128)S(1)}, f32[512,128]{1,0:T(8,128)S(1)}, u32[]{:S(2)}, u32[]{:S(2)}) %collective-permute-start.25) | collective-permute-done | bytes 262176 | tf_op jit(solution)/shard_map/ppermute | solution.py:288
  129.1 4.8 %collective-permute-done.27 = f32[512,128]{1,0:T(8,128)S(1)} collective-permute-done((f32[512,128]{1,0:T(8,128)S(1)}, f32[512,128]{1,0:T(8,128)S(1)}, u32[]{:S(2)}, u32[]{:S(2)}) %collective-permute-start.27) | collective-permute-done | bytes 262176 | tf_op jit(solution)/shard_map/ppermute | solution.py:289
  (79 shorter events, 11.2 us)
Async XLA Ops:
  0.0 4.4 %copy-start.4 = (s32[1,1,1,4,6]{4,3,2,1,0:T(4,128)S(1)}, s32[1,1,1,4,6]{4,3,2,1,0:T(4,128)}, u32[]{:S(2)}) copy-start(s32[1,1,1,4,6]{4,3,2,1,0:T(4,128)} %param.7) | copy-start | bytes 292
  0.0 4.6 %copy-start.7 = (s32[1,1,1,16]{3,2,1,0:T(1,128)S(1)}, s32[1,1,1,16]{3,2,1,0:T(1,128)}, u32[]{:S(2)}) copy-start(s32[1,1,1,16]{3,2,1,0:T(1,128)} %param.11) | copy-start | bytes 196
  0.0 4.6 %copy-start.5 = (s32[1,1,1,16,2]{3,4,2,1,0:T(2,128)S(1)}, s32[1,1,1,16,2]{3,4,2,1,0:T(2,128)}, u32[]{:S(2)}) copy-start(s32[1,1,1,16,2]{3,4,2,1,0:T(2,128)} %param.10) | copy-start | bytes 388
  0.0 21.9 %collective-permute-start.1 = (bf16[3072,128]{1,0:T(8,128)(2,1)}, bf16[3072,128]{1,0:T(8,128)(2,1)S(1)}, u32[]{:S(2)}, u32[]{:S(2)}) collective-permute-start(bf16[3072,128]{1,0:T(8,128)(2,1)} %bitcast.25), channel_id=1, source_target_pairs={{0,8},{4,24},{8,0},{12,16},{16,12},{20,28},{24,4},{28,20},{32,40},... | collective-permute-start | bytes 2359304 | tf_op jit(solution)/shard_map/ppermute | solution.py:221
  2.9 19.3 %collective-permute-start = (bf16[2048,128]{1,0:T(8,128)(2,1)S(1)}, bf16[2048,128]{1,0:T(8,128)(2,1)S(1)}, u32[]{:S(2)}, u32[]{:S(2)}) collective-permute-start(bf16[2048,128]{1,0:T(8,128)(2,1)S(1)} %bitcast.20), channel_id=1, source_target_pairs={{0,4},{4,0},{8,12},{12,8},{1,5},{5,1},{9,13},{13,9},{2,6},{6,2},{1... | collective-permute-start | bytes 1572872 | tf_op jit(solution)/shard_map/ppermute | solution.py:225
  4.9 3.6 %collective-permute-start.2 = (s32[1,128]{1,0:T(1,128)S(1)}, s32[1,128]{1,0:T(1,128)S(1)}, u32[]{:S(2)}, u32[]{:S(2)}) collective-permute-start(s32[1,128]{1,0:T(1,128)S(1)} %pad_add_fusion.8), channel_id=1, source_target_pairs={{0,32},{4,36},{8,40},{12,44},{16,48},{20,52},{24,56},{28,60},{32,0... | collective-permute-start | bytes 1544 | tf_op jit(solution)/shard_map/ppermute | solution.py:211
  8.5 4.8 %collective-permute-start.3 = (s32[2,128]{1,0:T(2,128)S(1)}, s32[2,128]{1,0:T(2,128)S(1)}, u32[]{:S(2)}, u32[]{:S(2)}) collective-permute-start(s32[2,128]{1,0:T(2,128)S(1)} %pad_add_fusion.7), channel_id=1, source_target_pairs={{0,64},{4,68},{8,72},{12,76},{16,80},{20,84},{24,88},{28,92},{32,9... | collective-permute-start | bytes 3080 | tf_op jit(solution)/shard_map/ppermute | solution.py:211
  13.5 8.4 %collective-permute-start.4 = (s32[4,128]{1,0:T(4,128)S(1)}, s32[4,128]{1,0:T(4,128)S(1)}, u32[]{:S(2)}, u32[]{:S(2)}) collective-permute-start(s32[4,128]{1,0:T(4,128)S(1)} %pad_add_fusion.4), channel_id=1, source_target_pairs={{0,128},{4,132},{8,136},{12,140},{16,144},{20,148},{24,152},{28,15... | collective-permute-start | bytes 6152 | tf_op jit(solution)/shard_map/ppermute | solution.py:211
  22.0 5.1 %collective-permute-start.5 = (s32[8,128]{1,0:T(8,128)S(1)}, s32[8,128]{1,0:T(8,128)S(1)}, u32[]{:S(2)}, u32[]{:S(2)}) collective-permute-start(s32[8,128]{1,0:T(8,128)S(1)} %pad_add_fusion.3), channel_id=1, source_target_pairs={{0,8},{4,12},{8,0},{12,4},{16,24},{20,28},{24,16},{28,20},{32,40},... | collective-permute-start | bytes 12296 | tf_op jit(solution)/shard_map/ppermute | solution.py:211
  22.3 18.3 %collective-permute-start.11 = (bf16[3072,128]{1,0:T(8,128)(2,1)S(1)}, bf16[3072,128]{1,0:T(8,128)(2,1)S(1)}, u32[]{:S(2)}, u32[]{:S(2)}) collective-permute-start(bf16[3072,128]{1,0:T(8,128)(2,1)S(1)} %collective-permute-done.1.refs_2_), channel_id=1, source_target_pairs={{0,224},{16,240},{32,0},{48,16},{64,32},{80,48},{96,64},{112,80},{... | collective-permute-start | bytes 2359304 | tf_op jit(solution)/shard_map/ppermute | solution.py:196
  27.1 17.7 %collective-permute-start.10 = (bf16[3072,128]{1,0:T(8,128)(2,1)S(1)}, bf16[3072,128]{1,0:T(8,128)(2,1)S(1)}, u32[]{:S(2)}, u32[]{:S(2)}) collective-permute-start(bf16[3072,128]{1,0:T(8,128)(2,1)S(1)} %collective-permute-done.1.refs_2_), channel_id=1, source_target_pairs={{0,32},{16,48},{32,64},{48,80},{64,96},{80,112},{96,128},{112,144}... | collective-permute-start | bytes 2359304 | tf_op jit(solution)/shard_map/ppermute | solution.py:196
  27.2 20.8 %collective-permute-start.7 = (bf16[3072,128]{1,0:T(8,128)(2,1)S(1)}, bf16[3072,128]{1,0:T(8,128)(2,1)S(1)}, u32[]{:S(2)}, u32[]{:S(2)}) collective-permute-start(bf16[3072,128]{1,0:T(8,128)(2,1)S(1)} %get-tuple-element.67), channel_id=1, source_target_pairs={{0,24},{4,28},{8,16},{12,20},{16,8},{20,12},{24,0},{28,4},{32,56},... | collective-permute-start | bytes 2359304 | tf_op jit(solution)/shard_map/ppermute | solution.py:204
  28.5 19.5 %collective-permute-start.6 = (bf16[3072,128]{1,0:T(8,128)(2,1)S(1)}, bf16[3072,128]{1,0:T(8,128)(2,1)S(1)}, u32[]{:S(2)}, u32[]{:S(2)}) collective-permute-start(bf16[3072,128]{1,0:T(8,128)(2,1)S(1)} %get-tuple-element.68), channel_id=1, source_target_pairs={{0,8},{4,12},{8,0},{12,4},{1,9},{5,13},{9,1},{13,5},{2,10},{6,14},... | collective-permute-start | bytes 2359304 | tf_op jit(solution)/shard_map/ppermute | solution.py:200
  29.2 1.2 collective-permute-start.8
  44.8 17.5 %collective-permute-start.12 = (bf16[3072,128]{1,0:T(8,128)(2,1)S(1)}, bf16[3072,128]{1,0:T(8,128)(2,1)}, u32[]{:S(2)}, u32[]{:S(2)}) collective-permute-start(bf16[3072,128]{1,0:T(8,128)(2,1)S(1)} %collective-permute-done.10.refs_3_), channel_id=1, source_target_pairs={{0,32},{16,48},{32,64},{48,80},{64,96},{80,112},{96,128},{112,144}... | collective-permute-start | bytes 2359304 | tf_op jit(solution)/shard_map/ppermute | solution.py:196
  44.8 17.5 %collective-permute-start.13 = (bf16[3072,128]{1,0:T(8,128)(2,1)S(1)}, bf16[3072,128]{1,0:T(8,128)(2,1)}, u32[]{:S(2)}, u32[]{:S(2)}) collective-permute-start(bf16[3072,128]{1,0:T(8,128)(2,1)S(1)} %collective-permute-done.11.refs_4_), channel_id=1, source_target_pairs={{0,224},{16,240},{32,0},{48,16},{64,32},{80,48},{96,64},{112,80},{... | collective-permute-start | bytes 2359304 | tf_op jit(solution)/shard_map/ppermute | solution.py:196
  48.0 5.6 %collective-permute-start.9 = (s32[32,128]{1,0:T(8,128)S(1)}, s32[32,128]{1,0:T(8,128)S(1)}, u32[]{:S(2)}, u32[]{:S(2)}) collective-permute-start(s32[32,128]{1,0:T(8,128)S(1)} %pad_add_fusion.1), channel_id=1, source_target_pairs={{0,16},{4,20},{8,24},{12,28},{16,0},{20,4},{24,8},{28,12},{32,48},... | collective-permute-start | bytes 49160 | tf_op jit(solution)/shard_map/ppermute | solution.py:211
  53.6 12.6 %collective-permute-start.16 = (bf16[3072,128]{1,0:T(8,128)(2,1)}, bf16[3072,128]{1,0:T(8,128)(2,1)}, u32[]{:S(2)}, u32[]{:S(2)}) collective-permute-start(bf16[3072,128]{1,0:T(8,128)(2,1)} %get-tuple-element.44), channel_id=1, source_target_pairs={{0,8},{4,12},{8,0},{12,4},{1,9},{5,13},{9,1},{13,5},{2,10},{6,14},... | collective-permute-start | bytes 2359304 | tf_op jit(solution)/shard_map/ppermute | solution.py:200
  55.4 13.5 %collective-permute-start.17 = (bf16[3072,128]{1,0:T(8,128)(2,1)}, bf16[3072,128]{1,0:T(8,128)(2,1)}, u32[]{:S(2)}, u32[]{:S(2)}) collective-permute-start(bf16[3072,128]{1,0:T(8,128)(2,1)} %get-tuple-element.45), channel_id=1, source_target_pairs={{0,24},{4,28},{8,16},{12,20},{16,8},{20,12},{24,0},{28,4},{32,56},... | collective-permute-start | bytes 2359304 | tf_op jit(solution)/shard_map/ppermute | solution.py:204
  55.8 12.5 %copy-start.3 = (bf16[3072,128]{1,0:T(8,128)(2,1)S(1)}, bf16[3072,128]{1,0:T(8,128)(2,1)}, u32[]{:S(2)}) copy-start(bf16[3072,128]{1,0:T(8,128)(2,1)} %copy-done.2) | copy-start | bytes 2359300
  62.3 22.1 %collective-permute-start.14 = (bf16[3072,128]{1,0:T(8,128)(2,1)}, bf16[3072,128]{1,0:T(8,128)(2,1)S(1)}, u32[]{:S(2)}, u32[]{:S(2)}) collective-permute-start(bf16[3072,128]{1,0:T(8,128)(2,1)} %collective-permute-done.12.refs_5_), channel_id=1, source_target_pairs={{0,32},{16,48},{32,64},{48,80},{64,96},{80,112},{96,128},{112,144}... | collective-permute-start | bytes 2359304 | tf_op jit(solution)/shard_map/ppermute | solution.py:196
  62.3 22.1 %collective-permute-start.15 = (bf16[3072,128]{1,0:T(8,128)(2,1)}, bf16[3072,128]{1,0:T(8,128)(2,1)S(1)}, u32[]{:S(2)}, u32[]{:S(2)}) collective-permute-start(bf16[3072,128]{1,0:T(8,128)(2,1)} %collective-permute-done.13.refs_6_), channel_id=1, source_target_pairs={{0,224},{16,240},{32,0},{48,16},{64,32},{80,48},{96,64},{112,80},{... | collective-permute-start | bytes 2359304 | tf_op jit(solution)/shard_map/ppermute | solution.py:196
  84.4 9.4 %collective-permute-start.18 = (bf16[1536,128]{1,0:T(8,128)(2,1)S(1)}, bf16[1536,128]{1,0:T(8,128)(2,1)S(1)}, u32[]{:S(2)}, u32[]{:S(2)}) collective-permute-start(bf16[1536,128]{1,0:T(8,128)(2,1)S(1)} %slice.94), channel_id=1, source_target_pairs={{0,32},{16,48},{32,64},{48,80},{64,96},{80,112},{96,128},{112,144}... | collective-permute-start | bytes 1179656 | tf_op jit(solution)/shard_map/ppermute | solution.py:270
  84.5 9.3 %collective-permute-start.19 = (bf16[1536,128]{1,0:T(8,128)(2,1)S(1)}, bf16[1536,128]{1,0:T(8,128)(2,1)S(1)}, u32[]{:S(2)}, u32[]{:S(2)}) collective-permute-start(bf16[1536,128]{1,0:T(8,128)(2,1)S(1)} %slice.95), channel_id=1, source_target_pairs={{0,224},{16,240},{32,0},{48,16},{64,32},{80,48},{96,64},{112,80},{... | collective-permute-start | bytes 1179656 | tf_op jit(solution)/shard_map/ppermute | solution.py:270
  98.6 4.2 %collective-permute-start.20 = (f32[4096,128]{1,0:T(8,128)S(1)}, f32[4096,128]{1,0:T(8,128)S(1)}, u32[]{:S(2)}, u32[]{:S(2)}) collective-permute-start(f32[4096,128]{1,0:T(8,128)S(1)} %get-tuple-element.50), channel_id=1, source_target_pairs={{0,4},{4,0},{8,12},{12,8},{1,5},{5,1},{9,13},{13,9},{2,6},{6,2},{1... | collective-permute-start | bytes 6291464 | tf_op jit(solution)/shard_map/ppermute | solution.py:274
  103.1 15.5 %collective-permute-start.23 = (f32[1024,128]{1,0:T(8,128)S(1)}, f32[1024,128]{1,0:T(8,128)S(1)}, u32[]{:S(2)}, u32[]{:S(2)}) collective-permute-start(f32[1024,128]{1,0:T(8,128)S(1)} %slice_add_fusion), channel_id=1, source_target_pairs={{0,8},{4,24},{8,0},{12,16},{16,12},{20,28},{24,4},{28,20},{32,40},... | collective-permute-start | bytes 1572872 | tf_op jit(solution)/shard_map/ppermute | solution.py:284
  103.7 9.2 %collective-permute-start.21 = (f32[512,128]{1,0:T(8,128)S(1)}, f32[512,128]{1,0:T(8,128)S(1)}, u32[]{:S(2)}, u32[]{:S(2)}) collective-permute-start(f32[512,128]{1,0:T(8,128)S(1)} %get-tuple-element.51), channel_id=1, source_target_pairs={{0,1},{1,2},{2,3},{3,0},{4,5},{5,6},{6,7},{7,4},{8,9},{9,10},{10,1... | collective-permute-start | bytes 786440 | tf_op jit(solution)/shard_map/ppermute | solution.py:282
  107.0 11.5 %collective-permute-start.22 = (f32[512,128]{1,0:T(8,128)S(1)}, f32[512,128]{1,0:T(8,128)S(1)}, u32[]{:S(2)}, u32[]{:S(2)}) collective-permute-start(f32[512,128]{1,0:T(8,128)S(1)} %get-tuple-element.52), channel_id=1, source_target_pairs={{0,3},{1,0},{2,1},{3,2},{4,7},{5,4},{6,5},{7,6},{8,11},{9,8},{10,9... | collective-permute-start | bytes 786440 | tf_op jit(solution)/shard_map/ppermute | solution.py:283
  107.1 15.5 %collective-permute-start.24 = (f32[512,128]{1,0:T(8,128)S(1)}, f32[512,128]{1,0:T(8,128)S(1)}, u32[]{:S(2)}, u32[]{:S(2)}) collective-permute-start(f32[512,128]{1,0:T(8,128)S(1)} %get-tuple-element.55), channel_id=1, source_target_pairs={{0,11},{1,8},{2,9},{3,10},{4,27},{5,24},{6,25},{7,26},{8,3},{9,0},... | collective-permute-start | bytes 786440 | tf_op jit(solution)/shard_map/ppermute | solution.py:286
  107.1 15.5 %collective-permute-start.26 = (f32[512,128]{1,0:T(8,128)S(1)}, f32[512,128]{1,0:T(8,128)S(1)}, u32[]{:S(2)}, u32[]{:S(2)}) collective-permute-start(f32[512,128]{1,0:T(8,128)S(1)} %get-tuple-element.57), channel_id=1, source_target_pairs={{0,9},{1,10},{2,11},{3,8},{4,25},{5,26},{6,27},{7,24},{8,1},{9,2},... | collective-permute-start | bytes 786440 | tf_op jit(solution)/shard_map/ppermute | solution.py:285
  118.6 10.5 %collective-permute-start.25 = (f32[512,128]{1,0:T(8,128)S(1)}, f32[512,128]{1,0:T(8,128)S(1)}, u32[]{:S(2)}, u32[]{:S(2)}) collective-permute-start(f32[512,128]{1,0:T(8,128)S(1)} %get-tuple-element.59), channel_id=1, source_target_pairs={{0,9},{1,10},{2,11},{3,8},{4,25},{5,26},{6,27},{7,24},{8,1},{9,2},... | collective-permute-start | bytes 786440 | tf_op jit(solution)/shard_map/ppermute | solution.py:288
  122.6 11.4 %collective-permute-start.27 = (f32[512,128]{1,0:T(8,128)S(1)}, f32[512,128]{1,0:T(8,128)S(1)}, u32[]{:S(2)}, u32[]{:S(2)}) collective-permute-start(f32[512,128]{1,0:T(8,128)S(1)} %get-tuple-element.60), channel_id=1, source_target_pairs={{0,11},{1,8},{2,9},{3,10},{4,27},{5,24},{6,25},{7,26},{8,3},{9,0},... | collective-permute-start | bytes 786440 | tf_op jit(solution)/shard_map/ppermute | solution.py:289
  (4 other events, 10.3 us)

commit v3 on v2

--- a/solution.py
+++ b/solution.py
@@ -51,7 +51,7 @@
     return [(gid(z, h, l, c), gid(z, 1 - h, 1 - l, c)) for z, h, l, c in group()]
 
 
-BITS = (3, 4, 5, 1, 0, 2)
+BITS = (3, 4, 1, 0, 2, 5)
 
 
 def slot(offset):
@@ -83,7 +83,7 @@
 
     ids, meta = take(2)
     lefts = take(n * nparts)
-    rights = take(4)
+    right, in1, in2, out1, out2 = take(5)
     c_in = None if first else take(1)[0]
     outs = take(len(outs_rows))
     abuf, bbuf, acc, work, in_sem = refs
@@ -96,13 +96,42 @@
         for p, (start, size) in enumerate(parts):
             pairs.append((lefts[s * nparts + p].at[pl.ds(start, size)], abuf.at[pl.ds(spot, size)]))
             spot += size
+    copies = copy_all(pairs, in_sem)
+
+    def fetch(src, start, s, k):
+        rows = pl.ds(pl.multiple_of(start, 256), 256)
+        at = n * nparts + s * 8 + k
+        return pltpu.make_async_copy(src.at[rows], bbuf.at[pl.ds((s * 8 + k) * 256, 256)], in_sem.at[at])
+
     for s, delta in enumerate(deltas):
         zs = (z + delta) & (NZ - 1)
-        for k in range(4):
-            for rel in range(2):
-                rows = pl.ds(pl.multiple_of(rel * RIGHT_ROWS + zs * 256, 256), 256)
-                pairs.append((rights[k].at[rows], bbuf.at[pl.ds((s * 8 + k * 2 + rel) * 256, 256)]))
-    copies = copy_all(pairs, in_sem)
+        at = zs * 256
+        low = zs < NZ // 2
+        whole = [
+            fetch(right, at, s, 0),
+            fetch(right, RIGHT_ROWS + at, s, 1),
+            fetch(in1, RIGHT_ROWS - QUARTER + at, s, 3),
+            fetch(out1, at, s, 4),
+            fetch(in2, QUARTER + at, s, 6),
+            fetch(out2, QUARTER + at, s, 7),
+        ]
+        near = (zs & 3) * 256
+        first_half = [fetch(in2, near, s, 2), fetch(out1, RIGHT_ROWS + near, s, 5)]
+        second_half = [fetch(in1, near, s, 2), fetch(out2, near, s, 5)]
+        for copy in whole:
+            copy.start()
+
+        @pl.when(low)
+        def _(chosen=first_half):
+            for copy in chosen:
+                copy.start()
+
+        @pl.when(jnp.logical_not(low))
+        def _(chosen=second_half):
+            for copy in chosen:
+                copy.start()
+
+        copies = copies + whole + first_half
 
     if first:
         acc[...] = jnp.zeros_like(acc)
@@ -171,7 +200,7 @@
     return pl.pallas_call(
         functools.partial(kernel, deltas, parts, tiles, first, outs_rows),
         out_shape=[jax.ShapeDtypeStruct((k * TILE, TILE), jnp.float32) for _, k in outs_rows],
-        in_specs=[SMEM, SMEM] + [HBM] * (len(lefts) + 4) + ([] if first else [VMEM]),
+        in_specs=[SMEM, SMEM] + [HBM] * (len(lefts) + 5) + ([] if first else [VMEM]),
         out_specs=[VMEM] * len(outs_rows),
         scratch_shapes=[
             pltpu.VMEM((n * tiles * TILE, TILE), jnp.bfloat16),
@@ -232,33 +261,29 @@
     meta = jnp.concatenate(
         [left_meta.reshape(1, 32), right_meta.reshape(1, 64), jnp.zeros((1, 32), jnp.int32)], axis=1
     )
-    for bit in BITS[:3]:
-        meta = spread(meta, bit)
+    around = [send(meta, BOTH, [(i, i ^ (k << 3)) for i in range(64)]) for k in (1, 2, 3)]
+    meta = jnp.concatenate([meta, *around], axis=0)
     own, meta = barrier((own, meta))
 
     f1, b1 = onward(own, own)
-    meta = spread(meta, BITS[3])
+    meta = spread(meta, BITS[2])
     right, meta = barrier((right, meta))
     in1, out1 = inner(right[QUARTER:]), outer(right[:REST])
-    meta = spread(meta, BITS[4])
+    meta = spread(meta, BITS[3])
     f1, b1 = barrier((f1, b1))
 
     f2, b2 = onward(f1, b1)
     in1, out1, meta = barrier((in1, out1, meta))
-    meta = spread(meta, BITS[5])
+    meta = spread(meta, BITS[4])
     in2 = jnp.concatenate([right[:QUARTER], out1[:RIGHT_ROWS]], axis=0)
     out2 = jnp.concatenate([right[REST:], in1[RIGHT_ROWS - QUARTER :]], axis=0)
     in2, out2, meta = barrier((in2, out2, meta))
     in2, out2 = inner(in2), outer(out2)
-    f2, b2 = barrier((f2, b2))
+    meta = spread(meta, BITS[5])
+    f2, b2, meta = barrier((f2, b2, meta))
 
     f3, b3 = onward(f2, b2)
-    rights = [
-        right,
-        jnp.concatenate([in2[:QUARTER], in1], axis=0),
-        jnp.concatenate([out1, out2[:QUARTER]], axis=0),
-        jnp.concatenate([in2[QUARTER:], out2[QUARTER:]], axis=0),
-    ]
+    rights = [right, in1, in2, out1, out2]
     near = LEFT_ROWS // 2
     one = ((0, LEFT_ROWS),)
     two = ((0, near), (0, LEFT_ROWS - near))
@@ -278,13 +303,13 @@
         rows = slice(k * half, (k + count) * half)
         return kept[rows] + other[rows]
 
-    units = barrier((unit(6), unit(7), unit(3), unit(4), unit(0, 2)))
+    units = barrier((unit(6), unit(7), unit(3), unit(4)))
     up2 = send(units[0], "depth", y_route(1))
     down2 = send(units[1], "depth", y_route(-1))
-    still = send(units[4], BOTH, swap_route())
     up1 = send(units[2], ALL, home_route(1))
     down1 = send(units[3], ALL, home_route(-1))
-    up2, down2, still = barrier((up2, down2, still))
+    still = send(unit(0, 2), BOTH, swap_route())
+    up2, down2 = barrier((up2, down2))
     up3 = send(unit(2) + up2, ALL, home_route(1))
     down3 = send(unit(5) + down2, ALL, home_route(-1))
     low = still[:half] + down1 + up3

time: 135 us -> 138 us (1.022)
  waiting for transfers between devices: 54.3 us -> 57.7 us
  Pallas kernels: 24 us -> 20.9 us
    ppermute x6 -> x4, starting transfers between devices: 14 us -> 4.23 us  [spread(): send(meta, BOTH, [(i, i ^ 1 << bit) for i in range(64)])]
    ppermute x1 -> x4, starting transfers between devices: 0.64 us -> 9.76 us  [the longest x3 5.31 us: shards(): send(meta, BOTH, [(i, i ^ k << 3) for i in range(64)])]
    ppermute x1, waiting for transfers between devices: 0.01 us -> 5.64 us  [shards(): up1 = send(units[2], ALL, home_route(1))]
    ppermute x1, waiting for transfers between devices: 5.62 us -> 0.47 us  [shards(): down2 = send(units[1], 'depth', y_route(-1))]
    ppermute x1, waiting for transfers between devices: 0.01 us -> 4.43 us  [shards(): down1 = send(units[3], ALL, home_route(-1))]
    slice x4 -> x0, local copies, waits for them, and re-layouts: 4.09 us -> none  [the longest x1 1.08 us: shards(): out2[QUARTER:]]
    ppermute x2, waiting for transfers between devices: 0.69 us -> 4.66 us  [inner(): return send(x, 'col', INNER_ROUTE)]
    ppermute x1 -> x4, waiting for transfers between devices: 0.01 us -> 3.78 us  [the longest x3 3.78 us: shards(): send(meta, BOTH, [(i, i ^ k << 3) for i in range(64)])]
  transfers between devices with their start and end apart: 28 -> 29, of which waited for: 15 -> 16; matrix products, arithmetic and copies ran while one was open for 6% -> 3% of each run, Pallas kernels for 14% -> 12%
where the time goes in v3:
time: 138 us; the launch traced here: 137 us
  waiting for transfers between devices  57.7 us (42%)
  starting transfers between devices  47.5 us (34%)
  Pallas kernels  20.9 us (15%)
  local copies, waits for them, and re-layouts  7.39 us (5%)
  other arithmetic  2.83 us (2%)
    pallas_call x3, Pallas kernels, multiply(): pl.pallas_call(functools.partial(kernel, deltas, parts, tiles, first, out...  20.9 us
    ppermute x6, waiting for transfers between devices, onward(): return (send(f, 'row', z_route(1)), send(b, 'row', z_route(-1)))  17.3 us
    ppermute x6, starting transfers between devices, onward(): return (send(f, 'row', z_route(1)), send(b, 'row', z_route(-1)))  11.8 us
    ppermute x4, waiting for transfers between devices, spread(): send(meta, BOTH, [(i, i ^ 1 << bit) for i in range(64)])  7.13 us
    ppermute x1, waiting for transfers between devices, shards(): up1 = send(units[2], ALL, home_route(1))  5.64 us
    ppermute x3, starting transfers between devices, shards(): send(meta, BOTH, [(i, i ^ k << 3) for i in range(64)])  5.31 us
    ppermute x2, waiting for transfers between devices, inner(): return send(x, 'col', INNER_ROUTE)  4.66 us
    ppermute x1, starting transfers between devices, shards(): still = send(unit(0, 2), BOTH, swap_route())  4.44 us
  transfers between devices with their start and end apart: 29, of which 16 were waited for; matrix products, arithmetic and copies ran while one was open for 3% of the time, Pallas kernels for 12%

profile of v3, /device:TPU:8, one launch (start us, length us, event | category | flops | bytes accessed | tf_op | source)
XLA Modules:
  0.0 136.6 jit_solution(9540272535273844705)
XLA Ops:
  0.0 1.6 %collective-permute-start = (bf16[3072,128]{1,0:T(8,128)(2,1)}, bf16[3072,128]{1,0:T(8,128)(2,1)S(1)}, u32[]{:S(2)}, u32[]{:S(2)}) collective-permute-start(bf16[3072,128]{1,0:T(8,128)(2,1)} %bitcast.25), channel_id=1, source_target_pairs={{0,8},{4,24},{8,0},{12,16},{16,12},{20,28},{24,4},{28,20},{32,40},... | collective-permute-start | bytes 2359304 | tf_op jit(solution)/shard_map/ppermute | solution.py:250
  2.9 1.5 %collective-permute-start.8 = (bf16[2048,128]{1,0:T(8,128)(2,1)S(1)}, bf16[2048,128]{1,0:T(8,128)(2,1)S(1)}, u32[]{:S(2)}, u32[]{:S(2)}) collective-permute-start(bf16[2048,128]{1,0:T(8,128)(2,1)S(1)} %bitcast.20), channel_id=1, source_target_pairs={{0,4},{4,0},{8,12},{12,8},{1,5},{5,1},{9,13},{13,9},{2,6},{6,2},{1... | collective-permute-start | bytes 1572872 | tf_op jit(solution)/shard_map/ppermute | solution.py:254
  4.9 4.7 %collective-permute-start.3 = (s32[1,128]{1,0:T(1,128)S(1)}, s32[1,128]{1,0:T(1,128)S(1)}, u32[]{:S(2)}, u32[]{:S(2)}) collective-permute-start(s32[1,128]{1,0:T(1,128)S(1)} %pad_add_fusion.7), channel_id=1, source_target_pairs={{0,96},{4,100},{8,104},{12,108},{16,112},{20,116},{24,120},{28,124... | collective-permute-start | bytes 1544 | tf_op jit(solution)/shard_map/ppermute | solution.py:264
  11.1 2.9 %collective-permute-done.2 = s32[1,128]{1,0:T(1,128)S(1)} collective-permute-done((s32[1,128]{1,0:T(1,128)S(1)}, s32[1,128]{1,0:T(1,128)S(1)}, u32[]{:S(2)}, u32[]{:S(2)}) %collective-permute-start.2) | collective-permute-done | bytes 544 | tf_op jit(solution)/shard_map/ppermute | solution.py:264
  14.4 5.4 %collective-permute-start.5 = (bf16[3072,128]{1,0:T(8,128)(2,1)S(1)}, bf16[3072,128]{1,0:T(8,128)(2,1)S(1)}, u32[]{:S(2)}, u32[]{:S(2)}) collective-permute-start(bf16[3072,128]{1,0:T(8,128)(2,1)S(1)} %collective-permute-done.refs_2_), channel_id=1, source_target_pairs={{0,224},{16,240},{32,0},{48,16},{64,32},{80,48},{96,64},{112,80},{... | collective-permute-start | bytes 2359304 | tf_op jit(solution)/shard_map/ppermute | solution.py:225
  19.9 2.0 %collective-permute-start.11 = (bf16[3072,128]{1,0:T(8,128)(2,1)S(1)}, bf16[3072,128]{1,0:T(8,128)(2,1)S(1)}, u32[]{:S(2)}, u32[]{:S(2)}) collective-permute-start(bf16[3072,128]{1,0:T(8,128)(2,1)S(1)} %get-tuple-element.65), channel_id=1, source_target_pairs={{0,24},{4,28},{8,16},{12,20},{16,8},{20,12},{24,0},{28,4},{32,56},... | collective-permute-start | bytes 2359304 | tf_op jit(solution)/shard_map/ppermute | solution.py:233
  21.9 1.4 %collective-permute-start.10 = (bf16[3072,128]{1,0:T(8,128)(2,1)S(1)}, bf16[3072,128]{1,0:T(8,128)(2,1)S(1)}, u32[]{:S(2)}, u32[]{:S(2)}) collective-permute-start(bf16[3072,128]{1,0:T(8,128)(2,1)S(1)} %get-tuple-element.66), channel_id=1, source_target_pairs={{0,8},{4,12},{8,0},{12,4},{1,9},{5,13},{9,1},{13,5},{2,10},{6,14},... | collective-permute-start | bytes 2359304 | tf_op jit(solution)/shard_map/ppermute | solution.py:229
  23.4 12.7 %collective-permute-done.5.refs_4_ = bf16[3072,128]{1,0:T(8,128)(2,1)S(1)} collective-permute-done((bf16[3072,128]{1,0:T(8,128)(2,1)S(1)}, bf16[3072,128]{1,0:T(8,128)(2,1)S(1)}, u32[]{:S(2)}, u32[]{:S(2)}) %collective-permute-start.5) | collective-permute-done | bytes 786464 | tf_op jit(solution)/shard_map/ppermute | solution.py:225
  36.1 3.4 %collective-permute-done.4.refs_3_ = bf16[3072,128]{1,0:T(8,128)(2,1)S(1)} collective-permute-done((bf16[3072,128]{1,0:T(8,128)(2,1)S(1)}, bf16[3072,128]{1,0:T(8,128)(2,1)S(1)}, u32[]{:S(2)}, u32[]{:S(2)}) %collective-permute-start.4) | collective-permute-done | bytes 786464 | tf_op jit(solution)/shard_map/ppermute | solution.py:225
  39.5 3.2 %collective-permute-start.7 = (bf16[3072,128]{1,0:T(8,128)(2,1)S(1)}, bf16[3072,128]{1,0:T(8,128)(2,1)}, u32[]{:S(2)}, u32[]{:S(2)}) collective-permute-start(bf16[3072,128]{1,0:T(8,128)(2,1)S(1)} %collective-permute-done.5.refs_4_), channel_id=1, source_target_pairs={{0,224},{16,240},{32,0},{48,16},{64,32},{80,48},{96,64},{112,80},{... | collective-permute-start | bytes 2359304 | tf_op jit(solution)/shard_map/ppermute | solution.py:225
  42.8 2.2 %collective-permute-start.13 = (s32[16,128]{1,0:T(8,128)S(1)}, s32[16,128]{1,0:T(8,128)S(1)}, u32[]{:S(2)}, u32[]{:S(2)}) collective-permute-start(s32[16,128]{1,0:T(8,128)S(1)} %pad_add_fusion.2), channel_id=1, source_target_pairs={{0,16},{4,20},{8,24},{12,28},{16,0},{20,4},{24,8},{28,12},{32,48},... | collective-permute-start | bytes 24584 | tf_op jit(solution)/shard_map/ppermute | solution.py:240
  46.4 1.7 %collective-permute-done.13 = s32[16,128]{1,0:T(8,128)S(1)} collective-permute-done((s32[16,128]{1,0:T(8,128)S(1)}, s32[16,128]{1,0:T(8,128)S(1)}, u32[]{:S(2)}, u32[]{:S(2)}) %collective-permute-start.13) | collective-permute-done | bytes 8224 | tf_op jit(solution)/shard_map/ppermute | solution.py:240
  48.1 1.7 %collective-permute-start.14 = (s32[32,128]{1,0:T(8,128)S(1)}, s32[32,128]{1,0:T(8,128)S(1)}, u32[]{:S(2)}, u32[]{:S(2)}) collective-permute-start(s32[32,128]{1,0:T(8,128)S(1)} %pad_add_fusion.1), channel_id=1, source_target_pairs={{0,128},{4,132},{8,136},{12,140},{16,144},{20,148},{24,152},{28,15... | collective-permute-start | bytes 49160 | tf_op jit(solution)/shard_map/ppermute | solution.py:240
  49.8 1.5 %collective-permute-start.17 = (bf16[3072,128]{1,0:T(8,128)(2,1)}, bf16[3072,128]{1,0:T(8,128)(2,1)S(1)}, u32[]{:S(2)}, u32[]{:S(2)}) collective-permute-start(bf16[3072,128]{1,0:T(8,128)(2,1)} %get-tuple-element.44), channel_id=1, source_target_pairs={{0,8},{4,12},{8,0},{12,4},{1,9},{5,13},{9,1},{13,5},{2,10},{6,14},... | collective-permute-start | bytes 2359304 | tf_op jit(solution)/shard_map/ppermute | solution.py:229
  52.5 5.5 %collective-permute-done.14 = s32[32,128]{1,0:T(8,128)S(1)} collective-permute-done((s32[32,128]{1,0:T(8,128)S(1)}, s32[32,128]{1,0:T(8,128)S(1)}, u32[]{:S(2)}, u32[]{:S(2)}) %collective-permute-start.14) | collective-permute-done | bytes 16416 | tf_op jit(solution)/shard_map/ppermute | solution.py:240
  59.7 2.6 %collective-permute-start.16 = (bf16[3072,128]{1,0:T(8,128)(2,1)}, bf16[3072,128]{1,0:T(8,128)(2,1)}, u32[]{:S(2)}, u32[]{:S(2)}) collective-permute-start(bf16[3072,128]{1,0:T(8,128)(2,1)} %collective-permute-done.7.refs_6_), channel_id=1, source_target_pairs={{0,224},{16,240},{32,0},{48,16},{64,32},{80,48},{96,64},{112,80},{... | collective-permute-start | bytes 2359304 | tf_op jit(solution)/shard_map/ppermute | solution.py:225
  62.4 4.7 %collective-permute-done.17.refs_9_.refs_6_ = bf16[3072,128]{1,0:T(8,128)(2,1)S(1)} collective-permute-done((bf16[3072,128]{1,0:T(8,128)(2,1)}, bf16[3072,128]{1,0:T(8,128)(2,1)S(1)}, u32[]{:S(2)}, u32[]{:S(2)}) %collective-permute-start.17) | collective-permute-done | bytes 786464 | tf_op jit(solution)/shard_map/ppermute | solution.py:229
  67.0 2.8 %collective-permute-done.18.refs_11_.refs_8_ = bf16[3072,128]{1,0:T(8,128)(2,1)} collective-permute-done((bf16[3072,128]{1,0:T(8,128)(2,1)}, bf16[3072,128]{1,0:T(8,128)(2,1)}, u32[]{:S(2)}, u32[]{:S(2)}) %collective-permute-start.18) | collective-permute-done | bytes 786464 | tf_op jit(solution)/shard_map/ppermute | solution.py:233
  73.2 11.5 %products_0_7_1_6_2.1.refs_9_ = f32[8192,128]{1,0:T(8,128)S(1)} custom-call(s32[8]{0:T(128)S(1)} %stack.26.refs_0_, s32[64,128]{1,0:T(8,128)S(1)} %pad_add_fusion.refs_1_, bf16[3072,128]{1,0:T(8,128)(2,1)S(1)} %copy-done.1, bf16[3072,128]{1,0:T(8,128)(2,1)S(1)} %copy-done.5, bf16[3072,128]{1,0:T(8,128)(2,1)S(1)} %copy-done.3, ...), custom_call_target="tpu_custom_call" | custom-call | flops 200000000 | bytes 28000000 | tf_op jit(solution)/shard_map/products_0_7_1_6_2/pallas_call | solution.py:200
  86.9 3.2 %collective-permute-start.20 = (bf16[1536,128]{1,0:T(8,128)(2,1)S(1)}, bf16[1536,128]{1,0:T(8,128)(2,1)S(1)}, u32[]{:S(2)}, u32[]{:S(2)}) collective-permute-start(bf16[1536,128]{1,0:T(8,128)(2,1)S(1)} %slice.79), channel_id=1, source_target_pairs={{0,224},{16,240},{32,0},{48,16},{64,32},{80,48},{96,64},{112,80},{... | collective-permute-start | bytes 1179656 | tf_op jit(solution)/shard_map/ppermute | solution.py:295
  90.1 5.6 %products_5_3.1.refs_9_ = f32[8192,128]{1,0:T(8,128)S(1)} custom-call(s32[8]{0:T(128)S(1)} %stack.26.refs_0_, s32[64,128]{1,0:T(8,128)S(1)} %pad_add_fusion.refs_1_, bf16[3072,128]{1,0:T(8,128)(2,1)} %collective-permute-done.15.refs_2_, bf16[3072,128]{1,0:T(8,128)(2,1)} %collective-permute-done.16.refs_3_, ...), custom_call_target="tpu_custom_call" | custom-call | flops 80000000 | bytes 16000000 | tf_op jit(solution)/shard_map/products_5_3/pallas_call | solution.py:200
  96.2 3.8 %products_4.1 = (f32[4096,128]{1,0:T(8,128)S(1)}, f32[4096,128]{1,0:T(8,128)S(1)}) custom-call(s32[8]{0:T(128)S(1)} %stack.26.refs_0_, s32[64,128]{1,0:T(8,128)S(1)} %pad_add_fusion.refs_1_, bf16[1536,128]{1,0:T(8,128)(2,1)S(1)} %collective-permute-done.19.refs_2_, bf16[1536,128]{1,0:T(8,128)(2,1)S(1)} %collective-permute-done.20.refs_3_, ...), custom_call_target="tpu_custom_call" | custom-call | flops 40000000 | bytes 12000000 | tf_op jit(solution)/shard_map/products_4/pallas_call | solution.py:200
  100.1 4.1 %collective-permute-done.21 = f32[4096,128]{1,0:T(8,128)S(1)} collective-permute-done((f32[4096,128]{1,0:T(8,128)S(1)}, f32[4096,128]{1,0:T(8,128)S(1)}, u32[]{:S(2)}, u32[]{:S(2)}) %collective-permute-start.21) | collective-permute-done | bytes 2097184 | tf_op jit(solution)/shard_map/ppermute | solution.py:299
  104.4 1.9 %collective-permute-start.24 = (f32[512,128]{1,0:T(8,128)S(1)}, f32[512,128]{1,0:T(8,128)S(1)}, u32[]{:S(2)}, u32[]{:S(2)}) collective-permute-start(f32[512,128]{1,0:T(8,128)S(1)} %get-tuple-element.52), channel_id=1, source_target_pairs={{0,1},{1,2},{2,3},{3,0},{4,5},{5,6},{6,7},{7,4},{8,9},{9,10},{10,1... | collective-permute-start | bytes 786440 | tf_op jit(solution)/shard_map/ppermute | solution.py:307
  106.6 4.4 %collective-permute-start.22 = (f32[1024,128]{1,0:T(8,128)S(1)}, f32[1024,128]{1,0:T(8,128)S(1)}, u32[]{:S(2)}, u32[]{:S(2)}) collective-permute-start(f32[1024,128]{1,0:T(8,128)S(1)} %slice_add_fusion), channel_id=1, source_target_pairs={{0,8},{4,24},{8,0},{12,16},{16,12},{20,28},{24,4},{28,20},{32,40},... | collective-permute-start | bytes 1572872 | tf_op jit(solution)/shard_map/ppermute | solution.py:311
  111.0 2.9 %collective-permute-start.27 = (f32[512,128]{1,0:T(8,128)S(1)}, f32[512,128]{1,0:T(8,128)S(1)}, u32[]{:S(2)}, u32[]{:S(2)}) collective-permute-start(f32[512,128]{1,0:T(8,128)S(1)} %get-tuple-element.55), channel_id=1, source_target_pairs={{0,9},{1,10},{2,11},{3,8},{4,25},{5,26},{6,27},{7,24},{8,1},{9,2},... | collective-permute-start | bytes 786440 | tf_op jit(solution)/shard_map/ppermute | solution.py:309
  114.5 2.6 %collective-permute-start.26 = (f32[512,128]{1,0:T(8,128)S(1)}, f32[512,128]{1,0:T(8,128)S(1)}, u32[]{:S(2)}, u32[]{:S(2)}) collective-permute-start(f32[512,128]{1,0:T(8,128)S(1)} %get-tuple-element.57), channel_id=1, source_target_pairs={{0,9},{1,10},{2,11},{3,8},{4,25},{5,26},{6,27},{7,24},{8,1},{9,2},... | collective-permute-start | bytes 786440 | tf_op jit(solution)/shard_map/ppermute | solution.py:313
  117.1 1.5 %collective-permute-start.28 = (f32[512,128]{1,0:T(8,128)S(1)}, f32[512,128]{1,0:T(8,128)S(1)}, u32[]{:S(2)}, u32[]{:S(2)}) collective-permute-start(f32[512,128]{1,0:T(8,128)S(1)} %get-tuple-element.58), channel_id=1, source_target_pairs={{0,11},{1,8},{2,9},{3,10},{4,27},{5,24},{6,25},{7,26},{8,3},{9,0},... | collective-permute-start | bytes 786440 | tf_op jit(solution)/shard_map/ppermute | solution.py:314
  118.7 4.4 %collective-permute-done.23 = f32[512,128]{1,0:T(8,128)S(1)} collective-permute-done((f32[512,128]{1,0:T(8,128)S(1)}, f32[512,128]{1,0:T(8,128)S(1)}, u32[]{:S(2)}, u32[]{:S(2)}) %collective-permute-start.23) | collective-permute-done | bytes 262176 | tf_op jit(solution)/shard_map/ppermute | solution.py:310
  123.1 5.6 %collective-permute-done.27 = f32[512,128]{1,0:T(8,128)S(1)} collective-permute-done((f32[512,128]{1,0:T(8,128)S(1)}, f32[512,128]{1,0:T(8,128)S(1)}, u32[]{:S(2)}, u32[]{:S(2)}) %collective-permute-start.27) | collective-permute-done | bytes 262176 | tf_op jit(solution)/shard_map/ppermute | solution.py:309
  128.7 4.0 %collective-permute-done.26 = f32[512,128]{1,0:T(8,128)S(1)} collective-permute-done((f32[512,128]{1,0:T(8,128)S(1)}, f32[512,128]{1,0:T(8,128)S(1)}, u32[]{:S(2)}, u32[]{:S(2)}) %collective-permute-start.26) | collective-permute-done | bytes 262176 | tf_op jit(solution)/shard_map/ppermute | solution.py:313
  132.8 2.9 %collective-permute-done.28 = f32[512,128]{1,0:T(8,128)S(1)} collective-permute-done((f32[512,128]{1,0:T(8,128)S(1)}, f32[512,128]{1,0:T(8,128)S(1)}, u32[]{:S(2)}, u32[]{:S(2)}) %collective-permute-start.28) | collective-permute-done | bytes 262176 | tf_op jit(solution)/shard_map/ppermute | solution.py:314
  (77 shorter events, 16.3 us)
Async XLA Ops:
  0.0 14.0 %collective-permute-start = (bf16[3072,128]{1,0:T(8,128)(2,1)}, bf16[3072,128]{1,0:T(8,128)(2,1)S(1)}, u32[]{:S(2)}, u32[]{:S(2)}) collective-permute-start(bf16[3072,128]{1,0:T(8,128)(2,1)} %bitcast.25), channel_id=1, source_target_pairs={{0,8},{4,24},{8,0},{12,16},{16,12},{20,28},{24,4},{28,20},{32,40},... | collective-permute-start | bytes 2359304 | tf_op jit(solution)/shard_map/ppermute | solution.py:250
  2.9 11.5 %collective-permute-start.8 = (bf16[2048,128]{1,0:T(8,128)(2,1)S(1)}, bf16[2048,128]{1,0:T(8,128)(2,1)S(1)}, u32[]{:S(2)}, u32[]{:S(2)}) collective-permute-start(bf16[2048,128]{1,0:T(8,128)(2,1)S(1)} %bitcast.20), channel_id=1, source_target_pairs={{0,4},{4,0},{8,12},{12,8},{1,5},{5,1},{9,13},{13,9},{2,6},{6,2},{1... | collective-permute-start | bytes 1572872 | tf_op jit(solution)/shard_map/ppermute | solution.py:254
  4.9 6.2 %collective-permute-start.3 = (s32[1,128]{1,0:T(1,128)S(1)}, s32[1,128]{1,0:T(1,128)S(1)}, u32[]{:S(2)}, u32[]{:S(2)}) collective-permute-start(s32[1,128]{1,0:T(1,128)S(1)} %pad_add_fusion.7), channel_id=1, source_target_pairs={{0,96},{4,100},{8,104},{12,108},{16,112},{20,116},{24,120},{28,124... | collective-permute-start | bytes 1544 | tf_op jit(solution)/shard_map/ppermute | solution.py:264
  9.5 4.4 %collective-permute-start.2 = (s32[1,128]{1,0:T(1,128)S(1)}, s32[1,128]{1,0:T(1,128)S(1)}, u32[]{:S(2)}, u32[]{:S(2)}) collective-permute-start(s32[1,128]{1,0:T(1,128)S(1)} %pad_add_fusion.7), channel_id=1, source_target_pairs={{0,64},{4,68},{8,72},{12,76},{16,80},{20,84},{24,88},{28,92},{32,9... | collective-permute-start | bytes 1544 | tf_op jit(solution)/shard_map/ppermute | solution.py:264
  9.5 4.4 %collective-permute-start.1 = (s32[1,128]{1,0:T(1,128)S(1)}, s32[1,128]{1,0:T(1,128)S(1)}, u32[]{:S(2)}, u32[]{:S(2)}) collective-permute-start(s32[1,128]{1,0:T(1,128)S(1)} %pad_add_fusion.7), channel_id=1, source_target_pairs={{0,32},{4,36},{8,40},{12,44},{16,48},{20,52},{24,56},{28,60},{32,0... | collective-permute-start | bytes 1544 | tf_op jit(solution)/shard_map/ppermute | solution.py:264
  14.1 5.9 %copy-start = (bf16[3072,128]{1,0:T(8,128)(2,1)}, bf16[3072,128]{1,0:T(8,128)(2,1)S(1)}, u32[]{:S(2)}) copy-start(bf16[3072,128]{1,0:T(8,128)(2,1)S(1)} %collective-permute-done.refs_2_) | copy-start | bytes 2359300
  14.1 5.8 %collective-permute-start.9 = (s32[4,128]{1,0:T(4,128)S(1)}, s32[4,128]{1,0:T(4,128)S(1)}, u32[]{:S(2)}, u32[]{:S(2)}) collective-permute-start(s32[4,128]{1,0:T(4,128)S(1)} %pad_add_fusion.4), channel_id=1, source_target_pairs={{0,8},{4,12},{8,0},{12,4},{16,24},{20,28},{24,16},{28,20},{32,40},... | collective-permute-start | bytes 6152 | tf_op jit(solution)/shard_map/ppermute | solution.py:240
  14.4 21.6 %collective-permute-start.5 = (bf16[3072,128]{1,0:T(8,128)(2,1)S(1)}, bf16[3072,128]{1,0:T(8,128)(2,1)S(1)}, u32[]{:S(2)}, u32[]{:S(2)}) collective-permute-start(bf16[3072,128]{1,0:T(8,128)(2,1)S(1)} %collective-permute-done.refs_2_), channel_id=1, source_target_pairs={{0,224},{16,240},{32,0},{48,16},{64,32},{80,48},{96,64},{112,80},{... | collective-permute-start | bytes 2359304 | tf_op jit(solution)/shard_map/ppermute | solution.py:225
  19.8 19.7 %collective-permute-start.4 = (bf16[3072,128]{1,0:T(8,128)(2,1)S(1)}, bf16[3072,128]{1,0:T(8,128)(2,1)S(1)}, u32[]{:S(2)}, u32[]{:S(2)}) collective-permute-start(bf16[3072,128]{1,0:T(8,128)(2,1)S(1)} %collective-permute-done.refs_2_), channel_id=1, source_target_pairs={{0,32},{16,48},{32,64},{48,80},{64,96},{80,112},{96,128},{112,144}... | collective-permute-start | bytes 2359304 | tf_op jit(solution)/shard_map/ppermute | solution.py:225
  19.9 22.8 %collective-permute-start.11 = (bf16[3072,128]{1,0:T(8,128)(2,1)S(1)}, bf16[3072,128]{1,0:T(8,128)(2,1)S(1)}, u32[]{:S(2)}, u32[]{:S(2)}) collective-permute-start(bf16[3072,128]{1,0:T(8,128)(2,1)S(1)} %get-tuple-element.65), channel_id=1, source_target_pairs={{0,24},{4,28},{8,16},{12,20},{16,8},{20,12},{24,0},{28,4},{32,56},... | collective-permute-start | bytes 2359304 | tf_op jit(solution)/shard_map/ppermute | solution.py:233
  21.9 20.9 %collective-permute-start.10 = (bf16[3072,128]{1,0:T(8,128)(2,1)S(1)}, bf16[3072,128]{1,0:T(8,128)(2,1)S(1)}, u32[]{:S(2)}, u32[]{:S(2)}) collective-permute-start(bf16[3072,128]{1,0:T(8,128)(2,1)S(1)} %get-tuple-element.66), channel_id=1, source_target_pairs={{0,8},{4,12},{8,0},{12,4},{1,9},{5,13},{9,1},{13,5},{2,10},{6,14},... | collective-permute-start | bytes 2359304 | tf_op jit(solution)/shard_map/ppermute | solution.py:229
  23.4 19.4 %collective-permute-start.12 = (s32[8,128]{1,0:T(8,128)S(1)}, s32[8,128]{1,0:T(8,128)S(1)}, u32[]{:S(2)}, u32[]{:S(2)}) collective-permute-start(s32[8,128]{1,0:T(8,128)S(1)} %pad_add_fusion.3), channel_id=1, source_target_pairs={{0,4},{4,0},{8,12},{12,8},{16,20},{20,16},{24,28},{28,24},{32,36},... | collective-permute-start | bytes 12296 | tf_op jit(solution)/shard_map/ppermute | solution.py:240
  36.1 10.3 %copy-start.2 = (bf16[3072,128]{1,0:T(8,128)(2,1)}, bf16[3072,128]{1,0:T(8,128)(2,1)S(1)}, u32[]{:S(2)}) copy-start(bf16[3072,128]{1,0:T(8,128)(2,1)S(1)} %collective-permute-done.5.refs_4_) | copy-start | bytes 2359300
  39.5 6.9 %copy-start.4 = (bf16[3072,128]{1,0:T(8,128)(2,1)}, bf16[3072,128]{1,0:T(8,128)(2,1)S(1)}, u32[]{:S(2)}) copy-start(bf16[3072,128]{1,0:T(8,128)(2,1)S(1)} %collective-permute-done.4.refs_3_) | copy-start | bytes 2359300
  39.5 19.6 %collective-permute-start.6 = (bf16[3072,128]{1,0:T(8,128)(2,1)S(1)}, bf16[3072,128]{1,0:T(8,128)(2,1)}, u32[]{:S(2)}, u32[]{:S(2)}) collective-permute-start(bf16[3072,128]{1,0:T(8,128)(2,1)S(1)} %collective-permute-done.4.refs_3_), channel_id=1, source_target_pairs={{0,32},{16,48},{32,64},{48,80},{64,96},{80,112},{96,128},{112,144}... | collective-permute-start | bytes 2359304 | tf_op jit(solution)/shard_map/ppermute | solution.py:225
  39.5 19.6 %collective-permute-start.7 = (bf16[3072,128]{1,0:T(8,128)(2,1)S(1)}, bf16[3072,128]{1,0:T(8,128)(2,1)}, u32[]{:S(2)}, u32[]{:S(2)}) collective-permute-start(bf16[3072,128]{1,0:T(8,128)(2,1)S(1)} %collective-permute-done.5.refs_4_), channel_id=1, source_target_pairs={{0,224},{16,240},{32,0},{48,16},{64,32},{80,48},{96,64},{112,80},{... | collective-permute-start | bytes 2359304 | tf_op jit(solution)/shard_map/ppermute | solution.py:225
  42.8 5.2 %collective-permute-start.13 = (s32[16,128]{1,0:T(8,128)S(1)}, s32[16,128]{1,0:T(8,128)S(1)}, u32[]{:S(2)}, u32[]{:S(2)}) collective-permute-start(s32[16,128]{1,0:T(8,128)S(1)} %pad_add_fusion.2), channel_id=1, source_target_pairs={{0,16},{4,20},{8,24},{12,28},{16,0},{20,4},{24,8},{28,12},{32,48},... | collective-permute-start | bytes 24584 | tf_op jit(solution)/shard_map/ppermute | solution.py:240
  48.1 9.9 %collective-permute-start.14 = (s32[32,128]{1,0:T(8,128)S(1)}, s32[32,128]{1,0:T(8,128)S(1)}, u32[]{:S(2)}, u32[]{:S(2)}) collective-permute-start(s32[32,128]{1,0:T(8,128)S(1)} %pad_add_fusion.1), channel_id=1, source_target_pairs={{0,128},{4,132},{8,136},{12,140},{16,144},{20,148},{24,152},{28,15... | collective-permute-start | bytes 49160 | tf_op jit(solution)/shard_map/ppermute | solution.py:240
  49.8 17.3 %collective-permute-start.17 = (bf16[3072,128]{1,0:T(8,128)(2,1)}, bf16[3072,128]{1,0:T(8,128)(2,1)S(1)}, u32[]{:S(2)}, u32[]{:S(2)}) collective-permute-start(bf16[3072,128]{1,0:T(8,128)(2,1)} %get-tuple-element.44), channel_id=1, source_target_pairs={{0,8},{4,12},{8,0},{12,4},{1,9},{5,13},{9,1},{13,5},{2,10},{6,14},... | collective-permute-start | bytes 2359304 | tf_op jit(solution)/shard_map/ppermute | solution.py:229
  51.3 18.6 %collective-permute-start.18 = (bf16[3072,128]{1,0:T(8,128)(2,1)}, bf16[3072,128]{1,0:T(8,128)(2,1)}, u32[]{:S(2)}, u32[]{:S(2)}) collective-permute-start(bf16[3072,128]{1,0:T(8,128)(2,1)} %get-tuple-element.45), channel_id=1, source_target_pairs={{0,24},{4,28},{8,16},{12,20},{16,8},{20,12},{24,0},{28,4},{32,56},... | collective-permute-start | bytes 2359304 | tf_op jit(solution)/shard_map/ppermute | solution.py:233
  59.1 25.7 %collective-permute-start.15 = (bf16[3072,128]{1,0:T(8,128)(2,1)}, bf16[3072,128]{1,0:T(8,128)(2,1)}, u32[]{:S(2)}, u32[]{:S(2)}) collective-permute-start(bf16[3072,128]{1,0:T(8,128)(2,1)} %collective-permute-done.6.refs_5_), channel_id=1, source_target_pairs={{0,32},{16,48},{32,64},{48,80},{64,96},{80,112},{96,128},{112,144}... | collective-permute-start | bytes 2359304 | tf_op jit(solution)/shard_map/ppermute | solution.py:225
  59.7 25.0 %collective-permute-start.16 = (bf16[3072,128]{1,0:T(8,128)(2,1)}, bf16[3072,128]{1,0:T(8,128)(2,1)}, u32[]{:S(2)}, u32[]{:S(2)}) collective-permute-start(bf16[3072,128]{1,0:T(8,128)(2,1)} %collective-permute-done.7.refs_6_), channel_id=1, source_target_pairs={{0,224},{16,240},{32,0},{48,16},{64,32},{80,48},{96,64},{112,80},{... | collective-permute-start | bytes 2359304 | tf_op jit(solution)/shard_map/ppermute | solution.py:225
  86.8 9.3 %collective-permute-start.19 = (bf16[1536,128]{1,0:T(8,128)(2,1)S(1)}, bf16[1536,128]{1,0:T(8,128)(2,1)S(1)}, u32[]{:S(2)}, u32[]{:S(2)}) collective-permute-start(bf16[1536,128]{1,0:T(8,128)(2,1)S(1)} %slice.78), channel_id=1, source_target_pairs={{0,32},{16,48},{32,64},{48,80},{64,96},{80,112},{96,128},{112,144}... | collective-permute-start | bytes 1179656 | tf_op jit(solution)/shard_map/ppermute | solution.py:295
  86.9 9.3 %collective-permute-start.20 = (bf16[1536,128]{1,0:T(8,128)(2,1)S(1)}, bf16[1536,128]{1,0:T(8,128)(2,1)S(1)}, u32[]{:S(2)}, u32[]{:S(2)}) collective-permute-start(bf16[1536,128]{1,0:T(8,128)(2,1)S(1)} %slice.79), channel_id=1, source_target_pairs={{0,224},{16,240},{32,0},{48,16},{64,32},{80,48},{96,64},{112,80},{... | collective-permute-start | bytes 1179656 | tf_op jit(solution)/shard_map/ppermute | solution.py:295
  100.0 4.2 %collective-permute-start.21 = (f32[4096,128]{1,0:T(8,128)S(1)}, f32[4096,128]{1,0:T(8,128)S(1)}, u32[]{:S(2)}, u32[]{:S(2)}) collective-permute-start(f32[4096,128]{1,0:T(8,128)S(1)} %get-tuple-element.50), channel_id=1, source_target_pairs={{0,4},{4,0},{8,12},{12,8},{1,5},{5,1},{9,13},{13,9},{2,6},{6,2},{1... | collective-permute-start | bytes 6291464 | tf_op jit(solution)/shard_map/ppermute | solution.py:299
  104.4 9.5 %collective-permute-start.24 = (f32[512,128]{1,0:T(8,128)S(1)}, f32[512,128]{1,0:T(8,128)S(1)}, u32[]{:S(2)}, u32[]{:S(2)}) collective-permute-start(f32[512,128]{1,0:T(8,128)S(1)} %get-tuple-element.52), channel_id=1, source_target_pairs={{0,1},{1,2},{2,3},{3,0},{4,5},{5,6},{6,7},{7,4},{8,9},{9,10},{10,1... | collective-permute-start | bytes 786440 | tf_op jit(solution)/shard_map/ppermute | solution.py:307
  106.4 8.1 %collective-permute-start.25 = (f32[512,128]{1,0:T(8,128)S(1)}, f32[512,128]{1,0:T(8,128)S(1)}, u32[]{:S(2)}, u32[]{:S(2)}) collective-permute-start(f32[512,128]{1,0:T(8,128)S(1)} %get-tuple-element.53), channel_id=1, source_target_pairs={{0,3},{1,0},{2,1},{3,2},{4,7},{5,4},{6,5},{7,6},{8,11},{9,8},{10,9... | collective-permute-start | bytes 786440 | tf_op jit(solution)/shard_map/ppermute | solution.py:308
  106.6 22.1 %collective-permute-start.22 = (f32[1024,128]{1,0:T(8,128)S(1)}, f32[1024,128]{1,0:T(8,128)S(1)}, u32[]{:S(2)}, u32[]{:S(2)}) collective-permute-start(f32[1024,128]{1,0:T(8,128)S(1)} %slice_add_fusion), channel_id=1, source_target_pairs={{0,8},{4,24},{8,0},{12,16},{16,12},{20,28},{24,4},{28,20},{32,40},... | collective-permute-start | bytes 1572872 | tf_op jit(solution)/shard_map/ppermute | solution.py:311
  111.0 12.1 %collective-permute-start.23 = (f32[512,128]{1,0:T(8,128)S(1)}, f32[512,128]{1,0:T(8,128)S(1)}, u32[]{:S(2)}, u32[]{:S(2)}) collective-permute-start(f32[512,128]{1,0:T(8,128)S(1)} %get-tuple-element.51), channel_id=1, source_target_pairs={{0,11},{1,8},{2,9},{3,10},{4,27},{5,24},{6,25},{7,26},{8,3},{9,0},... | collective-permute-start | bytes 786440 | tf_op jit(solution)/shard_map/ppermute | solution.py:310
  111.0 17.7 %collective-permute-start.27 = (f32[512,128]{1,0:T(8,128)S(1)}, f32[512,128]{1,0:T(8,128)S(1)}, u32[]{:S(2)}, u32[]{:S(2)}) collective-permute-start(f32[512,128]{1,0:T(8,128)S(1)} %get-tuple-element.55), channel_id=1, source_target_pairs={{0,9},{1,10},{2,11},{3,8},{4,25},{5,26},{6,27},{7,24},{8,1},{9,2},... | collective-permute-start | bytes 786440 | tf_op jit(solution)/shard_map/ppermute | solution.py:309
  114.5 18.2 %collective-permute-start.26 = (f32[512,128]{1,0:T(8,128)S(1)}, f32[512,128]{1,0:T(8,128)S(1)}, u32[]{:S(2)}, u32[]{:S(2)}) collective-permute-start(f32[512,128]{1,0:T(8,128)S(1)} %get-tuple-element.57), channel_id=1, source_target_pairs={{0,9},{1,10},{2,11},{3,8},{4,25},{5,26},{6,27},{7,24},{8,1},{9,2},... | collective-permute-start | bytes 786440 | tf_op jit(solution)/shard_map/ppermute | solution.py:313
  117.1 18.5 %collective-permute-start.28 = (f32[512,128]{1,0:T(8,128)S(1)}, f32[512,128]{1,0:T(8,128)S(1)}, u32[]{:S(2)}, u32[]{:S(2)}) collective-permute-start(f32[512,128]{1,0:T(8,128)S(1)} %get-tuple-element.58), channel_id=1, source_target_pairs={{0,11},{1,8},{2,9},{3,10},{4,27},{5,24},{6,25},{7,26},{8,3},{9,0},... | collective-permute-start | bytes 786440 | tf_op jit(solution)/shard_map/ppermute | solution.py:314
  (7 other events, 21.4 us)

commit v4 on v3

--- a/solution.py
+++ b/solution.py
@@ -51,7 +51,7 @@
     return [(gid(z, h, l, c), gid(z, 1 - h, 1 - l, c)) for z, h, l, c in group()]
 
 
-BITS = (3, 4, 1, 0, 2, 5)
+BITS = (3, 4, 1, 2, 0, 5)
 
 
 def slot(offset):
@@ -236,6 +236,11 @@
 REST = 2 * RIGHT_ROWS - QUARTER
 
 
+def spread_two(meta, low):
+    around = [send(meta, BOTH, [(i, i ^ (k << low)) for i in range(64)]) for k in (1, 2, 3)]
+    return jnp.concatenate([meta, *around], axis=0)
+
+
 def spread(meta, bit):
     return jnp.concatenate([meta, send(meta, BOTH, [(i, i ^ (1 << bit)) for i in range(64)])], axis=0)
 
@@ -261,26 +266,21 @@
     meta = jnp.concatenate(
         [left_meta.reshape(1, 32), right_meta.reshape(1, 64), jnp.zeros((1, 32), jnp.int32)], axis=1
     )
-    around = [send(meta, BOTH, [(i, i ^ (k << 3)) for i in range(64)]) for k in (1, 2, 3)]
-    meta = jnp.concatenate([meta, *around], axis=0)
+    meta = spread_two(meta, 3)
     own, meta = barrier((own, meta))
 
     f1, b1 = onward(own, own)
-    meta = spread(meta, BITS[2])
+    meta = spread_two(meta, 1)
     right, meta = barrier((right, meta))
     in1, out1 = inner(right[QUARTER:]), outer(right[:REST])
-    meta = spread(meta, BITS[3])
-    f1, b1 = barrier((f1, b1))
+    meta = spread(spread(meta, BITS[4]), BITS[5])
+    f1, b1, meta = barrier((f1, b1, meta))
 
     f2, b2 = onward(f1, b1)
-    in1, out1, meta = barrier((in1, out1, meta))
-    meta = spread(meta, BITS[4])
     in2 = jnp.concatenate([right[:QUARTER], out1[:RIGHT_ROWS]], axis=0)
     out2 = jnp.concatenate([right[REST:], in1[RIGHT_ROWS - QUARTER :]], axis=0)
-    in2, out2, meta = barrier((in2, out2, meta))
     in2, out2 = inner(in2), outer(out2)
-    meta = spread(meta, BITS[5])
-    f2, b2, meta = barrier((f2, b2, meta))
+    f2, b2 = barrier((f2, b2))
 
     f3, b3 = onward(f2, b2)
     rights = [right, in1, in2, out1, out2]
@@ -288,12 +288,10 @@
     one = ((0, LEFT_ROWS),)
     two = ((0, near), (0, LEFT_ROWS - near))
     whole = ((0, 64),)
-    (total,) = multiply(
-        (0, -1, 1, -2, 2), one, ATILES, ids, meta, [own, f1, b1, f2, b2], rights, None, whole
-    )
+    (total,) = multiply((0, -1, 1), one, ATILES, ids, meta, [own, f1, b1], rights, None, whole)
     f3, b3, total = barrier((f3, b3, total))
     far = [send(f3[:near], "row", z_route(1)), send(b3[near:], "row", z_route(-1))]
-    (total,) = multiply((-3, 3), one, ATILES, ids, meta, [f3, b3], rights, total, whole)
+    (total,) = multiply((-2, 2, -3, 3), one, ATILES, ids, meta, [f2, b2, f3, b3], rights, total, whole)
     kept, other = multiply((4,), two, ATILES, ids, meta, far, rights, total, ((0, 32), (32, 32)))
 
     other = send(other, "col", CORE_ROUTE)

time: 138 us -> 137 us (level)
  Pallas kernels: 20.9 us -> 24.3 us
  starting transfers between devices: 47.5 us -> 44.5 us
    ppermute x4 -> x2, waiting for transfers between devices: 7.13 us -> 13.9 us  [spread(): send(meta, BOTH, [(i, i ^ 1 << bit) for i in range(64)])]
    ppermute x6, waiting for transfers between devices: 17.3 us -> 11.6 us  [onward(): return (send(f, 'row', z_route(1)), send(b, 'row', z_route(-1)))]
    ppermute x2, waiting for transfers between devices: 4.66 us -> 0.01 us  [inner(): return send(x, 'col', INNER_ROUTE)]
    ppermute x1, starting transfers between devices: 4.44 us -> 0.09 us  [shards(): still = send(unit(0, 2), BOTH, swap_route())]
    ppermute x3 -> x6, starting transfers between devices: 5.31 us -> 9.49 us  [spread_two(): send(meta, BOTH, [(i, i ^ k << low) for i in range(64)])]
    pallas_call x3, Pallas kernels: 20.9 us -> 24.3 us  [multiply(): pl.pallas_call(functools.partial(kernel, deltas, parts, tiles, first, out...]
    ppermute x1, waiting for transfers between devices: 0.01 us -> 3.16 us  [shards(): up2 = send(units[0], 'depth', y_route(1))]
    ppermute x2, starting transfers between devices: 2.92 us -> 0.73 us  [inner(): return send(x, 'col', INNER_ROUTE)]
  transfers between devices with their start and end apart: 29 -> 30, of which waited for: 16 -> 14; matrix products, arithmetic and copies ran while one was open for 3% -> 3% of each run, Pallas kernels for 12% -> 15%
where the time goes in v4:
time: 137 us; the launch traced here: 136 us
  waiting for transfers between devices  56.4 us (41%)
  starting transfers between devices  44.5 us (32%)
  Pallas kernels  24.3 us (18%)
  local copies, waits for them, and re-layouts  7.39 us (5%)
  other arithmetic  3.44 us (3%)
    pallas_call x3, Pallas kernels, multiply(): pl.pallas_call(functools.partial(kernel, deltas, parts, tiles, first, out...  24.3 us
    ppermute x2, waiting for transfers between devices, spread(): send(meta, BOTH, [(i, i ^ 1 << bit) for i in range(64)])  13.9 us
    ppermute x6, waiting for transfers between devices, onward(): return (send(f, 'row', z_route(1)), send(b, 'row', z_route(-1)))  11.6 us
    ppermute x6, starting transfers between devices, onward(): return (send(f, 'row', z_route(1)), send(b, 'row', z_route(-1)))  10.8 us
    ppermute x6, starting transfers between devices, spread_two(): send(meta, BOTH, [(i, i ^ k << low) for i in range(64)])  9.49 us
    ppermute x1, waiting for transfers between devices, shards(): up1 = send(units[2], ALL, home_route(1))  5.99 us
    ppermute x1, waiting for transfers between devices, shards(): down1 = send(units[3], ALL, home_route(-1))  4.96 us
    ppermute x2, starting transfers between devices, outer(): return send(x, BOTH, outer_route())  4.72 us
  transfers between devices with their start and end apart: 30, of which 14 were waited for; matrix products, arithmetic and copies ran while one was open for 3% of the time, Pallas kernels for 15%

profile of v4, /device:TPU:8, one launch (start us, length us, event | category | flops | bytes accessed | tf_op | source)
XLA Modules:
  0.0 136.2 jit_solution(7676049126553290994)
XLA Ops:
  0.0 1.6 %collective-permute-start = (bf16[3072,128]{1,0:T(8,128)(2,1)}, bf16[3072,128]{1,0:T(8,128)(2,1)S(1)}, u32[]{:S(2)}, u32[]{:S(2)}) collective-permute-start(bf16[3072,128]{1,0:T(8,128)(2,1)} %bitcast.25), channel_id=1, source_target_pairs={{0,8},{4,24},{8,0},{12,16},{16,12},{20,28},{24,4},{28,20},{32,40},... | collective-permute-start | bytes 2359304 | tf_op jit(solution)/shard_map/ppermute | solution.py:255
  1.6 1.3 constant_dynamic-slice_fusion.1
  2.9 1.5 %collective-permute-start.6 = (bf16[2048,128]{1,0:T(8,128)(2,1)S(1)}, bf16[2048,128]{1,0:T(8,128)(2,1)S(1)}, u32[]{:S(2)}, u32[]{:S(2)}) collective-permute-start(bf16[2048,128]{1,0:T(8,128)(2,1)S(1)} %bitcast.20), channel_id=1, source_target_pairs={{0,4},{4,0},{8,12},{12,8},{1,5},{5,1},{9,13},{13,9},{2,6},{6,2},{1... | collective-permute-start | bytes 1572872 | tf_op jit(solution)/shard_map/ppermute | solution.py:259
  4.9 4.7 %collective-permute-start.3 = (s32[1,128]{1,0:T(1,128)S(1)}, s32[1,128]{1,0:T(1,128)S(1)}, u32[]{:S(2)}, u32[]{:S(2)}) collective-permute-start(s32[1,128]{1,0:T(1,128)S(1)} %pad_add_fusion.6), channel_id=1, source_target_pairs={{0,96},{4,100},{8,104},{12,108},{16,112},{20,116},{24,120},{28,124... | collective-permute-start | bytes 1544 | tf_op jit(solution)/shard_map/ppermute | solution.py:240
  11.1 2.9 %collective-permute-done.2 = s32[1,128]{1,0:T(1,128)S(1)} collective-permute-done((s32[1,128]{1,0:T(1,128)S(1)}, s32[1,128]{1,0:T(1,128)S(1)}, u32[]{:S(2)}, u32[]{:S(2)}) %collective-permute-start.2) | collective-permute-done | bytes 544 | tf_op jit(solution)/shard_map/ppermute | solution.py:240
  14.1 1.6 %collective-permute-start.9 = (s32[4,128]{1,0:T(4,128)S(1)}, s32[4,128]{1,0:T(4,128)S(1)}, u32[]{:S(2)}, u32[]{:S(2)}) collective-permute-start(s32[4,128]{1,0:T(4,128)S(1)} %pad_add_fusion.3), channel_id=1, source_target_pairs={{0,24},{4,28},{8,16},{12,20},{16,8},{20,12},{24,0},{28,4},{32,56},... | collective-permute-start | bytes 6152 | tf_op jit(solution)/shard_map/ppermute | solution.py:240
  16.4 1.8 %collective-permute-start.7 = (s32[4,128]{1,0:T(4,128)S(1)}, s32[4,128]{1,0:T(4,128)S(1)}, u32[]{:S(2)}, u32[]{:S(2)}) collective-permute-start(s32[4,128]{1,0:T(4,128)S(1)} %pad_add_fusion.3), channel_id=1, source_target_pairs={{0,8},{4,12},{8,0},{12,4},{16,24},{20,28},{24,16},{28,20},{32,40},... | collective-permute-start | bytes 6152 | tf_op jit(solution)/shard_map/ppermute | solution.py:240
  18.3 4.3 %collective-permute-start.5 = (bf16[3072,128]{1,0:T(8,128)(2,1)S(1)}, bf16[3072,128]{1,0:T(8,128)(2,1)S(1)}, u32[]{:S(2)}, u32[]{:S(2)}) collective-permute-start(bf16[3072,128]{1,0:T(8,128)(2,1)S(1)} %collective-permute-done.refs_2_), channel_id=1, source_target_pairs={{0,224},{16,240},{32,0},{48,16},{64,32},{80,48},{96,64},{112,80},{... | collective-permute-start | bytes 2359304 | tf_op jit(solution)/shard_map/ppermute | solution.py:225
  22.7 3.3 %collective-permute-start.17 = (bf16[3072,128]{1,0:T(8,128)(2,1)S(1)}, bf16[3072,128]{1,0:T(8,128)(2,1)S(1)}, u32[]{:S(2)}, u32[]{:S(2)}) collective-permute-start(bf16[3072,128]{1,0:T(8,128)(2,1)S(1)} %get-tuple-element.53), channel_id=1, source_target_pairs={{0,24},{4,28},{8,16},{12,20},{16,8},{20,12},{24,0},{28,4},{32,56},... | collective-permute-start | bytes 2359304 | tf_op jit(solution)/shard_map/ppermute | solution.py:233
  26.1 1.2 collective-permute-done.10
  27.2 3.4 %collective-permute-start.11 = (s32[32,128]{1,0:T(8,128)S(1)}, s32[32,128]{1,0:T(8,128)S(1)}, u32[]{:S(2)}, u32[]{:S(2)}) collective-permute-start(s32[32,128]{1,0:T(8,128)S(1)} %pad_add_fusion.1), channel_id=1, source_target_pairs={{0,128},{4,132},{8,136},{12,140},{16,144},{20,148},{24,152},{28,15... | collective-permute-start | bytes 49160 | tf_op jit(solution)/shard_map/ppermute | solution.py:245
  30.6 12.8 %collective-permute-done.11 = s32[32,128]{1,0:T(8,128)S(1)} collective-permute-done((s32[32,128]{1,0:T(8,128)S(1)}, s32[32,128]{1,0:T(8,128)S(1)}, u32[]{:S(2)}, u32[]{:S(2)}) %collective-permute-start.11) | collective-permute-done | bytes 16416 | tf_op jit(solution)/shard_map/ppermute | solution.py:245
  43.6 3.1 %collective-permute-start.13 = (bf16[3072,128]{1,0:T(8,128)(2,1)S(1)}, bf16[3072,128]{1,0:T(8,128)(2,1)}, u32[]{:S(2)}, u32[]{:S(2)}) collective-permute-start(bf16[3072,128]{1,0:T(8,128)(2,1)S(1)} %collective-permute-done.5.refs_4_), channel_id=1, source_target_pairs={{0,224},{16,240},{32,0},{48,16},{64,32},{80,48},{96,64},{112,80},{... | collective-permute-start | bytes 2359304 | tf_op jit(solution)/shard_map/ppermute | solution.py:225
  49.5 1.4 %collective-permute-start.19 = (bf16[3072,128]{1,0:T(8,128)(2,1)}, bf16[3072,128]{1,0:T(8,128)(2,1)}, u32[]{:S(2)}, u32[]{:S(2)}) collective-permute-start(bf16[3072,128]{1,0:T(8,128)(2,1)} %pad_maximum_fusion.2), channel_id=1, source_target_pairs={{0,24},{4,28},{8,16},{12,20},{16,8},{20,12},{24,0},{28,4},{32,56},... | collective-permute-start | bytes 2359304 | tf_op jit(solution)/shard_map/ppermute | solution.py:233
  50.9 11.2 %collective-permute-done.12.refs_2_ = bf16[3072,128]{1,0:T(8,128)(2,1)} collective-permute-done((bf16[3072,128]{1,0:T(8,128)(2,1)S(1)}, bf16[3072,128]{1,0:T(8,128)(2,1)}, u32[]{:S(2)}, u32[]{:S(2)}) %collective-permute-start.12) | collective-permute-done | bytes 786464 | tf_op jit(solution)/shard_map/ppermute | solution.py:225
  62.5 2.9 %collective-permute-start.15 = (bf16[3072,128]{1,0:T(8,128)(2,1)}, bf16[3072,128]{1,0:T(8,128)(2,1)}, u32[]{:S(2)}, u32[]{:S(2)}) collective-permute-start(bf16[3072,128]{1,0:T(8,128)(2,1)} %collective-permute-done.13.refs_3_), channel_id=1, source_target_pairs={{0,224},{16,240},{32,0},{48,16},{64,32},{80,48},{96,64},{112,80},{... | collective-permute-start | bytes 2359304 | tf_op jit(solution)/shard_map/ppermute | solution.py:225
  65.4 2.3 %collective-permute-done.19.refs_9_.refs_10_.refs_8_ = bf16[3072,128]{1,0:T(8,128)(2,1)} collective-permute-done((bf16[3072,128]{1,0:T(8,128)(2,1)}, bf16[3072,128]{1,0:T(8,128)(2,1)}, u32[]{:S(2)}, u32[]{:S(2)}) %collective-permute-start.19) | collective-permute-done | bytes 786464 | tf_op jit(solution)/shard_map/ppermute | solution.py:233
  71.2 8.5 %products_0_7_1.1.refs_11_ = f32[8192,128]{1,0:T(8,128)S(1)} custom-call(s32[8]{0:T(128)S(1)} %stack.26.refs_0_, s32[64,128]{1,0:T(8,128)S(1)} %pad_add_fusion.refs_1_, bf16[3072,128]{1,0:T(8,128)(2,1)S(1)} %copy-done.1, bf16[3072,128]{1,0:T(8,128)(2,1)S(1)} %copy-done.5, bf16[3072,128]{1,0:T(8,128)(2,1)S(1)} %copy-done.3, ...), custom_call_target="tpu_custom_call" | custom-call | flops 120000000 | bytes 20000000 | tf_op jit(solution)/shard_map/products_0_7_1/pallas_call | solution.py:200
  82.1 1.2 collective-permute-start.20
  83.3 2.8 %collective-permute-start.21 = (bf16[1536,128]{1,0:T(8,128)(2,1)S(1)}, bf16[1536,128]{1,0:T(8,128)(2,1)S(1)}, u32[]{:S(2)}, u32[]{:S(2)}) collective-permute-start(bf16[1536,128]{1,0:T(8,128)(2,1)S(1)} %slice.79), channel_id=1, source_target_pairs={{0,224},{16,240},{32,0},{48,16},{64,32},{80,48},{96,64},{112,80},{... | collective-permute-start | bytes 1179656 | tf_op jit(solution)/shard_map/ppermute | solution.py:293
  86.1 11.3 %products_6_2_5_3.1.refs_9_ = f32[8192,128]{1,0:T(8,128)S(1)} custom-call(s32[8]{0:T(128)S(1)} %stack.26.refs_0_, s32[64,128]{1,0:T(8,128)S(1)} %pad_add_fusion.refs_1_, bf16[3072,128]{1,0:T(8,128)(2,1)} %collective-permute-done.12.refs_2_, bf16[3072,128]{1,0:T(8,128)(2,1)} %collective-permute-done.13.refs_3_, ...), custom_call_target="tpu_custom_call" | custom-call | flops 160000000 | bytes 24000000 | tf_op jit(solution)/shard_map/products_6_2_5_3/pallas_call | solution.py:200
  97.4 4.4 %products_4.1 = (f32[4096,128]{1,0:T(8,128)S(1)}, f32[4096,128]{1,0:T(8,128)S(1)}) custom-call(s32[8]{0:T(128)S(1)} %stack.26.refs_0_, s32[64,128]{1,0:T(8,128)S(1)} %pad_add_fusion.refs_1_, bf16[1536,128]{1,0:T(8,128)(2,1)S(1)} %collective-permute-done.20.refs_2_, bf16[1536,128]{1,0:T(8,128)(2,1)S(1)} %collective-permute-done.21.refs_3_, ...), custom_call_target="tpu_custom_call" | custom-call | flops 40000000 | bytes 12000000 | tf_op jit(solution)/shard_map/products_4/pallas_call | solution.py:200
  102.0 4.1 %collective-permute-done.22 = f32[4096,128]{1,0:T(8,128)S(1)} collective-permute-done((f32[4096,128]{1,0:T(8,128)S(1)}, f32[4096,128]{1,0:T(8,128)S(1)}, u32[]{:S(2)}, u32[]{:S(2)}) %collective-permute-start.22) | collective-permute-done | bytes 2097184 | tf_op jit(solution)/shard_map/ppermute | solution.py:297
  106.4 2.0 %collective-permute-start.26 = (f32[512,128]{1,0:T(8,128)S(1)}, f32[512,128]{1,0:T(8,128)S(1)}, u32[]{:S(2)}, u32[]{:S(2)}) collective-permute-start(f32[512,128]{1,0:T(8,128)S(1)} %get-tuple-element.41), channel_id=1, source_target_pairs={{0,3},{1,0},{2,1},{3,2},{4,7},{5,4},{6,5},{7,6},{8,11},{9,8},{10,9... | collective-permute-start | bytes 786440 | tf_op jit(solution)/shard_map/ppermute | solution.py:306
  108.5 1.8 %collective-permute-start.24 = (f32[512,128]{1,0:T(8,128)S(1)}, f32[512,128]{1,0:T(8,128)S(1)}, u32[]{:S(2)}, u32[]{:S(2)}) collective-permute-start(f32[512,128]{1,0:T(8,128)S(1)} %get-tuple-element.39), channel_id=1, source_target_pairs={{0,11},{1,8},{2,9},{3,10},{4,27},{5,24},{6,25},{7,26},{8,3},{9,0},... | collective-permute-start | bytes 786440 | tf_op jit(solution)/shard_map/ppermute | solution.py:308
  110.4 1.2 collective-permute-start.28
  111.5 3.2 %collective-permute-done.25 = f32[512,128]{1,0:T(8,128)S(1)} collective-permute-done((f32[512,128]{1,0:T(8,128)S(1)}, f32[512,128]{1,0:T(8,128)S(1)}, u32[]{:S(2)}, u32[]{:S(2)}) %collective-permute-start.25) | collective-permute-done | bytes 262176 | tf_op jit(solution)/shard_map/ppermute | solution.py:305
  116.0 1.9 %collective-permute-start.29 = (f32[512,128]{1,0:T(8,128)S(1)}, f32[512,128]{1,0:T(8,128)S(1)}, u32[]{:S(2)}, u32[]{:S(2)}) collective-permute-start(f32[512,128]{1,0:T(8,128)S(1)} %get-tuple-element.46), channel_id=1, source_target_pairs={{0,11},{1,8},{2,9},{3,10},{4,27},{5,24},{6,25},{7,26},{8,3},{9,0},... | collective-permute-start | bytes 786440 | tf_op jit(solution)/shard_map/ppermute | solution.py:312
  117.9 5.0 %collective-permute-done.24 = f32[512,128]{1,0:T(8,128)S(1)} collective-permute-done((f32[512,128]{1,0:T(8,128)S(1)}, f32[512,128]{1,0:T(8,128)S(1)}, u32[]{:S(2)}, u32[]{:S(2)}) %collective-permute-start.24) | collective-permute-done | bytes 262176 | tf_op jit(solution)/shard_map/ppermute | solution.py:308
  122.8 6.0 %collective-permute-done.28 = f32[512,128]{1,0:T(8,128)S(1)} collective-permute-done((f32[512,128]{1,0:T(8,128)S(1)}, f32[512,128]{1,0:T(8,128)S(1)}, u32[]{:S(2)}, u32[]{:S(2)}) %collective-permute-start.28) | collective-permute-done | bytes 262176 | tf_op jit(solution)/shard_map/ppermute | solution.py:307
  128.8 3.6 %collective-permute-done.27 = f32[512,128]{1,0:T(8,128)S(1)} collective-permute-done((f32[512,128]{1,0:T(8,128)S(1)}, f32[512,128]{1,0:T(8,128)S(1)}, u32[]{:S(2)}, u32[]{:S(2)}) %collective-permute-start.27) | collective-permute-done | bytes 262176 | tf_op jit(solution)/shard_map/ppermute | solution.py:311
  132.4 2.8 %collective-permute-done.29 = f32[512,128]{1,0:T(8,128)S(1)} collective-permute-done((f32[512,128]{1,0:T(8,128)S(1)}, f32[512,128]{1,0:T(8,128)S(1)}, u32[]{:S(2)}, u32[]{:S(2)}) %collective-permute-start.29) | collective-permute-done | bytes 262176 | tf_op jit(solution)/shard_map/ppermute | solution.py:312
  (79 shorter events, 15.0 us)
Async XLA Ops:
  0.0 14.0 %collective-permute-start = (bf16[3072,128]{1,0:T(8,128)(2,1)}, bf16[3072,128]{1,0:T(8,128)(2,1)S(1)}, u32[]{:S(2)}, u32[]{:S(2)}) collective-permute-start(bf16[3072,128]{1,0:T(8,128)(2,1)} %bitcast.25), channel_id=1, source_target_pairs={{0,8},{4,24},{8,0},{12,16},{16,12},{20,28},{24,4},{28,20},{32,40},... | collective-permute-start | bytes 2359304 | tf_op jit(solution)/shard_map/ppermute | solution.py:255
  2.9 15.4 %collective-permute-start.6 = (bf16[2048,128]{1,0:T(8,128)(2,1)S(1)}, bf16[2048,128]{1,0:T(8,128)(2,1)S(1)}, u32[]{:S(2)}, u32[]{:S(2)}) collective-permute-start(bf16[2048,128]{1,0:T(8,128)(2,1)S(1)} %bitcast.20), channel_id=1, source_target_pairs={{0,4},{4,0},{8,12},{12,8},{1,5},{5,1},{9,13},{13,9},{2,6},{6,2},{1... | collective-permute-start | bytes 1572872 | tf_op jit(solution)/shard_map/ppermute | solution.py:259
  4.9 6.2 %collective-permute-start.3 = (s32[1,128]{1,0:T(1,128)S(1)}, s32[1,128]{1,0:T(1,128)S(1)}, u32[]{:S(2)}, u32[]{:S(2)}) collective-permute-start(s32[1,128]{1,0:T(1,128)S(1)} %pad_add_fusion.6), channel_id=1, source_target_pairs={{0,96},{4,100},{8,104},{12,108},{16,112},{20,116},{24,120},{28,124... | collective-permute-start | bytes 1544 | tf_op jit(solution)/shard_map/ppermute | solution.py:240
  9.5 4.4 %collective-permute-start.2 = (s32[1,128]{1,0:T(1,128)S(1)}, s32[1,128]{1,0:T(1,128)S(1)}, u32[]{:S(2)}, u32[]{:S(2)}) collective-permute-start(s32[1,128]{1,0:T(1,128)S(1)} %pad_add_fusion.6), channel_id=1, source_target_pairs={{0,64},{4,68},{8,72},{12,76},{16,80},{20,84},{24,88},{28,92},{32,9... | collective-permute-start | bytes 1544 | tf_op jit(solution)/shard_map/ppermute | solution.py:240
  9.5 4.4 %collective-permute-start.1 = (s32[1,128]{1,0:T(1,128)S(1)}, s32[1,128]{1,0:T(1,128)S(1)}, u32[]{:S(2)}, u32[]{:S(2)}) collective-permute-start(s32[1,128]{1,0:T(1,128)S(1)} %pad_add_fusion.6), channel_id=1, source_target_pairs={{0,32},{4,36},{8,40},{12,44},{16,48},{20,52},{24,56},{28,60},{32,0... | collective-permute-start | bytes 1544 | tf_op jit(solution)/shard_map/ppermute | solution.py:240
  14.1 8.7 %copy-start = (bf16[3072,128]{1,0:T(8,128)(2,1)}, bf16[3072,128]{1,0:T(8,128)(2,1)S(1)}, u32[]{:S(2)}) copy-start(bf16[3072,128]{1,0:T(8,128)(2,1)S(1)} %collective-permute-done.refs_2_) | copy-start | bytes 2359300
  14.1 8.5 %collective-permute-start.9 = (s32[4,128]{1,0:T(4,128)S(1)}, s32[4,128]{1,0:T(4,128)S(1)}, u32[]{:S(2)}, u32[]{:S(2)}) collective-permute-start(s32[4,128]{1,0:T(4,128)S(1)} %pad_add_fusion.3), channel_id=1, source_target_pairs={{0,24},{4,28},{8,16},{12,20},{16,8},{20,12},{24,0},{28,4},{32,56},... | collective-permute-start | bytes 6152 | tf_op jit(solution)/shard_map/ppermute | solution.py:240
  15.7 6.9 %collective-permute-start.8 = (s32[4,128]{1,0:T(4,128)S(1)}, s32[4,128]{1,0:T(4,128)S(1)}, u32[]{:S(2)}, u32[]{:S(2)}) collective-permute-start(s32[4,128]{1,0:T(4,128)S(1)} %pad_add_fusion.3), channel_id=1, source_target_pairs={{0,16},{4,20},{8,24},{12,28},{16,0},{20,4},{24,8},{28,12},{32,48},... | collective-permute-start | bytes 6152 | tf_op jit(solution)/shard_map/ppermute | solution.py:240
  16.4 6.2 %collective-permute-start.7 = (s32[4,128]{1,0:T(4,128)S(1)}, s32[4,128]{1,0:T(4,128)S(1)}, u32[]{:S(2)}, u32[]{:S(2)}) collective-permute-start(s32[4,128]{1,0:T(4,128)S(1)} %pad_add_fusion.3), channel_id=1, source_target_pairs={{0,8},{4,12},{8,0},{12,4},{16,24},{20,28},{24,16},{28,20},{32,40},... | collective-permute-start | bytes 6152 | tf_op jit(solution)/shard_map/ppermute | solution.py:240
  18.3 25.0 %collective-permute-start.5 = (bf16[3072,128]{1,0:T(8,128)(2,1)S(1)}, bf16[3072,128]{1,0:T(8,128)(2,1)S(1)}, u32[]{:S(2)}, u32[]{:S(2)}) collective-permute-start(bf16[3072,128]{1,0:T(8,128)(2,1)S(1)} %collective-permute-done.refs_2_), channel_id=1, source_target_pairs={{0,224},{16,240},{32,0},{48,16},{64,32},{80,48},{96,64},{112,80},{... | collective-permute-start | bytes 2359304 | tf_op jit(solution)/shard_map/ppermute | solution.py:225
  22.6 20.8 %collective-permute-start.4 = (bf16[3072,128]{1,0:T(8,128)(2,1)S(1)}, bf16[3072,128]{1,0:T(8,128)(2,1)S(1)}, u32[]{:S(2)}, u32[]{:S(2)}) collective-permute-start(bf16[3072,128]{1,0:T(8,128)(2,1)S(1)} %collective-permute-done.refs_2_), channel_id=1, source_target_pairs={{0,32},{16,48},{32,64},{48,80},{64,96},{80,112},{96,128},{112,144}... | collective-permute-start | bytes 2359304 | tf_op jit(solution)/shard_map/ppermute | solution.py:225
  22.7 24.0 %collective-permute-start.17 = (bf16[3072,128]{1,0:T(8,128)(2,1)S(1)}, bf16[3072,128]{1,0:T(8,128)(2,1)S(1)}, u32[]{:S(2)}, u32[]{:S(2)}) collective-permute-start(bf16[3072,128]{1,0:T(8,128)(2,1)S(1)} %get-tuple-element.53), channel_id=1, source_target_pairs={{0,24},{4,28},{8,16},{12,20},{16,8},{20,12},{24,0},{28,4},{32,56},... | collective-permute-start | bytes 2359304 | tf_op jit(solution)/shard_map/ppermute | solution.py:233
  26.1 1.2 collective-permute-start.10
  26.1 22.4 %collective-permute-start.16 = (bf16[3072,128]{1,0:T(8,128)(2,1)S(1)}, bf16[3072,128]{1,0:T(8,128)(2,1)S(1)}, u32[]{:S(2)}, u32[]{:S(2)}) collective-permute-start(bf16[3072,128]{1,0:T(8,128)(2,1)S(1)} %get-tuple-element.54), channel_id=1, source_target_pairs={{0,8},{4,12},{8,0},{12,4},{1,9},{5,13},{9,1},{13,5},{2,10},{6,14},... | collective-permute-start | bytes 2359304 | tf_op jit(solution)/shard_map/ppermute | solution.py:229
  27.2 16.1 %collective-permute-start.11 = (s32[32,128]{1,0:T(8,128)S(1)}, s32[32,128]{1,0:T(8,128)S(1)}, u32[]{:S(2)}, u32[]{:S(2)}) collective-permute-start(s32[32,128]{1,0:T(8,128)S(1)} %pad_add_fusion.1), channel_id=1, source_target_pairs={{0,128},{4,132},{8,136},{12,140},{16,144},{20,148},{24,152},{28,15... | collective-permute-start | bytes 49160 | tf_op jit(solution)/shard_map/ppermute | solution.py:245
  43.3 5.1 %copy-start.2 = (bf16[3072,128]{1,0:T(8,128)(2,1)}, bf16[3072,128]{1,0:T(8,128)(2,1)S(1)}, u32[]{:S(2)}) copy-start(bf16[3072,128]{1,0:T(8,128)(2,1)S(1)} %collective-permute-done.5.refs_4_) | copy-start | bytes 2359300
  43.4 18.7 %collective-permute-start.12 = (bf16[3072,128]{1,0:T(8,128)(2,1)S(1)}, bf16[3072,128]{1,0:T(8,128)(2,1)}, u32[]{:S(2)}, u32[]{:S(2)}) collective-permute-start(bf16[3072,128]{1,0:T(8,128)(2,1)S(1)} %collective-permute-done.4.refs_3_), channel_id=1, source_target_pairs={{0,32},{16,48},{32,64},{48,80},{64,96},{80,112},{96,128},{112,144}... | collective-permute-start | bytes 2359304 | tf_op jit(solution)/shard_map/ppermute | solution.py:225
  43.6 18.6 %collective-permute-start.13 = (bf16[3072,128]{1,0:T(8,128)(2,1)S(1)}, bf16[3072,128]{1,0:T(8,128)(2,1)}, u32[]{:S(2)}, u32[]{:S(2)}) collective-permute-start(bf16[3072,128]{1,0:T(8,128)(2,1)S(1)} %collective-permute-done.5.refs_4_), channel_id=1, source_target_pairs={{0,224},{16,240},{32,0},{48,16},{64,32},{80,48},{96,64},{112,80},{... | collective-permute-start | bytes 2359304 | tf_op jit(solution)/shard_map/ppermute | solution.py:225
  47.7 17.7 %collective-permute-start.18 = (bf16[3072,128]{1,0:T(8,128)(2,1)}, bf16[3072,128]{1,0:T(8,128)(2,1)S(1)}, u32[]{:S(2)}, u32[]{:S(2)}) collective-permute-start(bf16[3072,128]{1,0:T(8,128)(2,1)} %pad_maximum_fusion.1), channel_id=1, source_target_pairs={{0,8},{4,12},{8,0},{12,4},{1,9},{5,13},{9,1},{13,5},{2,10},{6,14},... | collective-permute-start | bytes 2359304 | tf_op jit(solution)/shard_map/ppermute | solution.py:229
  49.5 18.3 %collective-permute-start.19 = (bf16[3072,128]{1,0:T(8,128)(2,1)}, bf16[3072,128]{1,0:T(8,128)(2,1)}, u32[]{:S(2)}, u32[]{:S(2)}) collective-permute-start(bf16[3072,128]{1,0:T(8,128)(2,1)} %pad_maximum_fusion.2), channel_id=1, source_target_pairs={{0,24},{4,28},{8,16},{12,20},{16,8},{20,12},{24,0},{28,4},{32,56},... | collective-permute-start | bytes 2359304 | tf_op jit(solution)/shard_map/ppermute | solution.py:233
  62.1 17.9 %collective-permute-start.14 = (bf16[3072,128]{1,0:T(8,128)(2,1)}, bf16[3072,128]{1,0:T(8,128)(2,1)}, u32[]{:S(2)}, u32[]{:S(2)}) collective-permute-start(bf16[3072,128]{1,0:T(8,128)(2,1)} %collective-permute-done.12.refs_2_), channel_id=1, source_target_pairs={{0,32},{16,48},{32,64},{48,80},{64,96},{80,112},{96,128},{112,144}... | collective-permute-start | bytes 2359304 | tf_op jit(solution)/shard_map/ppermute | solution.py:225
  62.5 17.6 %collective-permute-start.15 = (bf16[3072,128]{1,0:T(8,128)(2,1)}, bf16[3072,128]{1,0:T(8,128)(2,1)}, u32[]{:S(2)}, u32[]{:S(2)}) collective-permute-start(bf16[3072,128]{1,0:T(8,128)(2,1)} %collective-permute-done.13.refs_3_), channel_id=1, source_target_pairs={{0,224},{16,240},{32,0},{48,16},{64,32},{80,48},{96,64},{112,80},{... | collective-permute-start | bytes 2359304 | tf_op jit(solution)/shard_map/ppermute | solution.py:225
  82.1 15.3 %collective-permute-start.20 = (bf16[1536,128]{1,0:T(8,128)(2,1)S(1)}, bf16[1536,128]{1,0:T(8,128)(2,1)S(1)}, u32[]{:S(2)}, u32[]{:S(2)}) collective-permute-start(bf16[1536,128]{1,0:T(8,128)(2,1)S(1)} %slice.78), channel_id=1, source_target_pairs={{0,32},{16,48},{32,64},{48,80},{64,96},{80,112},{96,128},{112,144}... | collective-permute-start | bytes 1179656 | tf_op jit(solution)/shard_map/ppermute | solution.py:293
  83.3 14.1 %collective-permute-start.21 = (bf16[1536,128]{1,0:T(8,128)(2,1)S(1)}, bf16[1536,128]{1,0:T(8,128)(2,1)S(1)}, u32[]{:S(2)}, u32[]{:S(2)}) collective-permute-start(bf16[1536,128]{1,0:T(8,128)(2,1)S(1)} %slice.79), channel_id=1, source_target_pairs={{0,224},{16,240},{32,0},{48,16},{64,32},{80,48},{96,64},{112,80},{... | collective-permute-start | bytes 1179656 | tf_op jit(solution)/shard_map/ppermute | solution.py:293
  101.9 4.2 %collective-permute-start.22 = (f32[4096,128]{1,0:T(8,128)S(1)}, f32[4096,128]{1,0:T(8,128)S(1)}, u32[]{:S(2)}, u32[]{:S(2)}) collective-permute-start(f32[4096,128]{1,0:T(8,128)S(1)} %get-tuple-element.38), channel_id=1, source_target_pairs={{0,4},{4,0},{8,12},{12,8},{1,5},{5,1},{9,13},{13,9},{2,6},{6,2},{1... | collective-permute-start | bytes 6291464 | tf_op jit(solution)/shard_map/ppermute | solution.py:297
  106.3 8.4 %collective-permute-start.25 = (f32[512,128]{1,0:T(8,128)S(1)}, f32[512,128]{1,0:T(8,128)S(1)}, u32[]{:S(2)}, u32[]{:S(2)}) collective-permute-start(f32[512,128]{1,0:T(8,128)S(1)} %get-tuple-element.40), channel_id=1, source_target_pairs={{0,1},{1,2},{2,3},{3,0},{4,5},{5,6},{6,7},{7,4},{8,9},{9,10},{10,1... | collective-permute-start | bytes 786440 | tf_op jit(solution)/shard_map/ppermute | solution.py:305
  106.4 8.4 %collective-permute-start.26 = (f32[512,128]{1,0:T(8,128)S(1)}, f32[512,128]{1,0:T(8,128)S(1)}, u32[]{:S(2)}, u32[]{:S(2)}) collective-permute-start(f32[512,128]{1,0:T(8,128)S(1)} %get-tuple-element.41), channel_id=1, source_target_pairs={{0,3},{1,0},{2,1},{3,2},{4,7},{5,4},{6,5},{7,6},{8,11},{9,8},{10,9... | collective-permute-start | bytes 786440 | tf_op jit(solution)/shard_map/ppermute | solution.py:306
  108.4 20.4 %collective-permute-start.23 = (f32[1024,128]{1,0:T(8,128)S(1)}, f32[1024,128]{1,0:T(8,128)S(1)}, u32[]{:S(2)}, u32[]{:S(2)}) collective-permute-start(f32[1024,128]{1,0:T(8,128)S(1)} %slice_add_fusion), channel_id=1, source_target_pairs={{0,8},{4,24},{8,0},{12,16},{16,12},{20,28},{24,4},{28,20},{32,40},... | collective-permute-start | bytes 1572872 | tf_op jit(solution)/shard_map/ppermute | solution.py:309
  108.5 14.3 %collective-permute-start.24 = (f32[512,128]{1,0:T(8,128)S(1)}, f32[512,128]{1,0:T(8,128)S(1)}, u32[]{:S(2)}, u32[]{:S(2)}) collective-permute-start(f32[512,128]{1,0:T(8,128)S(1)} %get-tuple-element.39), channel_id=1, source_target_pairs={{0,11},{1,8},{2,9},{3,10},{4,27},{5,24},{6,25},{7,26},{8,3},{9,0},... | collective-permute-start | bytes 786440 | tf_op jit(solution)/shard_map/ppermute | solution.py:308
  110.4 18.5 %collective-permute-start.28 = (f32[512,128]{1,0:T(8,128)S(1)}, f32[512,128]{1,0:T(8,128)S(1)}, u32[]{:S(2)}, u32[]{:S(2)}) collective-permute-start(f32[512,128]{1,0:T(8,128)S(1)} %get-tuple-element.43), channel_id=1, source_target_pairs={{0,9},{1,10},{2,11},{3,8},{4,25},{5,26},{6,27},{7,24},{8,1},{9,2},... | collective-permute-start | bytes 786440 | tf_op jit(solution)/shard_map/ppermute | solution.py:307
  114.9 17.6 %collective-permute-start.27 = (f32[512,128]{1,0:T(8,128)S(1)}, f32[512,128]{1,0:T(8,128)S(1)}, u32[]{:S(2)}, u32[]{:S(2)}) collective-permute-start(f32[512,128]{1,0:T(8,128)S(1)} %get-tuple-element.45), channel_id=1, source_target_pairs={{0,9},{1,10},{2,11},{3,8},{4,25},{5,26},{6,27},{7,24},{8,1},{9,2},... | collective-permute-start | bytes 786440 | tf_op jit(solution)/shard_map/ppermute | solution.py:311
  116.0 19.3 %collective-permute-start.29 = (f32[512,128]{1,0:T(8,128)S(1)}, f32[512,128]{1,0:T(8,128)S(1)}, u32[]{:S(2)}, u32[]{:S(2)}) collective-permute-start(f32[512,128]{1,0:T(8,128)S(1)} %get-tuple-element.46), channel_id=1, source_target_pairs={{0,11},{1,8},{2,9},{3,10},{4,27},{5,24},{6,25},{7,26},{8,3},{9,0},... | collective-permute-start | bytes 786440 | tf_op jit(solution)/shard_map/ppermute | solution.py:312
  (8 other events, 26.5 us)

commit v5 on v4

--- a/solution.py
+++ b/solution.py
@@ -266,12 +266,10 @@
     meta = jnp.concatenate(
         [left_meta.reshape(1, 32), right_meta.reshape(1, 64), jnp.zeros((1, 32), jnp.int32)], axis=1
     )
-    meta = spread_two(meta, 3)
-    own, meta = barrier((own, meta))
+    meta = spread_two(spread_two(meta, 3), 1)
+    own, right, meta = barrier((own, right, meta))
 
     f1, b1 = onward(own, own)
-    meta = spread_two(meta, 1)
-    right, meta = barrier((right, meta))
     in1, out1 = inner(right[QUARTER:]), outer(right[:REST])
     meta = spread(spread(meta, BITS[4]), BITS[5])
     f1, b1, meta = barrier((f1, b1, meta))

time: 137 us -> 136 us (level); the launches traced: 136 us -> 134 us
  starting transfers between devices: 44.5 us -> 41.8 us
  Pallas kernels: 24.3 us -> 22 us
  waiting for transfers between devices: 56.4 us -> 58.5 us
    ppermute x6, waiting for transfers between devices: 3.79 us -> 6.53 us  [spread_two(): send(meta, BOTH, [(i, i ^ k << low) for i in range(64)])]
    ppermute x1, waiting for transfers between devices: 5.99 us -> 3.71 us  [shards(): up1 = send(units[2], ALL, home_route(1))]
    pallas_call x3, Pallas kernels: 24.3 us -> 22 us  [multiply(): pl.pallas_call(functools.partial(kernel, deltas, parts, tiles, first, out...]
    ppermute x1, starting transfers between devices: 0.09 us -> 2.29 us  [shards(): still = send(unit(0, 2), BOTH, swap_route())]
    ppermute x1, waiting for transfers between devices: 3.16 us -> 1.05 us  [shards(): up2 = send(units[0], 'depth', y_route(1))]
    ppermute x2, starting transfers between devices: 4.72 us -> 2.76 us  [outer(): return send(x, BOTH, outer_route())]
    ppermute x1, starting transfers between devices: 0.08 us -> 2.02 us  [shards(): up2 = send(units[0], 'depth', y_route(1))]
    ppermute x1, starting transfers between devices: 2.01 us -> 0.09 us  [shards(): down2 = send(units[1], 'depth', y_route(-1))]
  transfers between devices with their start and end apart: 30 -> 30, of which waited for: 14 -> 15; matrix products, arithmetic and copies ran while one was open for 3% -> 2% of each run, Pallas kernels for 15% -> 13%
where the time goes in v5:
time: 136 us; the launch traced here: 134 us
  waiting for transfers between devices  58.5 us (43%)
  starting transfers between devices  41.8 us (31%)
  Pallas kernels  22 us (16%)
  local copies, waits for them, and re-layouts  7.46 us (5%)
  other arithmetic  3.43 us (3%)
    pallas_call x3, Pallas kernels, multiply(): pl.pallas_call(functools.partial(kernel, deltas, parts, tiles, first, out...  22 us
    ppermute x2, waiting for transfers between devices, spread(): send(meta, BOTH, [(i, i ^ 1 << bit) for i in range(64)])  14.1 us
    ppermute x6, waiting for transfers between devices, onward(): return (send(f, 'row', z_route(1)), send(b, 'row', z_route(-1)))  10.4 us
    ppermute x6, starting transfers between devices, onward(): return (send(f, 'row', z_route(1)), send(b, 'row', z_route(-1)))  9.75 us
    ppermute x6, starting transfers between devices, spread_two(): send(meta, BOTH, [(i, i ^ k << low) for i in range(64)])  9.43 us
    ppermute x6, waiting for transfers between devices, spread_two(): send(meta, BOTH, [(i, i ^ k << low) for i in range(64)])  6.53 us
    ppermute x1, waiting for transfers between devices, shards(): up3 = send(unit(2) + up2, ALL, home_route(1))  5.24 us
    ppermute x1, waiting for transfers between devices, shards(): down1 = send(units[3], ALL, home_route(-1))  5.22 us
  transfers between devices with their start and end apart: 30, of which 15 were waited for; matrix products, arithmetic and copies ran while one was open for 2% of the time, Pallas kernels for 13%

profile of v5, /device:TPU:8, one launch (start us, length us, event | category | flops | bytes accessed | tf_op | source)
XLA Modules:
  0.0 133.5 jit_solution(977713328227966028)
XLA Ops:
  0.0 1.3 constant_dynamic-slice_fusion.1
  1.4 1.6 %collective-permute-start = (bf16[3072,128]{1,0:T(8,128)(2,1)}, bf16[3072,128]{1,0:T(8,128)(2,1)S(1)}, u32[]{:S(2)}, u32[]{:S(2)}) collective-permute-start(bf16[3072,128]{1,0:T(8,128)(2,1)} %bitcast.5), channel_id=1, source_target_pairs={{0,8},{4,24},{8,0},{12,16},{16,12},{20,28},{24,4},{28,20},{32,40},... | collective-permute-start | bytes 2359304 | tf_op jit(solution)/shard_map/ppermute | solution.py:255
  3.6 4.7 %collective-permute-start.4 = (s32[1,128]{1,0:T(1,128)S(1)}, s32[1,128]{1,0:T(1,128)S(1)}, u32[]{:S(2)}, u32[]{:S(2)}) collective-permute-start(s32[1,128]{1,0:T(1,128)S(1)} %pad_add_fusion.5), channel_id=1, source_target_pairs={{0,96},{4,100},{8,104},{12,108},{16,112},{20,116},{24,120},{28,124... | collective-permute-start | bytes 1544 | tf_op jit(solution)/shard_map/ppermute | solution.py:240
  9.7 2.9 %collective-permute-done.3 = s32[1,128]{1,0:T(1,128)S(1)} collective-permute-done((s32[1,128]{1,0:T(1,128)S(1)}, s32[1,128]{1,0:T(1,128)S(1)}, u32[]{:S(2)}, u32[]{:S(2)}) %collective-permute-start.3) | collective-permute-done | bytes 544 | tf_op jit(solution)/shard_map/ppermute | solution.py:240
  12.7 1.8 %collective-permute-start.7 = (s32[4,128]{1,0:T(4,128)S(1)}, s32[4,128]{1,0:T(4,128)S(1)}, u32[]{:S(2)}, u32[]{:S(2)}) collective-permute-start(s32[4,128]{1,0:T(4,128)S(1)} %pad_add_fusion.2), channel_id=1, source_target_pairs={{0,24},{4,28},{8,16},{12,20},{16,8},{20,12},{24,0},{28,4},{32,56},... | collective-permute-start | bytes 6152 | tf_op jit(solution)/shard_map/ppermute | solution.py:240
  15.4 1.5 %collective-permute-start.5 = (s32[4,128]{1,0:T(4,128)S(1)}, s32[4,128]{1,0:T(4,128)S(1)}, u32[]{:S(2)}, u32[]{:S(2)}) collective-permute-start(s32[4,128]{1,0:T(4,128)S(1)} %pad_add_fusion.2), channel_id=1, source_target_pairs={{0,8},{4,12},{8,0},{12,4},{16,24},{20,28},{24,16},{28,20},{32,40},... | collective-permute-start | bytes 6152 | tf_op jit(solution)/shard_map/ppermute | solution.py:240
  17.6 2.1 %collective-permute-done.6 = s32[4,128]{1,0:T(4,128)S(1)} collective-permute-done((s32[4,128]{1,0:T(4,128)S(1)}, s32[4,128]{1,0:T(4,128)S(1)}, u32[]{:S(2)}, u32[]{:S(2)}) %collective-permute-start.6) | collective-permute-done | bytes 2080 | tf_op jit(solution)/shard_map/ppermute | solution.py:240
  19.8 3.2 %collective-permute-start.9 = (bf16[3072,128]{1,0:T(8,128)(2,1)S(1)}, bf16[3072,128]{1,0:T(8,128)(2,1)S(1)}, u32[]{:S(2)}, u32[]{:S(2)}) collective-permute-start(bf16[3072,128]{1,0:T(8,128)(2,1)S(1)} %collective-permute-done.refs_2_), channel_id=1, source_target_pairs={{0,224},{16,240},{32,0},{48,16},{64,32},{80,48},{96,64},{112,80},{... | collective-permute-start | bytes 2359304 | tf_op jit(solution)/shard_map/ppermute | solution.py:225
  23.1 1.6 %collective-permute-start.17 = (bf16[3072,128]{1,0:T(8,128)(2,1)S(1)}, bf16[3072,128]{1,0:T(8,128)(2,1)S(1)}, u32[]{:S(2)}, u32[]{:S(2)}) collective-permute-start(bf16[3072,128]{1,0:T(8,128)(2,1)S(1)} %get-tuple-element.51), channel_id=1, source_target_pairs={{0,24},{4,28},{8,16},{12,20},{16,8},{20,12},{24,0},{28,4},{32,56},... | collective-permute-start | bytes 2359304 | tf_op jit(solution)/shard_map/ppermute | solution.py:233
  25.8 3.4 %collective-permute-start.11 = (s32[32,128]{1,0:T(8,128)S(1)}, s32[32,128]{1,0:T(8,128)S(1)}, u32[]{:S(2)}, u32[]{:S(2)}) collective-permute-start(s32[32,128]{1,0:T(8,128)S(1)} %pad_add_fusion.1), channel_id=1, source_target_pairs={{0,128},{4,132},{8,136},{12,140},{16,144},{20,148},{24,152},{28,15... | collective-permute-start | bytes 49160 | tf_op jit(solution)/shard_map/ppermute | solution.py:245
  29.2 13.4 %collective-permute-done.11 = s32[32,128]{1,0:T(8,128)S(1)} collective-permute-done((s32[32,128]{1,0:T(8,128)S(1)}, s32[32,128]{1,0:T(8,128)S(1)}, u32[]{:S(2)}, u32[]{:S(2)}) %collective-permute-start.11) | collective-permute-done | bytes 16416 | tf_op jit(solution)/shard_map/ppermute | solution.py:245
  42.7 3.2 %collective-permute-start.13 = (bf16[3072,128]{1,0:T(8,128)(2,1)S(1)}, bf16[3072,128]{1,0:T(8,128)(2,1)}, u32[]{:S(2)}, u32[]{:S(2)}) collective-permute-start(bf16[3072,128]{1,0:T(8,128)(2,1)S(1)} %collective-permute-done.9.refs_4_), channel_id=1, source_target_pairs={{0,224},{16,240},{32,0},{48,16},{64,32},{80,48},{96,64},{112,80},{... | collective-permute-start | bytes 2359304 | tf_op jit(solution)/shard_map/ppermute | solution.py:225
  48.6 1.2 collective-permute-start.19
  49.8 10.4 %collective-permute-done.12.refs_2_ = bf16[3072,128]{1,0:T(8,128)(2,1)} collective-permute-done((bf16[3072,128]{1,0:T(8,128)(2,1)S(1)}, bf16[3072,128]{1,0:T(8,128)(2,1)}, u32[]{:S(2)}, u32[]{:S(2)}) %collective-permute-start.12) | collective-permute-done | bytes 786464 | tf_op jit(solution)/shard_map/ppermute | solution.py:225
  60.2 3.2 %collective-permute-start.15 = (bf16[3072,128]{1,0:T(8,128)(2,1)}, bf16[3072,128]{1,0:T(8,128)(2,1)}, u32[]{:S(2)}, u32[]{:S(2)}) collective-permute-start(bf16[3072,128]{1,0:T(8,128)(2,1)} %collective-permute-done.13.refs_3_), channel_id=1, source_target_pairs={{0,224},{16,240},{32,0},{48,16},{64,32},{80,48},{96,64},{112,80},{... | collective-permute-start | bytes 2359304 | tf_op jit(solution)/shard_map/ppermute | solution.py:225
  63.6 2.8 %collective-permute-done.19.refs_9_.refs_10_.refs_8_ = bf16[3072,128]{1,0:T(8,128)(2,1)} collective-permute-done((bf16[3072,128]{1,0:T(8,128)(2,1)}, bf16[3072,128]{1,0:T(8,128)(2,1)}, u32[]{:S(2)}, u32[]{:S(2)}) %collective-permute-start.19) | collective-permute-done | bytes 786464 | tf_op jit(solution)/shard_map/ppermute | solution.py:233
  66.3 1.1 copy-done.1
  67.5 1.1 copy-done.3
  69.7 8.4 %products_0_7_1.1.refs_11_ = f32[8192,128]{1,0:T(8,128)S(1)} custom-call(s32[8]{0:T(128)S(1)} %stack.26.refs_0_, s32[64,128]{1,0:T(8,128)S(1)} %pad_add_fusion.refs_1_, bf16[3072,128]{1,0:T(8,128)(2,1)S(1)} %copy-done.1, bf16[3072,128]{1,0:T(8,128)(2,1)S(1)} %copy-done.5, bf16[3072,128]{1,0:T(8,128)(2,1)S(1)} %copy-done.3, ...), custom_call_target="tpu_custom_call" | custom-call | flops 120000000 | bytes 20000000 | tf_op jit(solution)/shard_map/products_0_7_1/pallas_call | solution.py:200
  80.3 3.2 %collective-permute-start.21 = (bf16[1536,128]{1,0:T(8,128)(2,1)S(1)}, bf16[1536,128]{1,0:T(8,128)(2,1)S(1)}, u32[]{:S(2)}, u32[]{:S(2)}) collective-permute-start(bf16[1536,128]{1,0:T(8,128)(2,1)S(1)} %slice.79), channel_id=1, source_target_pairs={{0,224},{16,240},{32,0},{48,16},{64,32},{80,48},{96,64},{112,80},{... | collective-permute-start | bytes 1179656 | tf_op jit(solution)/shard_map/ppermute | solution.py:291
  83.5 9.6 %products_6_2_5_3.1.refs_9_ = f32[8192,128]{1,0:T(8,128)S(1)} custom-call(s32[8]{0:T(128)S(1)} %stack.26.refs_0_, s32[64,128]{1,0:T(8,128)S(1)} %pad_add_fusion.refs_1_, bf16[3072,128]{1,0:T(8,128)(2,1)} %collective-permute-done.12.refs_2_, bf16[3072,128]{1,0:T(8,128)(2,1)} %collective-permute-done.13.refs_3_, ...), custom_call_target="tpu_custom_call" | custom-call | flops 160000000 | bytes 24000000 | tf_op jit(solution)/shard_map/products_6_2_5_3/pallas_call | solution.py:200
  93.2 4.0 %products_4.1 = (f32[4096,128]{1,0:T(8,128)S(1)}, f32[4096,128]{1,0:T(8,128)S(1)}) custom-call(s32[8]{0:T(128)S(1)} %stack.26.refs_0_, s32[64,128]{1,0:T(8,128)S(1)} %pad_add_fusion.refs_1_, bf16[1536,128]{1,0:T(8,128)(2,1)S(1)} %collective-permute-done.20.refs_2_, bf16[1536,128]{1,0:T(8,128)(2,1)S(1)} %collective-permute-done.21.refs_3_, ...), custom_call_target="tpu_custom_call" | custom-call | flops 40000000 | bytes 12000000 | tf_op jit(solution)/shard_map/products_4/pallas_call | solution.py:200
  97.3 4.1 %collective-permute-done.22 = f32[4096,128]{1,0:T(8,128)S(1)} collective-permute-done((f32[4096,128]{1,0:T(8,128)S(1)}, f32[4096,128]{1,0:T(8,128)S(1)}, u32[]{:S(2)}, u32[]{:S(2)}) %collective-permute-start.22) | collective-permute-done | bytes 2097184 | tf_op jit(solution)/shard_map/ppermute | solution.py:295
  101.6 2.0 %collective-permute-start.25 = (f32[512,128]{1,0:T(8,128)S(1)}, f32[512,128]{1,0:T(8,128)S(1)}, u32[]{:S(2)}, u32[]{:S(2)}) collective-permute-start(f32[512,128]{1,0:T(8,128)S(1)} %get-tuple-element.38), channel_id=1, source_target_pairs={{0,1},{1,2},{2,3},{3,0},{4,5},{5,6},{6,7},{7,4},{8,9},{9,10},{10,1... | collective-permute-start | bytes 786440 | tf_op jit(solution)/shard_map/ppermute | solution.py:303
  103.8 2.3 %collective-permute-start.23 = (f32[1024,128]{1,0:T(8,128)S(1)}, f32[1024,128]{1,0:T(8,128)S(1)}, u32[]{:S(2)}, u32[]{:S(2)}) collective-permute-start(f32[1024,128]{1,0:T(8,128)S(1)} %slice_add_fusion), channel_id=1, source_target_pairs={{0,8},{4,24},{8,0},{12,16},{16,12},{20,28},{24,4},{28,20},{32,40},... | collective-permute-start | bytes 1572872 | tf_op jit(solution)/shard_map/ppermute | solution.py:307
  106.8 2.2 %collective-permute-start.28 = (f32[512,128]{1,0:T(8,128)S(1)}, f32[512,128]{1,0:T(8,128)S(1)}, u32[]{:S(2)}, u32[]{:S(2)}) collective-permute-start(f32[512,128]{1,0:T(8,128)S(1)} %get-tuple-element.41), channel_id=1, source_target_pairs={{0,9},{1,10},{2,11},{3,8},{4,25},{5,26},{6,27},{7,24},{8,1},{9,2},... | collective-permute-start | bytes 786440 | tf_op jit(solution)/shard_map/ppermute | solution.py:305
  110.0 1.7 %collective-permute-done.26 = f32[512,128]{1,0:T(8,128)S(1)} collective-permute-done((f32[512,128]{1,0:T(8,128)S(1)}, f32[512,128]{1,0:T(8,128)S(1)}, u32[]{:S(2)}, u32[]{:S(2)}) %collective-permute-start.26) | collective-permute-done | bytes 262176 | tf_op jit(solution)/shard_map/ppermute | solution.py:304
  111.8 2.2 %collective-permute-start.27 = (f32[512,128]{1,0:T(8,128)S(1)}, f32[512,128]{1,0:T(8,128)S(1)}, u32[]{:S(2)}, u32[]{:S(2)}) collective-permute-start(f32[512,128]{1,0:T(8,128)S(1)} %get-tuple-element.43), channel_id=1, source_target_pairs={{0,9},{1,10},{2,11},{3,8},{4,25},{5,26},{6,27},{7,24},{8,1},{9,2},... | collective-permute-start | bytes 786440 | tf_op jit(solution)/shard_map/ppermute | solution.py:309
  114.8 5.2 %collective-permute-done.24 = f32[512,128]{1,0:T(8,128)S(1)} collective-permute-done((f32[512,128]{1,0:T(8,128)S(1)}, f32[512,128]{1,0:T(8,128)S(1)}, u32[]{:S(2)}, u32[]{:S(2)}) %collective-permute-start.24) | collective-permute-done | bytes 262176 | tf_op jit(solution)/shard_map/ppermute | solution.py:306
  120.0 3.7 %collective-permute-done.28 = f32[512,128]{1,0:T(8,128)S(1)} collective-permute-done((f32[512,128]{1,0:T(8,128)S(1)}, f32[512,128]{1,0:T(8,128)S(1)}, u32[]{:S(2)}, u32[]{:S(2)}) %collective-permute-start.28) | collective-permute-done | bytes 262176 | tf_op jit(solution)/shard_map/ppermute | solution.py:305
  123.7 5.2 %collective-permute-done.27 = f32[512,128]{1,0:T(8,128)S(1)} collective-permute-done((f32[512,128]{1,0:T(8,128)S(1)}, f32[512,128]{1,0:T(8,128)S(1)}, u32[]{:S(2)}, u32[]{:S(2)}) %collective-permute-start.27) | collective-permute-done | bytes 262176 | tf_op jit(solution)/shard_map/ppermute | solution.py:309
  129.0 3.7 %collective-permute-done.29 = f32[512,128]{1,0:T(8,128)S(1)} collective-permute-done((f32[512,128]{1,0:T(8,128)S(1)}, f32[512,128]{1,0:T(8,128)S(1)}, u32[]{:S(2)}, u32[]{:S(2)}) %collective-permute-start.29) | collective-permute-done | bytes 262176 | tf_op jit(solution)/shard_map/ppermute | solution.py:310
  (79 shorter events, 15.2 us)
Async XLA Ops:
  1.3 18.3 %collective-permute-start.1 = (bf16[2048,128]{1,0:T(8,128)(2,1)S(1)}, bf16[2048,128]{1,0:T(8,128)(2,1)S(1)}, u32[]{:S(2)}, u32[]{:S(2)}) collective-permute-start(bf16[2048,128]{1,0:T(8,128)(2,1)S(1)} %bitcast.20), channel_id=1, source_target_pairs={{0,4},{4,0},{8,12},{12,8},{1,5},{5,1},{9,13},{13,9},{2,6},{6,2},{1... | collective-permute-start | bytes 1572872 | tf_op jit(solution)/shard_map/ppermute | solution.py:259
  1.4 18.3 %collective-permute-start = (bf16[3072,128]{1,0:T(8,128)(2,1)}, bf16[3072,128]{1,0:T(8,128)(2,1)S(1)}, u32[]{:S(2)}, u32[]{:S(2)}) collective-permute-start(bf16[3072,128]{1,0:T(8,128)(2,1)} %bitcast.5), channel_id=1, source_target_pairs={{0,8},{4,24},{8,0},{12,16},{16,12},{20,28},{24,4},{28,20},{32,40},... | collective-permute-start | bytes 2359304 | tf_op jit(solution)/shard_map/ppermute | solution.py:255
  3.6 6.2 %collective-permute-start.4 = (s32[1,128]{1,0:T(1,128)S(1)}, s32[1,128]{1,0:T(1,128)S(1)}, u32[]{:S(2)}, u32[]{:S(2)}) collective-permute-start(s32[1,128]{1,0:T(1,128)S(1)} %pad_add_fusion.5), channel_id=1, source_target_pairs={{0,96},{4,100},{8,104},{12,108},{16,112},{20,116},{24,120},{28,124... | collective-permute-start | bytes 1544 | tf_op jit(solution)/shard_map/ppermute | solution.py:240
  8.2 4.4 %collective-permute-start.3 = (s32[1,128]{1,0:T(1,128)S(1)}, s32[1,128]{1,0:T(1,128)S(1)}, u32[]{:S(2)}, u32[]{:S(2)}) collective-permute-start(s32[1,128]{1,0:T(1,128)S(1)} %pad_add_fusion.5), channel_id=1, source_target_pairs={{0,64},{4,68},{8,72},{12,76},{16,80},{20,84},{24,88},{28,92},{32,9... | collective-permute-start | bytes 1544 | tf_op jit(solution)/shard_map/ppermute | solution.py:240
  8.2 4.4 %collective-permute-start.2 = (s32[1,128]{1,0:T(1,128)S(1)}, s32[1,128]{1,0:T(1,128)S(1)}, u32[]{:S(2)}, u32[]{:S(2)}) collective-permute-start(s32[1,128]{1,0:T(1,128)S(1)} %pad_add_fusion.5), channel_id=1, source_target_pairs={{0,32},{4,36},{8,40},{12,44},{16,48},{20,52},{24,56},{28,60},{32,0... | collective-permute-start | bytes 1544 | tf_op jit(solution)/shard_map/ppermute | solution.py:240
  12.7 4.8 %collective-permute-start.7 = (s32[4,128]{1,0:T(4,128)S(1)}, s32[4,128]{1,0:T(4,128)S(1)}, u32[]{:S(2)}, u32[]{:S(2)}) collective-permute-start(s32[4,128]{1,0:T(4,128)S(1)} %pad_add_fusion.2), channel_id=1, source_target_pairs={{0,24},{4,28},{8,16},{12,20},{16,8},{20,12},{24,0},{28,4},{32,56},... | collective-permute-start | bytes 6152 | tf_op jit(solution)/shard_map/ppermute | solution.py:240
  14.5 5.1 %collective-permute-start.6 = (s32[4,128]{1,0:T(4,128)S(1)}, s32[4,128]{1,0:T(4,128)S(1)}, u32[]{:S(2)}, u32[]{:S(2)}) collective-permute-start(s32[4,128]{1,0:T(4,128)S(1)} %pad_add_fusion.2), channel_id=1, source_target_pairs={{0,16},{4,20},{8,24},{12,28},{16,0},{20,4},{24,8},{28,12},{32,48},... | collective-permute-start | bytes 6152 | tf_op jit(solution)/shard_map/ppermute | solution.py:240
  15.4 4.3 %collective-permute-start.5 = (s32[4,128]{1,0:T(4,128)S(1)}, s32[4,128]{1,0:T(4,128)S(1)}, u32[]{:S(2)}, u32[]{:S(2)}) collective-permute-start(s32[4,128]{1,0:T(4,128)S(1)} %pad_add_fusion.2), channel_id=1, source_target_pairs={{0,8},{4,12},{8,0},{12,4},{16,24},{20,28},{24,16},{28,20},{32,40},... | collective-permute-start | bytes 6152 | tf_op jit(solution)/shard_map/ppermute | solution.py:240
  19.7 26.3 %copy-start = (bf16[3072,128]{1,0:T(8,128)(2,1)}, bf16[3072,128]{1,0:T(8,128)(2,1)S(1)}, u32[]{:S(2)}) copy-start(bf16[3072,128]{1,0:T(8,128)(2,1)S(1)} %collective-permute-done.refs_2_) | copy-start | bytes 2359300
  19.8 22.9 %collective-permute-start.9 = (bf16[3072,128]{1,0:T(8,128)(2,1)S(1)}, bf16[3072,128]{1,0:T(8,128)(2,1)S(1)}, u32[]{:S(2)}, u32[]{:S(2)}) collective-permute-start(bf16[3072,128]{1,0:T(8,128)(2,1)S(1)} %collective-permute-done.refs_2_), channel_id=1, source_target_pairs={{0,224},{16,240},{32,0},{48,16},{64,32},{80,48},{96,64},{112,80},{... | collective-permute-start | bytes 2359304 | tf_op jit(solution)/shard_map/ppermute | solution.py:225
  23.0 19.7 %collective-permute-start.8 = (bf16[3072,128]{1,0:T(8,128)(2,1)S(1)}, bf16[3072,128]{1,0:T(8,128)(2,1)S(1)}, u32[]{:S(2)}, u32[]{:S(2)}) collective-permute-start(bf16[3072,128]{1,0:T(8,128)(2,1)S(1)} %collective-permute-done.refs_2_), channel_id=1, source_target_pairs={{0,32},{16,48},{32,64},{48,80},{64,96},{80,112},{96,128},{112,144}... | collective-permute-start | bytes 2359304 | tf_op jit(solution)/shard_map/ppermute | solution.py:225
  23.1 23.0 %collective-permute-start.17 = (bf16[3072,128]{1,0:T(8,128)(2,1)S(1)}, bf16[3072,128]{1,0:T(8,128)(2,1)S(1)}, u32[]{:S(2)}, u32[]{:S(2)}) collective-permute-start(bf16[3072,128]{1,0:T(8,128)(2,1)S(1)} %get-tuple-element.51), channel_id=1, source_target_pairs={{0,24},{4,28},{8,16},{12,20},{16,8},{20,12},{24,0},{28,4},{32,56},... | collective-permute-start | bytes 2359304 | tf_op jit(solution)/shard_map/ppermute | solution.py:233
  24.6 1.2 collective-permute-start.10
  24.6 22.9 %collective-permute-start.16 = (bf16[3072,128]{1,0:T(8,128)(2,1)S(1)}, bf16[3072,128]{1,0:T(8,128)(2,1)S(1)}, u32[]{:S(2)}, u32[]{:S(2)}) collective-permute-start(bf16[3072,128]{1,0:T(8,128)(2,1)S(1)} %get-tuple-element.52), channel_id=1, source_target_pairs={{0,8},{4,12},{8,0},{12,4},{1,9},{5,13},{9,1},{13,5},{2,10},{6,14},... | collective-permute-start | bytes 2359304 | tf_op jit(solution)/shard_map/ppermute | solution.py:229
  25.8 16.8 %collective-permute-start.11 = (s32[32,128]{1,0:T(8,128)S(1)}, s32[32,128]{1,0:T(8,128)S(1)}, u32[]{:S(2)}, u32[]{:S(2)}) collective-permute-start(s32[32,128]{1,0:T(8,128)S(1)} %pad_add_fusion.1), channel_id=1, source_target_pairs={{0,128},{4,132},{8,136},{12,140},{16,144},{20,148},{24,152},{28,15... | collective-permute-start | bytes 49160 | tf_op jit(solution)/shard_map/ppermute | solution.py:245
  42.6 5.0 %copy-start.2 = (bf16[3072,128]{1,0:T(8,128)(2,1)}, bf16[3072,128]{1,0:T(8,128)(2,1)S(1)}, u32[]{:S(2)}) copy-start(bf16[3072,128]{1,0:T(8,128)(2,1)S(1)} %collective-permute-done.9.refs_4_) | copy-start | bytes 2359300
  42.7 17.6 %collective-permute-start.12 = (bf16[3072,128]{1,0:T(8,128)(2,1)S(1)}, bf16[3072,128]{1,0:T(8,128)(2,1)}, u32[]{:S(2)}, u32[]{:S(2)}) collective-permute-start(bf16[3072,128]{1,0:T(8,128)(2,1)S(1)} %collective-permute-done.8.refs_3_), channel_id=1, source_target_pairs={{0,32},{16,48},{32,64},{48,80},{64,96},{80,112},{96,128},{112,144}... | collective-permute-start | bytes 2359304 | tf_op jit(solution)/shard_map/ppermute | solution.py:225
  42.7 17.5 %collective-permute-start.13 = (bf16[3072,128]{1,0:T(8,128)(2,1)S(1)}, bf16[3072,128]{1,0:T(8,128)(2,1)}, u32[]{:S(2)}, u32[]{:S(2)}) collective-permute-start(bf16[3072,128]{1,0:T(8,128)(2,1)S(1)} %collective-permute-done.9.refs_4_), channel_id=1, source_target_pairs={{0,224},{16,240},{32,0},{48,16},{64,32},{80,48},{96,64},{112,80},{... | collective-permute-start | bytes 2359304 | tf_op jit(solution)/shard_map/ppermute | solution.py:225
  47.0 16.6 %collective-permute-start.18 = (bf16[3072,128]{1,0:T(8,128)(2,1)}, bf16[3072,128]{1,0:T(8,128)(2,1)S(1)}, u32[]{:S(2)}, u32[]{:S(2)}) collective-permute-start(bf16[3072,128]{1,0:T(8,128)(2,1)} %pad_maximum_fusion.1), channel_id=1, source_target_pairs={{0,8},{4,12},{8,0},{12,4},{1,9},{5,13},{9,1},{13,5},{2,10},{6,14},... | collective-permute-start | bytes 2359304 | tf_op jit(solution)/shard_map/ppermute | solution.py:229
  48.6 17.7 %collective-permute-start.19 = (bf16[3072,128]{1,0:T(8,128)(2,1)}, bf16[3072,128]{1,0:T(8,128)(2,1)}, u32[]{:S(2)}, u32[]{:S(2)}) collective-permute-start(bf16[3072,128]{1,0:T(8,128)(2,1)} %pad_maximum_fusion.2), channel_id=1, source_target_pairs={{0,24},{4,28},{8,16},{12,20},{16,8},{20,12},{24,0},{28,4},{32,56},... | collective-permute-start | bytes 2359304 | tf_op jit(solution)/shard_map/ppermute | solution.py:233
  60.2 17.9 %collective-permute-start.14 = (bf16[3072,128]{1,0:T(8,128)(2,1)}, bf16[3072,128]{1,0:T(8,128)(2,1)}, u32[]{:S(2)}, u32[]{:S(2)}) collective-permute-start(bf16[3072,128]{1,0:T(8,128)(2,1)} %collective-permute-done.12.refs_2_), channel_id=1, source_target_pairs={{0,32},{16,48},{32,64},{48,80},{64,96},{80,112},{96,128},{112,144}... | collective-permute-start | bytes 2359304 | tf_op jit(solution)/shard_map/ppermute | solution.py:225
  60.2 17.9 %collective-permute-start.15 = (bf16[3072,128]{1,0:T(8,128)(2,1)}, bf16[3072,128]{1,0:T(8,128)(2,1)}, u32[]{:S(2)}, u32[]{:S(2)}) collective-permute-start(bf16[3072,128]{1,0:T(8,128)(2,1)} %collective-permute-done.13.refs_3_), channel_id=1, source_target_pairs={{0,224},{16,240},{32,0},{48,16},{64,32},{80,48},{96,64},{112,80},{... | collective-permute-start | bytes 2359304 | tf_op jit(solution)/shard_map/ppermute | solution.py:225
  80.2 13.0 %collective-permute-start.20 = (bf16[1536,128]{1,0:T(8,128)(2,1)S(1)}, bf16[1536,128]{1,0:T(8,128)(2,1)S(1)}, u32[]{:S(2)}, u32[]{:S(2)}) collective-permute-start(bf16[1536,128]{1,0:T(8,128)(2,1)S(1)} %slice.78), channel_id=1, source_target_pairs={{0,32},{16,48},{32,64},{48,80},{64,96},{80,112},{96,128},{112,144}... | collective-permute-start | bytes 1179656 | tf_op jit(solution)/shard_map/ppermute | solution.py:291
  80.3 12.9 %collective-permute-start.21 = (bf16[1536,128]{1,0:T(8,128)(2,1)S(1)}, bf16[1536,128]{1,0:T(8,128)(2,1)S(1)}, u32[]{:S(2)}, u32[]{:S(2)}) collective-permute-start(bf16[1536,128]{1,0:T(8,128)(2,1)S(1)} %slice.79), channel_id=1, source_target_pairs={{0,224},{16,240},{32,0},{48,16},{64,32},{80,48},{96,64},{112,80},{... | collective-permute-start | bytes 1179656 | tf_op jit(solution)/shard_map/ppermute | solution.py:291
  97.2 4.2 %collective-permute-start.22 = (f32[4096,128]{1,0:T(8,128)S(1)}, f32[4096,128]{1,0:T(8,128)S(1)}, u32[]{:S(2)}, u32[]{:S(2)}) collective-permute-start(f32[4096,128]{1,0:T(8,128)S(1)} %get-tuple-element.36), channel_id=1, source_target_pairs={{0,4},{4,0},{8,12},{12,8},{1,5},{5,1},{9,13},{13,9},{2,6},{6,2},{1... | collective-permute-start | bytes 6291464 | tf_op jit(solution)/shard_map/ppermute | solution.py:295
  101.6 8.4 %collective-permute-start.25 = (f32[512,128]{1,0:T(8,128)S(1)}, f32[512,128]{1,0:T(8,128)S(1)}, u32[]{:S(2)}, u32[]{:S(2)}) collective-permute-start(f32[512,128]{1,0:T(8,128)S(1)} %get-tuple-element.38), channel_id=1, source_target_pairs={{0,1},{1,2},{2,3},{3,0},{4,5},{5,6},{6,7},{7,4},{8,9},{9,10},{10,1... | collective-permute-start | bytes 786440 | tf_op jit(solution)/shard_map/ppermute | solution.py:303
  103.6 8.1 %collective-permute-start.26 = (f32[512,128]{1,0:T(8,128)S(1)}, f32[512,128]{1,0:T(8,128)S(1)}, u32[]{:S(2)}, u32[]{:S(2)}) collective-permute-start(f32[512,128]{1,0:T(8,128)S(1)} %get-tuple-element.39), channel_id=1, source_target_pairs={{0,3},{1,0},{2,1},{3,2},{4,7},{5,4},{6,5},{7,6},{8,11},{9,8},{10,9... | collective-permute-start | bytes 786440 | tf_op jit(solution)/shard_map/ppermute | solution.py:304
  103.8 20.0 %collective-permute-start.23 = (f32[1024,128]{1,0:T(8,128)S(1)}, f32[1024,128]{1,0:T(8,128)S(1)}, u32[]{:S(2)}, u32[]{:S(2)}) collective-permute-start(f32[1024,128]{1,0:T(8,128)S(1)} %slice_add_fusion), channel_id=1, source_target_pairs={{0,8},{4,24},{8,0},{12,16},{16,12},{20,28},{24,4},{28,20},{32,40},... | collective-permute-start | bytes 1572872 | tf_op jit(solution)/shard_map/ppermute | solution.py:307
  106.1 14.0 %collective-permute-start.24 = (f32[512,128]{1,0:T(8,128)S(1)}, f32[512,128]{1,0:T(8,128)S(1)}, u32[]{:S(2)}, u32[]{:S(2)}) collective-permute-start(f32[512,128]{1,0:T(8,128)S(1)} %get-tuple-element.37), channel_id=1, source_target_pairs={{0,11},{1,8},{2,9},{3,10},{4,27},{5,24},{6,25},{7,26},{8,3},{9,0},... | collective-permute-start | bytes 786440 | tf_op jit(solution)/shard_map/ppermute | solution.py:306
  106.8 16.9 %collective-permute-start.28 = (f32[512,128]{1,0:T(8,128)S(1)}, f32[512,128]{1,0:T(8,128)S(1)}, u32[]{:S(2)}, u32[]{:S(2)}) collective-permute-start(f32[512,128]{1,0:T(8,128)S(1)} %get-tuple-element.41), channel_id=1, source_target_pairs={{0,9},{1,10},{2,11},{3,8},{4,25},{5,26},{6,27},{7,24},{8,1},{9,2},... | collective-permute-start | bytes 786440 | tf_op jit(solution)/shard_map/ppermute | solution.py:305
  111.8 17.2 %collective-permute-start.27 = (f32[512,128]{1,0:T(8,128)S(1)}, f32[512,128]{1,0:T(8,128)S(1)}, u32[]{:S(2)}, u32[]{:S(2)}) collective-permute-start(f32[512,128]{1,0:T(8,128)S(1)} %get-tuple-element.43), channel_id=1, source_target_pairs={{0,9},{1,10},{2,11},{3,8},{4,25},{5,26},{6,27},{7,24},{8,1},{9,2},... | collective-permute-start | bytes 786440 | tf_op jit(solution)/shard_map/ppermute | solution.py:309
  114.0 18.7 %collective-permute-start.29 = (f32[512,128]{1,0:T(8,128)S(1)}, f32[512,128]{1,0:T(8,128)S(1)}, u32[]{:S(2)}, u32[]{:S(2)}) collective-permute-start(f32[512,128]{1,0:T(8,128)S(1)} %get-tuple-element.44), channel_id=1, source_target_pairs={{0,11},{1,8},{2,9},{3,10},{4,27},{5,24},{6,25},{7,26},{8,3},{9,0},... | collective-permute-start | bytes 786440 | tf_op jit(solution)/shard_map/ppermute | solution.py:310
  (8 other events, 21.1 us)

commit v6 on v5

--- a/solution.py
+++ b/solution.py
@@ -41,6 +41,10 @@
 
 def z_route(d):
     return [(2 * z + h, 2 * ((z + d) % NZ) + h) for z in range(NZ) for h in range(2)]
+
+
+def far_route():
+    return [(gid(z, h, l, c), gid((z + 1 - 2 * c) % NZ, h, l, c)) for z, h, l, c in group()]
 
 
 def y_route(d):
@@ -282,15 +286,13 @@
 
     f3, b3 = onward(f2, b2)
     rights = [right, in1, in2, out1, out2]
-    near = LEFT_ROWS // 2
     one = ((0, LEFT_ROWS),)
-    two = ((0, near), (0, LEFT_ROWS - near))
     whole = ((0, 64),)
     (total,) = multiply((0, -1, 1), one, ATILES, ids, meta, [own, f1, b1], rights, None, whole)
     f3, b3, total = barrier((f3, b3, total))
-    far = [send(f3[:near], "row", z_route(1)), send(b3[near:], "row", z_route(-1))]
+    far = [send(jnp.where(core == 0, f3, b3), BOTH, far_route())]
     (total,) = multiply((-2, 2, -3, 3), one, ATILES, ids, meta, [f2, b2, f3, b3], rights, total, whole)
-    kept, other = multiply((4,), two, ATILES, ids, meta, far, rights, total, ((0, 32), (32, 32)))
+    kept, other = multiply((4,), one, ATILES, ids, meta, far, rights, total, ((0, 32), (32, 32)))
 
     other = send(other, "col", CORE_ROUTE)
     half = 4 * TILE

time: 136 us -> 133 us (0.978)
  starting transfers between devices: 41.8 us -> 39.1 us
  waiting for transfers between devices: 58.5 us -> 61.1 us
  local copies, waits for them, and re-layouts: 7.46 us -> 5.42 us
    ppermute x1, waiting for transfers between devices: 3.71 us -> 9.06 us  [shards(): up1 = send(units[2], ALL, home_route(1))]
    ppermute x1, starting transfers between devices: 0.74 us -> 4.37 us  [shards(): down1 = send(units[3], ALL, home_route(-1))]
    ppermute x2 -> x1, waiting for transfers between devices: 0.01 us -> 2.89 us  [shards(): far = [send(jnp.where(core == 0, f3, b3), BOTH, far_route())]]
    ppermute x2 -> x1, starting transfers between devices: 3.31 us -> 0.77 us  [shards(): far = [send(jnp.where(core == 0, f3, b3), BOTH, far_route())]]
    ppermute x1, waiting for transfers between devices: 3.66 us -> 1.16 us  [shards(): down3 = send(unit(5) + down2, ALL, home_route(-1))]
    ppermute x1, starting transfers between devices: 2.19 us -> 0.01 us  [shards(): up1 = send(units[2], ALL, home_route(1))]
    slice x2 -> x0, local copies, waits for them, and re-layouts: 2.05 us -> none  [the longest x1 1.02 us: shards(): b3[near:]]
    ppermute x1, starting transfers between devices: 2.29 us -> 0.33 us  [shards(): still = send(unit(0, 2), BOTH, swap_route())]
  transfers between devices with their start and end apart: 30 -> 29, of which waited for: 15 -> 16; matrix products, arithmetic and copies ran while one was open for 2% -> 2% of each run, Pallas kernels for 13% -> 13%
where the time goes in v6:
time: 133 us; the launch traced here: 132 us
  waiting for transfers between devices  61.1 us (46%)
  starting transfers between devices  39.1 us (29%)
  Pallas kernels  21.3 us (16%)
  local copies, waits for them, and re-layouts  5.42 us (4%)
  other arithmetic  4.66 us (4%)
    pallas_call x3, Pallas kernels, multiply(): pl.pallas_call(functools.partial(kernel, deltas, parts, tiles, first, out...  21.3 us
    ppermute x2, waiting for transfers between devices, spread(): send(meta, BOTH, [(i, i ^ 1 << bit) for i in range(64)])  14.1 us
    ppermute x6, waiting for transfers between devices, onward(): return (send(f, 'row', z_route(1)), send(b, 'row', z_route(-1)))  10.4 us
    ppermute x6, starting transfers between devices, onward(): return (send(f, 'row', z_route(1)), send(b, 'row', z_route(-1)))  9.75 us
    ppermute x6, starting transfers between devices, spread_two(): send(meta, BOTH, [(i, i ^ k << low) for i in range(64)])  9.43 us
    ppermute x1, waiting for transfers between devices, shards(): up1 = send(units[2], ALL, home_route(1))  9.06 us
    ppermute x6, waiting for transfers between devices, spread_two(): send(meta, BOTH, [(i, i ^ k << low) for i in range(64)])  6.53 us
    ppermute x1, starting transfers between devices, shards(): down1 = send(units[3], ALL, home_route(-1))  4.37 us
  transfers between devices with their start and end apart: 29, of which 16 were waited for; matrix products, arithmetic and copies ran while one was open for 2% of the time, Pallas kernels for 13%

profile of v6, /device:TPU:8, one launch (start us, length us, event | category | flops | bytes accessed | tf_op | source)
XLA Modules:
  0.0 131.8 jit_solution(16933649219194189744)
XLA Ops:
  0.0 1.3 constant_dynamic-slice_fusion.1
  1.4 1.6 %collective-permute-start = (bf16[3072,128]{1,0:T(8,128)(2,1)}, bf16[3072,128]{1,0:T(8,128)(2,1)S(1)}, u32[]{:S(2)}, u32[]{:S(2)}) collective-permute-start(bf16[3072,128]{1,0:T(8,128)(2,1)} %bitcast.5), channel_id=1, source_target_pairs={{0,8},{4,24},{8,0},{12,16},{16,12},{20,28},{24,4},{28,20},{32,40},... | collective-permute-start | bytes 2359304 | tf_op jit(solution)/shard_map/ppermute | solution.py:259
  3.6 4.7 %collective-permute-start.4 = (s32[1,128]{1,0:T(1,128)S(1)}, s32[1,128]{1,0:T(1,128)S(1)}, u32[]{:S(2)}, u32[]{:S(2)}) collective-permute-start(s32[1,128]{1,0:T(1,128)S(1)} %pad_add_fusion.5), channel_id=1, source_target_pairs={{0,96},{4,100},{8,104},{12,108},{16,112},{20,116},{24,120},{28,124... | collective-permute-start | bytes 1544 | tf_op jit(solution)/shard_map/ppermute | solution.py:244
  9.7 2.9 %collective-permute-done.3 = s32[1,128]{1,0:T(1,128)S(1)} collective-permute-done((s32[1,128]{1,0:T(1,128)S(1)}, s32[1,128]{1,0:T(1,128)S(1)}, u32[]{:S(2)}, u32[]{:S(2)}) %collective-permute-start.3) | collective-permute-done | bytes 544 | tf_op jit(solution)/shard_map/ppermute | solution.py:244
  12.7 1.8 %collective-permute-start.7 = (s32[4,128]{1,0:T(4,128)S(1)}, s32[4,128]{1,0:T(4,128)S(1)}, u32[]{:S(2)}, u32[]{:S(2)}) collective-permute-start(s32[4,128]{1,0:T(4,128)S(1)} %pad_add_fusion.2), channel_id=1, source_target_pairs={{0,24},{4,28},{8,16},{12,20},{16,8},{20,12},{24,0},{28,4},{32,56},... | collective-permute-start | bytes 6152 | tf_op jit(solution)/shard_map/ppermute | solution.py:244
  15.4 1.5 %collective-permute-start.5 = (s32[4,128]{1,0:T(4,128)S(1)}, s32[4,128]{1,0:T(4,128)S(1)}, u32[]{:S(2)}, u32[]{:S(2)}) collective-permute-start(s32[4,128]{1,0:T(4,128)S(1)} %pad_add_fusion.2), channel_id=1, source_target_pairs={{0,8},{4,12},{8,0},{12,4},{16,24},{20,28},{24,16},{28,20},{32,40},... | collective-permute-start | bytes 6152 | tf_op jit(solution)/shard_map/ppermute | solution.py:244
  17.6 2.1 %collective-permute-done.6 = s32[4,128]{1,0:T(4,128)S(1)} collective-permute-done((s32[4,128]{1,0:T(4,128)S(1)}, s32[4,128]{1,0:T(4,128)S(1)}, u32[]{:S(2)}, u32[]{:S(2)}) %collective-permute-start.6) | collective-permute-done | bytes 2080 | tf_op jit(solution)/shard_map/ppermute | solution.py:244
  19.8 3.2 %collective-permute-start.9 = (bf16[3072,128]{1,0:T(8,128)(2,1)S(1)}, bf16[3072,128]{1,0:T(8,128)(2,1)S(1)}, u32[]{:S(2)}, u32[]{:S(2)}) collective-permute-start(bf16[3072,128]{1,0:T(8,128)(2,1)S(1)} %collective-permute-done.refs_2_), channel_id=1, source_target_pairs={{0,224},{16,240},{32,0},{48,16},{64,32},{80,48},{96,64},{112,80},{... | collective-permute-start | bytes 2359304 | tf_op jit(solution)/shard_map/ppermute | solution.py:229
  23.1 1.6 %collective-permute-start.17 = (bf16[3072,128]{1,0:T(8,128)(2,1)S(1)}, bf16[3072,128]{1,0:T(8,128)(2,1)S(1)}, u32[]{:S(2)}, u32[]{:S(2)}) collective-permute-start(bf16[3072,128]{1,0:T(8,128)(2,1)S(1)} %get-tuple-element.51), channel_id=1, source_target_pairs={{0,24},{4,28},{8,16},{12,20},{16,8},{20,12},{24,0},{28,4},{32,56},... | collective-permute-start | bytes 2359304 | tf_op jit(solution)/shard_map/ppermute | solution.py:237
  25.8 3.4 %collective-permute-start.11 = (s32[32,128]{1,0:T(8,128)S(1)}, s32[32,128]{1,0:T(8,128)S(1)}, u32[]{:S(2)}, u32[]{:S(2)}) collective-permute-start(s32[32,128]{1,0:T(8,128)S(1)} %pad_add_fusion.1), channel_id=1, source_target_pairs={{0,128},{4,132},{8,136},{12,140},{16,144},{20,148},{24,152},{28,15... | collective-permute-start | bytes 49160 | tf_op jit(solution)/shard_map/ppermute | solution.py:249
  29.2 13.4 %collective-permute-done.11 = s32[32,128]{1,0:T(8,128)S(1)} collective-permute-done((s32[32,128]{1,0:T(8,128)S(1)}, s32[32,128]{1,0:T(8,128)S(1)}, u32[]{:S(2)}, u32[]{:S(2)}) %collective-permute-start.11) | collective-permute-done | bytes 16416 | tf_op jit(solution)/shard_map/ppermute | solution.py:249
  42.7 3.2 %collective-permute-start.13 = (bf16[3072,128]{1,0:T(8,128)(2,1)S(1)}, bf16[3072,128]{1,0:T(8,128)(2,1)}, u32[]{:S(2)}, u32[]{:S(2)}) collective-permute-start(bf16[3072,128]{1,0:T(8,128)(2,1)S(1)} %collective-permute-done.9.refs_4_), channel_id=1, source_target_pairs={{0,224},{16,240},{32,0},{48,16},{64,32},{80,48},{96,64},{112,80},{... | collective-permute-start | bytes 2359304 | tf_op jit(solution)/shard_map/ppermute | solution.py:229
  48.6 1.2 collective-permute-start.19
  49.8 10.4 %collective-permute-done.12.refs_2_ = bf16[3072,128]{1,0:T(8,128)(2,1)} collective-permute-done((bf16[3072,128]{1,0:T(8,128)(2,1)S(1)}, bf16[3072,128]{1,0:T(8,128)(2,1)}, u32[]{:S(2)}, u32[]{:S(2)}) %collective-permute-start.12) | collective-permute-done | bytes 786464 | tf_op jit(solution)/shard_map/ppermute | solution.py:229
  60.2 3.2 %collective-permute-start.15 = (bf16[3072,128]{1,0:T(8,128)(2,1)}, bf16[3072,128]{1,0:T(8,128)(2,1)}, u32[]{:S(2)}, u32[]{:S(2)}) collective-permute-start(bf16[3072,128]{1,0:T(8,128)(2,1)} %collective-permute-done.13.refs_3_), channel_id=1, source_target_pairs={{0,224},{16,240},{32,0},{48,16},{64,32},{80,48},{96,64},{112,80},{... | collective-permute-start | bytes 2359304 | tf_op jit(solution)/shard_map/ppermute | solution.py:229
  63.6 2.8 %collective-permute-done.19.refs_9_.refs_10_.refs_7_ = bf16[3072,128]{1,0:T(8,128)(2,1)} collective-permute-done((bf16[3072,128]{1,0:T(8,128)(2,1)}, bf16[3072,128]{1,0:T(8,128)(2,1)}, u32[]{:S(2)}, u32[]{:S(2)}) %collective-permute-start.19) | collective-permute-done | bytes 786464 | tf_op jit(solution)/shard_map/ppermute | solution.py:237
  69.7 7.6 %products_0_7_1.1.refs_11_ = f32[8192,128]{1,0:T(8,128)S(1)} custom-call(s32[8]{0:T(128)S(1)} %stack.26.refs_0_, s32[64,128]{1,0:T(8,128)S(1)} %pad_add_fusion.refs_1_, bf16[3072,128]{1,0:T(8,128)(2,1)S(1)} %copy-done.1, bf16[3072,128]{1,0:T(8,128)(2,1)S(1)} %copy-done.5, bf16[3072,128]{1,0:T(8,128)(2,1)S(1)} %copy-done.3, ...), custom_call_target="tpu_custom_call" | custom-call | flops 120000000 | bytes 20000000 | tf_op jit(solution)/shard_map/products_0_7_1/pallas_call | solution.py:204
  77.4 1.2 broadcast_select_fusion
  79.4 10.0 %products_6_2_5_3.1.refs_8_ = f32[8192,128]{1,0:T(8,128)S(1)} custom-call(s32[8]{0:T(128)S(1)} %stack.26.refs_0_, s32[64,128]{1,0:T(8,128)S(1)} %pad_add_fusion.refs_1_, bf16[3072,128]{1,0:T(8,128)(2,1)} %collective-permute-done.12.refs_2_, bf16[3072,128]{1,0:T(8,128)(2,1)} %collective-permute-done.13.refs_3_, ...), custom_call_target="tpu_custom_call" | custom-call | flops 160000000 | bytes 24000000 | tf_op jit(solution)/shard_map/products_6_2_5_3/pallas_call | solution.py:204
  89.4 2.9 %collective-permute-done.20.refs_2_ = bf16[3072,128]{1,0:T(8,128)(2,1)S(1)} collective-permute-done((bf16[3072,128]{1,0:T(8,128)(2,1)S(1)}, bf16[3072,128]{1,0:T(8,128)(2,1)S(1)}, u32[]{:S(2)}, u32[]{:S(2)}) %collective-permute-start.20) | collective-permute-done | bytes 786464 | tf_op jit(solution)/shard_map/ppermute | solution.py:293
  92.3 3.7 %products_4.1 = (f32[4096,128]{1,0:T(8,128)S(1)}, f32[4096,128]{1,0:T(8,128)S(1)}) custom-call(s32[8]{0:T(128)S(1)} %stack.26.refs_0_, s32[64,128]{1,0:T(8,128)S(1)} %pad_add_fusion.refs_1_, bf16[3072,128]{1,0:T(8,128)(2,1)S(1)} %collective-permute-done.20.refs_2_, bf16[4096,128]{1,0:T(8,128)(2,1)S(1)} %pad_maximum_fusion.refs_5_.refs_6_.refs_3_, ...), custom_call_target="tpu_custom_call" | custom-call | flops 40000000 | bytes 12000000 | tf_op jit(solution)/shard_map/products_4/pallas_call | solution.py:204
  96.1 4.1 %collective-permute-done.21 = f32[4096,128]{1,0:T(8,128)S(1)} collective-permute-done((f32[4096,128]{1,0:T(8,128)S(1)}, f32[4096,128]{1,0:T(8,128)S(1)}, u32[]{:S(2)}, u32[]{:S(2)}) %collective-permute-start.21) | collective-permute-done | bytes 2097184 | tf_op jit(solution)/shard_map/ppermute | solution.py:297
  100.4 1.3 collective-permute-start.24
  101.7 1.2 collective-permute-start.25
  103.2 4.4 %collective-permute-start.23 = (f32[512,128]{1,0:T(8,128)S(1)}, f32[512,128]{1,0:T(8,128)S(1)}, u32[]{:S(2)}, u32[]{:S(2)}) collective-permute-start(f32[512,128]{1,0:T(8,128)S(1)} %get-tuple-element.37), channel_id=1, source_target_pairs={{0,11},{1,8},{2,9},{3,10},{4,27},{5,24},{6,25},{7,26},{8,3},{9,0},... | collective-permute-start | bytes 786440 | tf_op jit(solution)/shard_map/ppermute | solution.py:308
  107.6 1.8 %collective-permute-done.24 = f32[512,128]{1,0:T(8,128)S(1)} collective-permute-done((f32[512,128]{1,0:T(8,128)S(1)}, f32[512,128]{1,0:T(8,128)S(1)}, u32[]{:S(2)}, u32[]{:S(2)}) %collective-permute-start.24) | collective-permute-done | bytes 262176 | tf_op jit(solution)/shard_map/ppermute | solution.py:305
  110.1 1.3 collective-permute-start.26
  111.4 1.7 %collective-permute-start.28 = (f32[512,128]{1,0:T(8,128)S(1)}, f32[512,128]{1,0:T(8,128)S(1)}, u32[]{:S(2)}, u32[]{:S(2)}) collective-permute-start(f32[512,128]{1,0:T(8,128)S(1)} %get-tuple-element.44), channel_id=1, source_target_pairs={{0,11},{1,8},{2,9},{3,10},{4,27},{5,24},{6,25},{7,26},{8,3},{9,0},... | collective-permute-start | bytes 786440 | tf_op jit(solution)/shard_map/ppermute | solution.py:312
  113.1 4.0 %collective-permute-done.23 = f32[512,128]{1,0:T(8,128)S(1)} collective-permute-done((f32[512,128]{1,0:T(8,128)S(1)}, f32[512,128]{1,0:T(8,128)S(1)}, u32[]{:S(2)}, u32[]{:S(2)}) %collective-permute-start.23) | collective-permute-done | bytes 262176 | tf_op jit(solution)/shard_map/ppermute | solution.py:308
  117.1 9.1 %collective-permute-done.27 = f32[512,128]{1,0:T(8,128)S(1)} collective-permute-done((f32[512,128]{1,0:T(8,128)S(1)}, f32[512,128]{1,0:T(8,128)S(1)}, u32[]{:S(2)}, u32[]{:S(2)}) %collective-permute-start.27) | collective-permute-done | bytes 262176 | tf_op jit(solution)/shard_map/ppermute | solution.py:307
  126.1 3.6 %collective-permute-done.26 = f32[512,128]{1,0:T(8,128)S(1)} collective-permute-done((f32[512,128]{1,0:T(8,128)S(1)}, f32[512,128]{1,0:T(8,128)S(1)}, u32[]{:S(2)}, u32[]{:S(2)}) %collective-permute-start.26) | collective-permute-done | bytes 262176 | tf_op jit(solution)/shard_map/ppermute | solution.py:311
  129.8 1.2 collective-permute-done.28
  (76 shorter events, 14.4 us)
Async XLA Ops:
  1.3 18.3 %collective-permute-start.1 = (bf16[2048,128]{1,0:T(8,128)(2,1)S(1)}, bf16[2048,128]{1,0:T(8,128)(2,1)S(1)}, u32[]{:S(2)}, u32[]{:S(2)}) collective-permute-start(bf16[2048,128]{1,0:T(8,128)(2,1)S(1)} %bitcast.20), channel_id=1, source_target_pairs={{0,4},{4,0},{8,12},{12,8},{1,5},{5,1},{9,13},{13,9},{2,6},{6,2},{1... | collective-permute-start | bytes 1572872 | tf_op jit(solution)/shard_map/ppermute | solution.py:263
  1.4 18.3 %collective-permute-start = (bf16[3072,128]{1,0:T(8,128)(2,1)}, bf16[3072,128]{1,0:T(8,128)(2,1)S(1)}, u32[]{:S(2)}, u32[]{:S(2)}) collective-permute-start(bf16[3072,128]{1,0:T(8,128)(2,1)} %bitcast.5), channel_id=1, source_target_pairs={{0,8},{4,24},{8,0},{12,16},{16,12},{20,28},{24,4},{28,20},{32,40},... | collective-permute-start | bytes 2359304 | tf_op jit(solution)/shard_map/ppermute | solution.py:259
  3.6 6.2 %collective-permute-start.4 = (s32[1,128]{1,0:T(1,128)S(1)}, s32[1,128]{1,0:T(1,128)S(1)}, u32[]{:S(2)}, u32[]{:S(2)}) collective-permute-start(s32[1,128]{1,0:T(1,128)S(1)} %pad_add_fusion.5), channel_id=1, source_target_pairs={{0,96},{4,100},{8,104},{12,108},{16,112},{20,116},{24,120},{28,124... | collective-permute-start | bytes 1544 | tf_op jit(solution)/shard_map/ppermute | solution.py:244
  8.2 4.4 %collective-permute-start.3 = (s32[1,128]{1,0:T(1,128)S(1)}, s32[1,128]{1,0:T(1,128)S(1)}, u32[]{:S(2)}, u32[]{:S(2)}) collective-permute-start(s32[1,128]{1,0:T(1,128)S(1)} %pad_add_fusion.5), channel_id=1, source_target_pairs={{0,64},{4,68},{8,72},{12,76},{16,80},{20,84},{24,88},{28,92},{32,9... | collective-permute-start | bytes 1544 | tf_op jit(solution)/shard_map/ppermute | solution.py:244
  8.2 4.4 %collective-permute-start.2 = (s32[1,128]{1,0:T(1,128)S(1)}, s32[1,128]{1,0:T(1,128)S(1)}, u32[]{:S(2)}, u32[]{:S(2)}) collective-permute-start(s32[1,128]{1,0:T(1,128)S(1)} %pad_add_fusion.5), channel_id=1, source_target_pairs={{0,32},{4,36},{8,40},{12,44},{16,48},{20,52},{24,56},{28,60},{32,0... | collective-permute-start | bytes 1544 | tf_op jit(solution)/shard_map/ppermute | solution.py:244
  12.7 4.8 %collective-permute-start.7 = (s32[4,128]{1,0:T(4,128)S(1)}, s32[4,128]{1,0:T(4,128)S(1)}, u32[]{:S(2)}, u32[]{:S(2)}) collective-permute-start(s32[4,128]{1,0:T(4,128)S(1)} %pad_add_fusion.2), channel_id=1, source_target_pairs={{0,24},{4,28},{8,16},{12,20},{16,8},{20,12},{24,0},{28,4},{32,56},... | collective-permute-start | bytes 6152 | tf_op jit(solution)/shard_map/ppermute | solution.py:244
  14.5 5.1 %collective-permute-start.6 = (s32[4,128]{1,0:T(4,128)S(1)}, s32[4,128]{1,0:T(4,128)S(1)}, u32[]{:S(2)}, u32[]{:S(2)}) collective-permute-start(s32[4,128]{1,0:T(4,128)S(1)} %pad_add_fusion.2), channel_id=1, source_target_pairs={{0,16},{4,20},{8,24},{12,28},{16,0},{20,4},{24,8},{28,12},{32,48},... | collective-permute-start | bytes 6152 | tf_op jit(solution)/shard_map/ppermute | solution.py:244
  15.4 4.3 %collective-permute-start.5 = (s32[4,128]{1,0:T(4,128)S(1)}, s32[4,128]{1,0:T(4,128)S(1)}, u32[]{:S(2)}, u32[]{:S(2)}) collective-permute-start(s32[4,128]{1,0:T(4,128)S(1)} %pad_add_fusion.2), channel_id=1, source_target_pairs={{0,8},{4,12},{8,0},{12,4},{16,24},{20,28},{24,16},{28,20},{32,40},... | collective-permute-start | bytes 6152 | tf_op jit(solution)/shard_map/ppermute | solution.py:244
  19.7 26.3 %copy-start = (bf16[3072,128]{1,0:T(8,128)(2,1)}, bf16[3072,128]{1,0:T(8,128)(2,1)S(1)}, u32[]{:S(2)}) copy-start(bf16[3072,128]{1,0:T(8,128)(2,1)S(1)} %collective-permute-done.refs_2_) | copy-start | bytes 2359300
  19.8 22.9 %collective-permute-start.9 = (bf16[3072,128]{1,0:T(8,128)(2,1)S(1)}, bf16[3072,128]{1,0:T(8,128)(2,1)S(1)}, u32[]{:S(2)}, u32[]{:S(2)}) collective-permute-start(bf16[3072,128]{1,0:T(8,128)(2,1)S(1)} %collective-permute-done.refs_2_), channel_id=1, source_target_pairs={{0,224},{16,240},{32,0},{48,16},{64,32},{80,48},{96,64},{112,80},{... | collective-permute-start | bytes 2359304 | tf_op jit(solution)/shard_map/ppermute | solution.py:229
  23.0 19.7 %collective-permute-start.8 = (bf16[3072,128]{1,0:T(8,128)(2,1)S(1)}, bf16[3072,128]{1,0:T(8,128)(2,1)S(1)}, u32[]{:S(2)}, u32[]{:S(2)}) collective-permute-start(bf16[3072,128]{1,0:T(8,128)(2,1)S(1)} %collective-permute-done.refs_2_), channel_id=1, source_target_pairs={{0,32},{16,48},{32,64},{48,80},{64,96},{80,112},{96,128},{112,144}... | collective-permute-start | bytes 2359304 | tf_op jit(solution)/shard_map/ppermute | solution.py:229
  23.1 23.0 %collective-permute-start.17 = (bf16[3072,128]{1,0:T(8,128)(2,1)S(1)}, bf16[3072,128]{1,0:T(8,128)(2,1)S(1)}, u32[]{:S(2)}, u32[]{:S(2)}) collective-permute-start(bf16[3072,128]{1,0:T(8,128)(2,1)S(1)} %get-tuple-element.51), channel_id=1, source_target_pairs={{0,24},{4,28},{8,16},{12,20},{16,8},{20,12},{24,0},{28,4},{32,56},... | collective-permute-start | bytes 2359304 | tf_op jit(solution)/shard_map/ppermute | solution.py:237
  24.6 1.2 collective-permute-start.10
  24.6 23.0 %collective-permute-start.16 = (bf16[3072,128]{1,0:T(8,128)(2,1)S(1)}, bf16[3072,128]{1,0:T(8,128)(2,1)S(1)}, u32[]{:S(2)}, u32[]{:S(2)}) collective-permute-start(bf16[3072,128]{1,0:T(8,128)(2,1)S(1)} %get-tuple-element.52), channel_id=1, source_target_pairs={{0,8},{4,12},{8,0},{12,4},{1,9},{5,13},{9,1},{13,5},{2,10},{6,14},... | collective-permute-start | bytes 2359304 | tf_op jit(solution)/shard_map/ppermute | solution.py:233
  25.8 16.8 %collective-permute-start.11 = (s32[32,128]{1,0:T(8,128)S(1)}, s32[32,128]{1,0:T(8,128)S(1)}, u32[]{:S(2)}, u32[]{:S(2)}) collective-permute-start(s32[32,128]{1,0:T(8,128)S(1)} %pad_add_fusion.1), channel_id=1, source_target_pairs={{0,128},{4,132},{8,136},{12,140},{16,144},{20,148},{24,152},{28,15... | collective-permute-start | bytes 49160 | tf_op jit(solution)/shard_map/ppermute | solution.py:249
  42.6 5.0 %copy-start.2 = (bf16[3072,128]{1,0:T(8,128)(2,1)}, bf16[3072,128]{1,0:T(8,128)(2,1)S(1)}, u32[]{:S(2)}) copy-start(bf16[3072,128]{1,0:T(8,128)(2,1)S(1)} %collective-permute-done.9.refs_4_) | copy-start | bytes 2359300
  42.6 5.0 %copy-start.4 = (bf16[3072,128]{1,0:T(8,128)(2,1)}, bf16[3072,128]{1,0:T(8,128)(2,1)S(1)}, u32[]{:S(2)}) copy-start(bf16[3072,128]{1,0:T(8,128)(2,1)S(1)} %collective-permute-done.8.refs_3_) | copy-start | bytes 2359300
  42.7 17.6 %collective-permute-start.12 = (bf16[3072,128]{1,0:T(8,128)(2,1)S(1)}, bf16[3072,128]{1,0:T(8,128)(2,1)}, u32[]{:S(2)}, u32[]{:S(2)}) collective-permute-start(bf16[3072,128]{1,0:T(8,128)(2,1)S(1)} %collective-permute-done.8.refs_3_), channel_id=1, source_target_pairs={{0,32},{16,48},{32,64},{48,80},{64,96},{80,112},{96,128},{112,144}... | collective-permute-start | bytes 2359304 | tf_op jit(solution)/shard_map/ppermute | solution.py:229
  42.7 17.5 %collective-permute-start.13 = (bf16[3072,128]{1,0:T(8,128)(2,1)S(1)}, bf16[3072,128]{1,0:T(8,128)(2,1)}, u32[]{:S(2)}, u32[]{:S(2)}) collective-permute-start(bf16[3072,128]{1,0:T(8,128)(2,1)S(1)} %collective-permute-done.9.refs_4_), channel_id=1, source_target_pairs={{0,224},{16,240},{32,0},{48,16},{64,32},{80,48},{96,64},{112,80},{... | collective-permute-start | bytes 2359304 | tf_op jit(solution)/shard_map/ppermute | solution.py:229
  47.0 16.6 %collective-permute-start.18 = (bf16[3072,128]{1,0:T(8,128)(2,1)}, bf16[3072,128]{1,0:T(8,128)(2,1)S(1)}, u32[]{:S(2)}, u32[]{:S(2)}) collective-permute-start(bf16[3072,128]{1,0:T(8,128)(2,1)} %pad_maximum_fusion.1), channel_id=1, source_target_pairs={{0,8},{4,12},{8,0},{12,4},{1,9},{5,13},{9,1},{13,5},{2,10},{6,14},... | collective-permute-start | bytes 2359304 | tf_op jit(solution)/shard_map/ppermute | solution.py:233
  48.6 17.7 %collective-permute-start.19 = (bf16[3072,128]{1,0:T(8,128)(2,1)}, bf16[3072,128]{1,0:T(8,128)(2,1)}, u32[]{:S(2)}, u32[]{:S(2)}) collective-permute-start(bf16[3072,128]{1,0:T(8,128)(2,1)} %pad_maximum_fusion.2), channel_id=1, source_target_pairs={{0,24},{4,28},{8,16},{12,20},{16,8},{20,12},{24,0},{28,4},{32,56},... | collective-permute-start | bytes 2359304 | tf_op jit(solution)/shard_map/ppermute | solution.py:237
  60.2 17.1 %collective-permute-start.14 = (bf16[3072,128]{1,0:T(8,128)(2,1)}, bf16[3072,128]{1,0:T(8,128)(2,1)}, u32[]{:S(2)}, u32[]{:S(2)}) collective-permute-start(bf16[3072,128]{1,0:T(8,128)(2,1)} %collective-permute-done.12.refs_2_), channel_id=1, source_target_pairs={{0,32},{16,48},{32,64},{48,80},{64,96},{80,112},{96,128},{112,144}... | collective-permute-start | bytes 2359304 | tf_op jit(solution)/shard_map/ppermute | solution.py:229
  60.2 17.1 %collective-permute-start.15 = (bf16[3072,128]{1,0:T(8,128)(2,1)}, bf16[3072,128]{1,0:T(8,128)(2,1)}, u32[]{:S(2)}, u32[]{:S(2)}) collective-permute-start(bf16[3072,128]{1,0:T(8,128)(2,1)} %collective-permute-done.13.refs_3_), channel_id=1, source_target_pairs={{0,224},{16,240},{32,0},{48,16},{64,32},{80,48},{96,64},{112,80},{... | collective-permute-start | bytes 2359304 | tf_op jit(solution)/shard_map/ppermute | solution.py:229
  78.6 13.7 %collective-permute-start.20 = (bf16[3072,128]{1,0:T(8,128)(2,1)S(1)}, bf16[3072,128]{1,0:T(8,128)(2,1)S(1)}, u32[]{:S(2)}, u32[]{:S(2)}) collective-permute-start(bf16[3072,128]{1,0:T(8,128)(2,1)S(1)} %broadcast_select_fusion), channel_id=1, source_target_pairs={{0,32},{4,228},{8,40},{12,236},{16,48},{20,244},{24,56},{28,252},{... | collective-permute-start | bytes 2359304 | tf_op jit(solution)/shard_map/ppermute | solution.py:293
  96.0 4.2 %collective-permute-start.21 = (f32[4096,128]{1,0:T(8,128)S(1)}, f32[4096,128]{1,0:T(8,128)S(1)}, u32[]{:S(2)}, u32[]{:S(2)}) collective-permute-start(f32[4096,128]{1,0:T(8,128)S(1)} %get-tuple-element.36), channel_id=1, source_target_pairs={{0,4},{4,0},{8,12},{12,8},{1,5},{5,1},{9,13},{13,9},{2,6},{6,2},{1... | collective-permute-start | bytes 6291464 | tf_op jit(solution)/shard_map/ppermute | solution.py:297
  100.4 9.0 %collective-permute-start.24 = (f32[512,128]{1,0:T(8,128)S(1)}, f32[512,128]{1,0:T(8,128)S(1)}, u32[]{:S(2)}, u32[]{:S(2)}) collective-permute-start(f32[512,128]{1,0:T(8,128)S(1)} %get-tuple-element.38), channel_id=1, source_target_pairs={{0,1},{1,2},{2,3},{3,0},{4,5},{5,6},{6,7},{7,4},{8,9},{9,10},{10,1... | collective-permute-start | bytes 786440 | tf_op jit(solution)/shard_map/ppermute | solution.py:305
  101.7 8.3 %collective-permute-start.25 = (f32[512,128]{1,0:T(8,128)S(1)}, f32[512,128]{1,0:T(8,128)S(1)}, u32[]{:S(2)}, u32[]{:S(2)}) collective-permute-start(f32[512,128]{1,0:T(8,128)S(1)} %get-tuple-element.39), channel_id=1, source_target_pairs={{0,3},{1,0},{2,1},{3,2},{4,7},{5,4},{6,5},{7,6},{8,11},{9,8},{10,9... | collective-permute-start | bytes 786440 | tf_op jit(solution)/shard_map/ppermute | solution.py:306
  102.9 23.2 %collective-permute-start.22 = (f32[1024,128]{1,0:T(8,128)S(1)}, f32[1024,128]{1,0:T(8,128)S(1)}, u32[]{:S(2)}, u32[]{:S(2)}) collective-permute-start(f32[1024,128]{1,0:T(8,128)S(1)} %slice_add_fusion), channel_id=1, source_target_pairs={{0,8},{4,24},{8,0},{12,16},{16,12},{20,28},{24,4},{28,20},{32,40},... | collective-permute-start | bytes 1572872 | tf_op jit(solution)/shard_map/ppermute | solution.py:309
  103.2 13.8 %collective-permute-start.23 = (f32[512,128]{1,0:T(8,128)S(1)}, f32[512,128]{1,0:T(8,128)S(1)}, u32[]{:S(2)}, u32[]{:S(2)}) collective-permute-start(f32[512,128]{1,0:T(8,128)S(1)} %get-tuple-element.37), channel_id=1, source_target_pairs={{0,11},{1,8},{2,9},{3,10},{4,27},{5,24},{6,25},{7,26},{8,3},{9,0},... | collective-permute-start | bytes 786440 | tf_op jit(solution)/shard_map/ppermute | solution.py:308
  107.6 18.5 %collective-permute-start.27 = (f32[512,128]{1,0:T(8,128)S(1)}, f32[512,128]{1,0:T(8,128)S(1)}, u32[]{:S(2)}, u32[]{:S(2)}) collective-permute-start(f32[512,128]{1,0:T(8,128)S(1)} %get-tuple-element.41), channel_id=1, source_target_pairs={{0,9},{1,10},{2,11},{3,8},{4,25},{5,26},{6,27},{7,24},{8,1},{9,2},... | collective-permute-start | bytes 786440 | tf_op jit(solution)/shard_map/ppermute | solution.py:307
  110.1 19.7 %collective-permute-start.26 = (f32[512,128]{1,0:T(8,128)S(1)}, f32[512,128]{1,0:T(8,128)S(1)}, u32[]{:S(2)}, u32[]{:S(2)}) collective-permute-start(f32[512,128]{1,0:T(8,128)S(1)} %get-tuple-element.43), channel_id=1, source_target_pairs={{0,9},{1,10},{2,11},{3,8},{4,25},{5,26},{6,27},{7,24},{8,1},{9,2},... | collective-permute-start | bytes 786440 | tf_op jit(solution)/shard_map/ppermute | solution.py:311
  111.4 19.5 %collective-permute-start.28 = (f32[512,128]{1,0:T(8,128)S(1)}, f32[512,128]{1,0:T(8,128)S(1)}, u32[]{:S(2)}, u32[]{:S(2)}) collective-permute-start(f32[512,128]{1,0:T(8,128)S(1)} %get-tuple-element.44), channel_id=1, source_target_pairs={{0,11},{1,8},{2,9},{3,10},{4,27},{5,24},{6,25},{7,26},{8,3},{9,0},... | collective-permute-start | bytes 786440 | tf_op jit(solution)/shard_map/ppermute | solution.py:312
  (7 other events, 16.1 us)

commit v7 on v6

--- a/solution.py
+++ b/solution.py
@@ -173,7 +173,7 @@
             return count
 
         count = lax.fori_loop(0, 8, panel, count)
-    for k in range(3):
+    for k in range(7):
         work[count + k] = jnp.int32(64 << 20)
 
     for copy in copies:
@@ -183,15 +183,15 @@
         return pl.ds(pl.multiple_of(k * TILE, TILE), TILE)
 
     def products(g, carry):
-        for k in range(4):
-            w = work[g * 4 + k]
+        for k in range(8):
+            w = work[g * 8 + k]
             block = rows_of(w >> 20)
             acc[block] = acc[block] + jnp.dot(
                 abuf[rows_of(w & 1023)], bbuf[rows_of((w >> 10) & 1023)], preferred_element_type=jnp.float32
             )
         return carry
 
-    lax.fori_loop(0, (count + 3) >> 2, products, 0)
+    lax.fori_loop(0, (count + 7) >> 3, products, 0)
 
     for (start, size), out in zip(outs_rows, outs):
         out[...] = acc[pl.ds(start * TILE, size * TILE)]

time: 133 us -> 133 us (level)
  starting transfers between devices: 39.1 us -> 36.6 us
  waiting for transfers between devices: 61.1 us -> 63 us
    ppermute x1, waiting for transfers between devices: 9.06 us -> 5.88 us  [shards(): up1 = send(units[2], ALL, home_route(1))]
  transfers between devices with their start and end apart: 29 -> 29, of which waited for: 16 -> 16; matrix products, arithmetic and copies ran while one was open for 2% -> 2% of each run, Pallas kernels for 13% -> 14%
where the time goes in v7:
time: 133 us; the launch traced here: 132 us
  waiting for transfers between devices  63 us (47%)
  starting transfers between devices  36.6 us (28%)
  Pallas kernels  22.1 us (17%)
  local copies, waits for them, and re-layouts  5.42 us (4%)
  other arithmetic  4.66 us (4%)
    pallas_call x3, Pallas kernels, multiply(): pl.pallas_call(functools.partial(kernel, deltas, parts, tiles, first, out...  22.1 us
    ppermute x2, waiting for transfers between devices, spread(): send(meta, BOTH, [(i, i ^ 1 << bit) for i in range(64)])  14.1 us
    ppermute x6, waiting for transfers between devices, onward(): return (send(f, 'row', z_route(1)), send(b, 'row', z_route(-1)))  10.4 us
    ppermute x6, starting transfers between devices, onward(): return (send(f, 'row', z_route(1)), send(b, 'row', z_route(-1)))  9.75 us
    ppermute x6, starting transfers between devices, spread_two(): send(meta, BOTH, [(i, i ^ k << low) for i in range(64)])  9.43 us
    ppermute x6, waiting for transfers between devices, spread_two(): send(meta, BOTH, [(i, i ^ k << low) for i in range(64)])  6.53 us
    ppermute x1, waiting for transfers between devices, shards(): up1 = send(units[2], ALL, home_route(1))  5.88 us
    ppermute x1, waiting for transfers between devices, shards(): down1 = send(units[3], ALL, home_route(-1))  4.96 us
  transfers between devices with their start and end apart: 29, of which 16 were waited for; matrix products, arithmetic and copies ran while one was open for 2% of the time, Pallas kernels for 14%

profile of v7, /device:TPU:8, one launch (start us, length us, event | category | flops | bytes accessed | tf_op | source)
XLA Modules:
  0.0 132.1 jit_solution(16847140303850619046)
XLA Ops:
  0.0 1.3 constant_dynamic-slice_fusion.1
  1.4 1.6 %collective-permute-start = (bf16[3072,128]{1,0:T(8,128)(2,1)}, bf16[3072,128]{1,0:T(8,128)(2,1)S(1)}, u32[]{:S(2)}, u32[]{:S(2)}) collective-permute-start(bf16[3072,128]{1,0:T(8,128)(2,1)} %bitcast.5), channel_id=1, source_target_pairs={{0,8},{4,24},{8,0},{12,16},{16,12},{20,28},{24,4},{28,20},{32,40},... | collective-permute-start | bytes 2359304 | tf_op jit(solution)/shard_map/ppermute | solution.py:259
  3.6 4.7 %collective-permute-start.4 = (s32[1,128]{1,0:T(1,128)S(1)}, s32[1,128]{1,0:T(1,128)S(1)}, u32[]{:S(2)}, u32[]{:S(2)}) collective-permute-start(s32[1,128]{1,0:T(1,128)S(1)} %pad_add_fusion.5), channel_id=1, source_target_pairs={{0,96},{4,100},{8,104},{12,108},{16,112},{20,116},{24,120},{28,124... | collective-permute-start | bytes 1544 | tf_op jit(solution)/shard_map/ppermute | solution.py:244
  9.7 2.9 %collective-permute-done.3 = s32[1,128]{1,0:T(1,128)S(1)} collective-permute-done((s32[1,128]{1,0:T(1,128)S(1)}, s32[1,128]{1,0:T(1,128)S(1)}, u32[]{:S(2)}, u32[]{:S(2)}) %collective-permute-start.3) | collective-permute-done | bytes 544 | tf_op jit(solution)/shard_map/ppermute | solution.py:244
  12.7 1.8 %collective-permute-start.7 = (s32[4,128]{1,0:T(4,128)S(1)}, s32[4,128]{1,0:T(4,128)S(1)}, u32[]{:S(2)}, u32[]{:S(2)}) collective-permute-start(s32[4,128]{1,0:T(4,128)S(1)} %pad_add_fusion.2), channel_id=1, source_target_pairs={{0,24},{4,28},{8,16},{12,20},{16,8},{20,12},{24,0},{28,4},{32,56},... | collective-permute-start | bytes 6152 | tf_op jit(solution)/shard_map/ppermute | solution.py:244
  15.4 1.5 %collective-permute-start.5 = (s32[4,128]{1,0:T(4,128)S(1)}, s32[4,128]{1,0:T(4,128)S(1)}, u32[]{:S(2)}, u32[]{:S(2)}) collective-permute-start(s32[4,128]{1,0:T(4,128)S(1)} %pad_add_fusion.2), channel_id=1, source_target_pairs={{0,8},{4,12},{8,0},{12,4},{16,24},{20,28},{24,16},{28,20},{32,40},... | collective-permute-start | bytes 6152 | tf_op jit(solution)/shard_map/ppermute | solution.py:244
  17.6 2.1 %collective-permute-done.6 = s32[4,128]{1,0:T(4,128)S(1)} collective-permute-done((s32[4,128]{1,0:T(4,128)S(1)}, s32[4,128]{1,0:T(4,128)S(1)}, u32[]{:S(2)}, u32[]{:S(2)}) %collective-permute-start.6) | collective-permute-done | bytes 2080 | tf_op jit(solution)/shard_map/ppermute | solution.py:244
  19.8 3.2 %collective-permute-start.9 = (bf16[3072,128]{1,0:T(8,128)(2,1)S(1)}, bf16[3072,128]{1,0:T(8,128)(2,1)S(1)}, u32[]{:S(2)}, u32[]{:S(2)}) collective-permute-start(bf16[3072,128]{1,0:T(8,128)(2,1)S(1)} %collective-permute-done.refs_2_), channel_id=1, source_target_pairs={{0,224},{16,240},{32,0},{48,16},{64,32},{80,48},{96,64},{112,80},{... | collective-permute-start | bytes 2359304 | tf_op jit(solution)/shard_map/ppermute | solution.py:229
  23.1 1.6 %collective-permute-start.17 = (bf16[3072,128]{1,0:T(8,128)(2,1)S(1)}, bf16[3072,128]{1,0:T(8,128)(2,1)S(1)}, u32[]{:S(2)}, u32[]{:S(2)}) collective-permute-start(bf16[3072,128]{1,0:T(8,128)(2,1)S(1)} %get-tuple-element.51), channel_id=1, source_target_pairs={{0,24},{4,28},{8,16},{12,20},{16,8},{20,12},{24,0},{28,4},{32,56},... | collective-permute-start | bytes 2359304 | tf_op jit(solution)/shard_map/ppermute | solution.py:237
  25.8 3.4 %collective-permute-start.11 = (s32[32,128]{1,0:T(8,128)S(1)}, s32[32,128]{1,0:T(8,128)S(1)}, u32[]{:S(2)}, u32[]{:S(2)}) collective-permute-start(s32[32,128]{1,0:T(8,128)S(1)} %pad_add_fusion.1), channel_id=1, source_target_pairs={{0,128},{4,132},{8,136},{12,140},{16,144},{20,148},{24,152},{28,15... | collective-permute-start | bytes 49160 | tf_op jit(solution)/shard_map/ppermute | solution.py:249
  29.2 13.4 %collective-permute-done.11 = s32[32,128]{1,0:T(8,128)S(1)} collective-permute-done((s32[32,128]{1,0:T(8,128)S(1)}, s32[32,128]{1,0:T(8,128)S(1)}, u32[]{:S(2)}, u32[]{:S(2)}) %collective-permute-start.11) | collective-permute-done | bytes 16416 | tf_op jit(solution)/shard_map/ppermute | solution.py:249
  42.7 3.2 %collective-permute-start.13 = (bf16[3072,128]{1,0:T(8,128)(2,1)S(1)}, bf16[3072,128]{1,0:T(8,128)(2,1)}, u32[]{:S(2)}, u32[]{:S(2)}) collective-permute-start(bf16[3072,128]{1,0:T(8,128)(2,1)S(1)} %collective-permute-done.9.refs_4_), channel_id=1, source_target_pairs={{0,224},{16,240},{32,0},{48,16},{64,32},{80,48},{96,64},{112,80},{... | collective-permute-start | bytes 2359304 | tf_op jit(solution)/shard_map/ppermute | solution.py:229
  48.6 1.2 collective-permute-start.19
  49.8 10.4 %collective-permute-done.12.refs_2_ = bf16[3072,128]{1,0:T(8,128)(2,1)} collective-permute-done((bf16[3072,128]{1,0:T(8,128)(2,1)S(1)}, bf16[3072,128]{1,0:T(8,128)(2,1)}, u32[]{:S(2)}, u32[]{:S(2)}) %collective-permute-start.12) | collective-permute-done | bytes 786464 | tf_op jit(solution)/shard_map/ppermute | solution.py:229
  60.2 3.2 %collective-permute-start.15 = (bf16[3072,128]{1,0:T(8,128)(2,1)}, bf16[3072,128]{1,0:T(8,128)(2,1)}, u32[]{:S(2)}, u32[]{:S(2)}) collective-permute-start(bf16[3072,128]{1,0:T(8,128)(2,1)} %collective-permute-done.13.refs_3_), channel_id=1, source_target_pairs={{0,224},{16,240},{32,0},{48,16},{64,32},{80,48},{96,64},{112,80},{... | collective-permute-start | bytes 2359304 | tf_op jit(solution)/shard_map/ppermute | solution.py:229
  63.6 2.8 %collective-permute-done.19.refs_9_.refs_10_.refs_7_ = bf16[3072,128]{1,0:T(8,128)(2,1)} collective-permute-done((bf16[3072,128]{1,0:T(8,128)(2,1)}, bf16[3072,128]{1,0:T(8,128)(2,1)}, u32[]{:S(2)}, u32[]{:S(2)}) %collective-permute-start.19) | collective-permute-done | bytes 786464 | tf_op jit(solution)/shard_map/ppermute | solution.py:237
  66.3 1.1 copy-done.1
  67.5 1.1 copy-done.3
  69.7 8.1 %products_0_7_1.1.refs_11_ = f32[8192,128]{1,0:T(8,128)S(1)} custom-call(s32[8]{0:T(128)S(1)} %stack.26.refs_0_, s32[64,128]{1,0:T(8,128)S(1)} %pad_add_fusion.refs_1_, bf16[3072,128]{1,0:T(8,128)(2,1)S(1)} %copy-done.1, bf16[3072,128]{1,0:T(8,128)(2,1)S(1)} %copy-done.5, bf16[3072,128]{1,0:T(8,128)(2,1)S(1)} %copy-done.3, ...), custom_call_target="tpu_custom_call" | custom-call | flops 120000000 | bytes 20000000 | tf_op jit(solution)/shard_map/products_0_7_1/pallas_call | solution.py:204
  77.8 1.2 broadcast_select_fusion
  79.1 10.0 %products_6_2_5_3.1.refs_8_ = f32[8192,128]{1,0:T(8,128)S(1)} custom-call(s32[8]{0:T(128)S(1)} %stack.26.refs_0_, s32[64,128]{1,0:T(8,128)S(1)} %pad_add_fusion.refs_1_, bf16[3072,128]{1,0:T(8,128)(2,1)} %collective-permute-done.12.refs_2_, bf16[3072,128]{1,0:T(8,128)(2,1)} %collective-permute-done.13.refs_3_, ...), custom_call_target="tpu_custom_call" | custom-call | flops 160000000 | bytes 24000000 | tf_op jit(solution)/shard_map/products_6_2_5_3/pallas_call | solution.py:204
  89.1 3.7 %collective-permute-done.20.refs_2_ = bf16[3072,128]{1,0:T(8,128)(2,1)S(1)} collective-permute-done((bf16[3072,128]{1,0:T(8,128)(2,1)S(1)}, bf16[3072,128]{1,0:T(8,128)(2,1)S(1)}, u32[]{:S(2)}, u32[]{:S(2)}) %collective-permute-start.20) | collective-permute-done | bytes 786464 | tf_op jit(solution)/shard_map/ppermute | solution.py:293
  92.8 4.0 %products_4.1 = (f32[4096,128]{1,0:T(8,128)S(1)}, f32[4096,128]{1,0:T(8,128)S(1)}) custom-call(s32[8]{0:T(128)S(1)} %stack.26.refs_0_, s32[64,128]{1,0:T(8,128)S(1)} %pad_add_fusion.refs_1_, bf16[3072,128]{1,0:T(8,128)(2,1)S(1)} %collective-permute-done.20.refs_2_, bf16[4096,128]{1,0:T(8,128)(2,1)S(1)} %pad_maximum_fusion.refs_5_.refs_6_.refs_3_, ...), custom_call_target="tpu_custom_call" | custom-call | flops 40000000 | bytes 12000000 | tf_op jit(solution)/shard_map/products_4/pallas_call | solution.py:204
  96.9 4.1 %collective-permute-done.21 = f32[4096,128]{1,0:T(8,128)S(1)} collective-permute-done((f32[4096,128]{1,0:T(8,128)S(1)}, f32[4096,128]{1,0:T(8,128)S(1)}, u32[]{:S(2)}, u32[]{:S(2)}) %collective-permute-start.21) | collective-permute-done | bytes 2097184 | tf_op jit(solution)/shard_map/ppermute | solution.py:297
  102.2 1.2 collective-permute-start.25
  103.5 3.2 %collective-permute-start.23 = (f32[512,128]{1,0:T(8,128)S(1)}, f32[512,128]{1,0:T(8,128)S(1)}, u32[]{:S(2)}, u32[]{:S(2)}) collective-permute-start(f32[512,128]{1,0:T(8,128)S(1)} %get-tuple-element.37), channel_id=1, source_target_pairs={{0,11},{1,8},{2,9},{3,10},{4,27},{5,24},{6,25},{7,26},{8,3},{9,0},... | collective-permute-start | bytes 786440 | tf_op jit(solution)/shard_map/ppermute | solution.py:308
  106.7 3.0 %collective-permute-done.24 = f32[512,128]{1,0:T(8,128)S(1)} collective-permute-done((f32[512,128]{1,0:T(8,128)S(1)}, f32[512,128]{1,0:T(8,128)S(1)}, u32[]{:S(2)}, u32[]{:S(2)}) %collective-permute-start.24) | collective-permute-done | bytes 262176 | tf_op jit(solution)/shard_map/ppermute | solution.py:305
  110.9 2.9 %collective-permute-start.28 = (f32[512,128]{1,0:T(8,128)S(1)}, f32[512,128]{1,0:T(8,128)S(1)}, u32[]{:S(2)}, u32[]{:S(2)}) collective-permute-start(f32[512,128]{1,0:T(8,128)S(1)} %get-tuple-element.44), channel_id=1, source_target_pairs={{0,11},{1,8},{2,9},{3,10},{4,27},{5,24},{6,25},{7,26},{8,3},{9,0},... | collective-permute-start | bytes 786440 | tf_op jit(solution)/shard_map/ppermute | solution.py:312
  113.8 5.0 %collective-permute-done.23 = f32[512,128]{1,0:T(8,128)S(1)} collective-permute-done((f32[512,128]{1,0:T(8,128)S(1)}, f32[512,128]{1,0:T(8,128)S(1)}, u32[]{:S(2)}, u32[]{:S(2)}) %collective-permute-start.23) | collective-permute-done | bytes 262176 | tf_op jit(solution)/shard_map/ppermute | solution.py:308
  118.8 5.9 %collective-permute-done.27 = f32[512,128]{1,0:T(8,128)S(1)} collective-permute-done((f32[512,128]{1,0:T(8,128)S(1)}, f32[512,128]{1,0:T(8,128)S(1)}, u32[]{:S(2)}, u32[]{:S(2)}) %collective-permute-start.27) | collective-permute-done | bytes 262176 | tf_op jit(solution)/shard_map/ppermute | solution.py:307
  124.7 4.5 %collective-permute-done.26 = f32[512,128]{1,0:T(8,128)S(1)} collective-permute-done((f32[512,128]{1,0:T(8,128)S(1)}, f32[512,128]{1,0:T(8,128)S(1)}, u32[]{:S(2)}, u32[]{:S(2)}) %collective-permute-start.26) | collective-permute-done | bytes 262176 | tf_op jit(solution)/shard_map/ppermute | solution.py:311
  129.2 2.1 %collective-permute-done.28 = f32[512,128]{1,0:T(8,128)S(1)} collective-permute-done((f32[512,128]{1,0:T(8,128)S(1)}, f32[512,128]{1,0:T(8,128)S(1)}, u32[]{:S(2)}, u32[]{:S(2)}) %collective-permute-start.28) | collective-permute-done | bytes 262176 | tf_op jit(solution)/shard_map/ppermute | solution.py:312
  (76 shorter events, 12.7 us)
Async XLA Ops:
  1.3 18.3 %collective-permute-start.1 = (bf16[2048,128]{1,0:T(8,128)(2,1)S(1)}, bf16[2048,128]{1,0:T(8,128)(2,1)S(1)}, u32[]{:S(2)}, u32[]{:S(2)}) collective-permute-start(bf16[2048,128]{1,0:T(8,128)(2,1)S(1)} %bitcast.20), channel_id=1, source_target_pairs={{0,4},{4,0},{8,12},{12,8},{1,5},{5,1},{9,13},{13,9},{2,6},{6,2},{1... | collective-permute-start | bytes 1572872 | tf_op jit(solution)/shard_map/ppermute | solution.py:263
  1.4 18.3 %collective-permute-start = (bf16[3072,128]{1,0:T(8,128)(2,1)}, bf16[3072,128]{1,0:T(8,128)(2,1)S(1)}, u32[]{:S(2)}, u32[]{:S(2)}) collective-permute-start(bf16[3072,128]{1,0:T(8,128)(2,1)} %bitcast.5), channel_id=1, source_target_pairs={{0,8},{4,24},{8,0},{12,16},{16,12},{20,28},{24,4},{28,20},{32,40},... | collective-permute-start | bytes 2359304 | tf_op jit(solution)/shard_map/ppermute | solution.py:259
  3.6 6.2 %collective-permute-start.4 = (s32[1,128]{1,0:T(1,128)S(1)}, s32[1,128]{1,0:T(1,128)S(1)}, u32[]{:S(2)}, u32[]{:S(2)}) collective-permute-start(s32[1,128]{1,0:T(1,128)S(1)} %pad_add_fusion.5), channel_id=1, source_target_pairs={{0,96},{4,100},{8,104},{12,108},{16,112},{20,116},{24,120},{28,124... | collective-permute-start | bytes 1544 | tf_op jit(solution)/shard_map/ppermute | solution.py:244
  8.2 4.4 %collective-permute-start.3 = (s32[1,128]{1,0:T(1,128)S(1)}, s32[1,128]{1,0:T(1,128)S(1)}, u32[]{:S(2)}, u32[]{:S(2)}) collective-permute-start(s32[1,128]{1,0:T(1,128)S(1)} %pad_add_fusion.5), channel_id=1, source_target_pairs={{0,64},{4,68},{8,72},{12,76},{16,80},{20,84},{24,88},{28,92},{32,9... | collective-permute-start | bytes 1544 | tf_op jit(solution)/shard_map/ppermute | solution.py:244
  8.2 4.4 %collective-permute-start.2 = (s32[1,128]{1,0:T(1,128)S(1)}, s32[1,128]{1,0:T(1,128)S(1)}, u32[]{:S(2)}, u32[]{:S(2)}) collective-permute-start(s32[1,128]{1,0:T(1,128)S(1)} %pad_add_fusion.5), channel_id=1, source_target_pairs={{0,32},{4,36},{8,40},{12,44},{16,48},{20,52},{24,56},{28,60},{32,0... | collective-permute-start | bytes 1544 | tf_op jit(solution)/shard_map/ppermute | solution.py:244
  12.7 4.8 %collective-permute-start.7 = (s32[4,128]{1,0:T(4,128)S(1)}, s32[4,128]{1,0:T(4,128)S(1)}, u32[]{:S(2)}, u32[]{:S(2)}) collective-permute-start(s32[4,128]{1,0:T(4,128)S(1)} %pad_add_fusion.2), channel_id=1, source_target_pairs={{0,24},{4,28},{8,16},{12,20},{16,8},{20,12},{24,0},{28,4},{32,56},... | collective-permute-start | bytes 6152 | tf_op jit(solution)/shard_map/ppermute | solution.py:244
  14.5 5.1 %collective-permute-start.6 = (s32[4,128]{1,0:T(4,128)S(1)}, s32[4,128]{1,0:T(4,128)S(1)}, u32[]{:S(2)}, u32[]{:S(2)}) collective-permute-start(s32[4,128]{1,0:T(4,128)S(1)} %pad_add_fusion.2), channel_id=1, source_target_pairs={{0,16},{4,20},{8,24},{12,28},{16,0},{20,4},{24,8},{28,12},{32,48},... | collective-permute-start | bytes 6152 | tf_op jit(solution)/shard_map/ppermute | solution.py:244
  15.4 4.3 %collective-permute-start.5 = (s32[4,128]{1,0:T(4,128)S(1)}, s32[4,128]{1,0:T(4,128)S(1)}, u32[]{:S(2)}, u32[]{:S(2)}) collective-permute-start(s32[4,128]{1,0:T(4,128)S(1)} %pad_add_fusion.2), channel_id=1, source_target_pairs={{0,8},{4,12},{8,0},{12,4},{16,24},{20,28},{24,16},{28,20},{32,40},... | collective-permute-start | bytes 6152 | tf_op jit(solution)/shard_map/ppermute | solution.py:244
  19.7 26.3 %copy-start = (bf16[3072,128]{1,0:T(8,128)(2,1)}, bf16[3072,128]{1,0:T(8,128)(2,1)S(1)}, u32[]{:S(2)}) copy-start(bf16[3072,128]{1,0:T(8,128)(2,1)S(1)} %collective-permute-done.refs_2_) | copy-start | bytes 2359300
  19.8 22.9 %collective-permute-start.9 = (bf16[3072,128]{1,0:T(8,128)(2,1)S(1)}, bf16[3072,128]{1,0:T(8,128)(2,1)S(1)}, u32[]{:S(2)}, u32[]{:S(2)}) collective-permute-start(bf16[3072,128]{1,0:T(8,128)(2,1)S(1)} %collective-permute-done.refs_2_), channel_id=1, source_target_pairs={{0,224},{16,240},{32,0},{48,16},{64,32},{80,48},{96,64},{112,80},{... | collective-permute-start | bytes 2359304 | tf_op jit(solution)/shard_map/ppermute | solution.py:229
  23.0 19.7 %collective-permute-start.8 = (bf16[3072,128]{1,0:T(8,128)(2,1)S(1)}, bf16[3072,128]{1,0:T(8,128)(2,1)S(1)}, u32[]{:S(2)}, u32[]{:S(2)}) collective-permute-start(bf16[3072,128]{1,0:T(8,128)(2,1)S(1)} %collective-permute-done.refs_2_), channel_id=1, source_target_pairs={{0,32},{16,48},{32,64},{48,80},{64,96},{80,112},{96,128},{112,144}... | collective-permute-start | bytes 2359304 | tf_op jit(solution)/shard_map/ppermute | solution.py:229
  23.1 23.0 %collective-permute-start.17 = (bf16[3072,128]{1,0:T(8,128)(2,1)S(1)}, bf16[3072,128]{1,0:T(8,128)(2,1)S(1)}, u32[]{:S(2)}, u32[]{:S(2)}) collective-permute-start(bf16[3072,128]{1,0:T(8,128)(2,1)S(1)} %get-tuple-element.51), channel_id=1, source_target_pairs={{0,24},{4,28},{8,16},{12,20},{16,8},{20,12},{24,0},{28,4},{32,56},... | collective-permute-start | bytes 2359304 | tf_op jit(solution)/shard_map/ppermute | solution.py:237
  24.6 1.2 collective-permute-start.10
  24.6 23.0 %collective-permute-start.16 = (bf16[3072,128]{1,0:T(8,128)(2,1)S(1)}, bf16[3072,128]{1,0:T(8,128)(2,1)S(1)}, u32[]{:S(2)}, u32[]{:S(2)}) collective-permute-start(bf16[3072,128]{1,0:T(8,128)(2,1)S(1)} %get-tuple-element.52), channel_id=1, source_target_pairs={{0,8},{4,12},{8,0},{12,4},{1,9},{5,13},{9,1},{13,5},{2,10},{6,14},... | collective-permute-start | bytes 2359304 | tf_op jit(solution)/shard_map/ppermute | solution.py:233
  25.8 16.8 %collective-permute-start.11 = (s32[32,128]{1,0:T(8,128)S(1)}, s32[32,128]{1,0:T(8,128)S(1)}, u32[]{:S(2)}, u32[]{:S(2)}) collective-permute-start(s32[32,128]{1,0:T(8,128)S(1)} %pad_add_fusion.1), channel_id=1, source_target_pairs={{0,128},{4,132},{8,136},{12,140},{16,144},{20,148},{24,152},{28,15... | collective-permute-start | bytes 49160 | tf_op jit(solution)/shard_map/ppermute | solution.py:249
  42.6 5.0 %copy-start.2 = (bf16[3072,128]{1,0:T(8,128)(2,1)}, bf16[3072,128]{1,0:T(8,128)(2,1)S(1)}, u32[]{:S(2)}) copy-start(bf16[3072,128]{1,0:T(8,128)(2,1)S(1)} %collective-permute-done.9.refs_4_) | copy-start | bytes 2359300
  42.6 5.0 %copy-start.4 = (bf16[3072,128]{1,0:T(8,128)(2,1)}, bf16[3072,128]{1,0:T(8,128)(2,1)S(1)}, u32[]{:S(2)}) copy-start(bf16[3072,128]{1,0:T(8,128)(2,1)S(1)} %collective-permute-done.8.refs_3_) | copy-start | bytes 2359300
  42.7 17.6 %collective-permute-start.12 = (bf16[3072,128]{1,0:T(8,128)(2,1)S(1)}, bf16[3072,128]{1,0:T(8,128)(2,1)}, u32[]{:S(2)}, u32[]{:S(2)}) collective-permute-start(bf16[3072,128]{1,0:T(8,128)(2,1)S(1)} %collective-permute-done.8.refs_3_), channel_id=1, source_target_pairs={{0,32},{16,48},{32,64},{48,80},{64,96},{80,112},{96,128},{112,144}... | collective-permute-start | bytes 2359304 | tf_op jit(solution)/shard_map/ppermute | solution.py:229
  42.7 17.5 %collective-permute-start.13 = (bf16[3072,128]{1,0:T(8,128)(2,1)S(1)}, bf16[3072,128]{1,0:T(8,128)(2,1)}, u32[]{:S(2)}, u32[]{:S(2)}) collective-permute-start(bf16[3072,128]{1,0:T(8,128)(2,1)S(1)} %collective-permute-done.9.refs_4_), channel_id=1, source_target_pairs={{0,224},{16,240},{32,0},{48,16},{64,32},{80,48},{96,64},{112,80},{... | collective-permute-start | bytes 2359304 | tf_op jit(solution)/shard_map/ppermute | solution.py:229
  47.0 16.6 %collective-permute-start.18 = (bf16[3072,128]{1,0:T(8,128)(2,1)}, bf16[3072,128]{1,0:T(8,128)(2,1)S(1)}, u32[]{:S(2)}, u32[]{:S(2)}) collective-permute-start(bf16[3072,128]{1,0:T(8,128)(2,1)} %pad_maximum_fusion.1), channel_id=1, source_target_pairs={{0,8},{4,12},{8,0},{12,4},{1,9},{5,13},{9,1},{13,5},{2,10},{6,14},... | collective-permute-start | bytes 2359304 | tf_op jit(solution)/shard_map/ppermute | solution.py:233
  48.6 17.7 %collective-permute-start.19 = (bf16[3072,128]{1,0:T(8,128)(2,1)}, bf16[3072,128]{1,0:T(8,128)(2,1)}, u32[]{:S(2)}, u32[]{:S(2)}) collective-permute-start(bf16[3072,128]{1,0:T(8,128)(2,1)} %pad_maximum_fusion.2), channel_id=1, source_target_pairs={{0,24},{4,28},{8,16},{12,20},{16,8},{20,12},{24,0},{28,4},{32,56},... | collective-permute-start | bytes 2359304 | tf_op jit(solution)/shard_map/ppermute | solution.py:237
  60.2 17.6 %collective-permute-start.14 = (bf16[3072,128]{1,0:T(8,128)(2,1)}, bf16[3072,128]{1,0:T(8,128)(2,1)}, u32[]{:S(2)}, u32[]{:S(2)}) collective-permute-start(bf16[3072,128]{1,0:T(8,128)(2,1)} %collective-permute-done.12.refs_2_), channel_id=1, source_target_pairs={{0,32},{16,48},{32,64},{48,80},{64,96},{80,112},{96,128},{112,144}... | collective-permute-start | bytes 2359304 | tf_op jit(solution)/shard_map/ppermute | solution.py:229
  60.2 17.6 %collective-permute-start.15 = (bf16[3072,128]{1,0:T(8,128)(2,1)}, bf16[3072,128]{1,0:T(8,128)(2,1)}, u32[]{:S(2)}, u32[]{:S(2)}) collective-permute-start(bf16[3072,128]{1,0:T(8,128)(2,1)} %collective-permute-done.13.refs_3_), channel_id=1, source_target_pairs={{0,224},{16,240},{32,0},{48,16},{64,32},{80,48},{96,64},{112,80},{... | collective-permute-start | bytes 2359304 | tf_op jit(solution)/shard_map/ppermute | solution.py:229
  79.0 13.7 %collective-permute-start.20 = (bf16[3072,128]{1,0:T(8,128)(2,1)S(1)}, bf16[3072,128]{1,0:T(8,128)(2,1)S(1)}, u32[]{:S(2)}, u32[]{:S(2)}) collective-permute-start(bf16[3072,128]{1,0:T(8,128)(2,1)S(1)} %broadcast_select_fusion), channel_id=1, source_target_pairs={{0,32},{4,228},{8,40},{12,236},{16,48},{20,244},{24,56},{28,252},{... | collective-permute-start | bytes 2359304 | tf_op jit(solution)/shard_map/ppermute | solution.py:293
  96.8 4.2 %collective-permute-start.21 = (f32[4096,128]{1,0:T(8,128)S(1)}, f32[4096,128]{1,0:T(8,128)S(1)}, u32[]{:S(2)}, u32[]{:S(2)}) collective-permute-start(f32[4096,128]{1,0:T(8,128)S(1)} %get-tuple-element.36), channel_id=1, source_target_pairs={{0,4},{4,0},{8,12},{12,8},{1,5},{5,1},{9,13},{13,9},{2,6},{6,2},{1... | collective-permute-start | bytes 6291464 | tf_op jit(solution)/shard_map/ppermute | solution.py:297
  101.3 8.4 %collective-permute-start.24 = (f32[512,128]{1,0:T(8,128)S(1)}, f32[512,128]{1,0:T(8,128)S(1)}, u32[]{:S(2)}, u32[]{:S(2)}) collective-permute-start(f32[512,128]{1,0:T(8,128)S(1)} %get-tuple-element.38), channel_id=1, source_target_pairs={{0,1},{1,2},{2,3},{3,0},{4,5},{5,6},{6,7},{7,4},{8,9},{9,10},{10,1... | collective-permute-start | bytes 786440 | tf_op jit(solution)/shard_map/ppermute | solution.py:305
  102.2 8.5 %collective-permute-start.25 = (f32[512,128]{1,0:T(8,128)S(1)}, f32[512,128]{1,0:T(8,128)S(1)}, u32[]{:S(2)}, u32[]{:S(2)}) collective-permute-start(f32[512,128]{1,0:T(8,128)S(1)} %get-tuple-element.39), channel_id=1, source_target_pairs={{0,3},{1,0},{2,1},{3,2},{4,7},{5,4},{6,5},{7,6},{8,11},{9,8},{10,9... | collective-permute-start | bytes 786440 | tf_op jit(solution)/shard_map/ppermute | solution.py:306
  103.4 21.3 %collective-permute-start.22 = (f32[1024,128]{1,0:T(8,128)S(1)}, f32[1024,128]{1,0:T(8,128)S(1)}, u32[]{:S(2)}, u32[]{:S(2)}) collective-permute-start(f32[1024,128]{1,0:T(8,128)S(1)} %slice_add_fusion), channel_id=1, source_target_pairs={{0,8},{4,24},{8,0},{12,16},{16,12},{20,28},{24,4},{28,20},{32,40},... | collective-permute-start | bytes 1572872 | tf_op jit(solution)/shard_map/ppermute | solution.py:309
  103.5 15.3 %collective-permute-start.23 = (f32[512,128]{1,0:T(8,128)S(1)}, f32[512,128]{1,0:T(8,128)S(1)}, u32[]{:S(2)}, u32[]{:S(2)}) collective-permute-start(f32[512,128]{1,0:T(8,128)S(1)} %get-tuple-element.37), channel_id=1, source_target_pairs={{0,11},{1,8},{2,9},{3,10},{4,27},{5,24},{6,25},{7,26},{8,3},{9,0},... | collective-permute-start | bytes 786440 | tf_op jit(solution)/shard_map/ppermute | solution.py:308
  106.7 18.0 %collective-permute-start.27 = (f32[512,128]{1,0:T(8,128)S(1)}, f32[512,128]{1,0:T(8,128)S(1)}, u32[]{:S(2)}, u32[]{:S(2)}) collective-permute-start(f32[512,128]{1,0:T(8,128)S(1)} %get-tuple-element.41), channel_id=1, source_target_pairs={{0,9},{1,10},{2,11},{3,8},{4,25},{5,26},{6,27},{7,24},{8,1},{9,2},... | collective-permute-start | bytes 786440 | tf_op jit(solution)/shard_map/ppermute | solution.py:307
  110.8 18.3 %collective-permute-start.26 = (f32[512,128]{1,0:T(8,128)S(1)}, f32[512,128]{1,0:T(8,128)S(1)}, u32[]{:S(2)}, u32[]{:S(2)}) collective-permute-start(f32[512,128]{1,0:T(8,128)S(1)} %get-tuple-element.43), channel_id=1, source_target_pairs={{0,9},{1,10},{2,11},{3,8},{4,25},{5,26},{6,27},{7,24},{8,1},{9,2},... | collective-permute-start | bytes 786440 | tf_op jit(solution)/shard_map/ppermute | solution.py:311
  110.9 20.3 %collective-permute-start.28 = (f32[512,128]{1,0:T(8,128)S(1)}, f32[512,128]{1,0:T(8,128)S(1)}, u32[]{:S(2)}, u32[]{:S(2)}) collective-permute-start(f32[512,128]{1,0:T(8,128)S(1)} %get-tuple-element.44), channel_id=1, source_target_pairs={{0,11},{1,8},{2,9},{3,10},{4,27},{5,24},{6,25},{7,26},{8,3},{9,0},... | collective-permute-start | bytes 786440 | tf_op jit(solution)/shard_map/ppermute | solution.py:312
  (7 other events, 16.1 us)
